TPU v7x, 1024 devices: a whole 8x8x8 slice. The times are simulated.
1024 devices in a mesh: dp: 16 (over z, core), fsdp: 64 (over y, x).
Axes of the slice: x: 8, y: 8, z: 8, core: 2. Of those that a mesh axis runs over, the one named last changes fastest.
Arguments:
- qkv: bfloat16 [16, 64, 192, 3, 896], P('dp', 'fsdp'), may hold values from -8 to 8
- grad_out: bfloat16 [16, 64, 192, 896], P('dp', 'fsdp'), may hold values from -6 to 6
- lengths: int32 [16, 64, 3], P(None, 'fsdp'), may hold values from 1 to 128, 192 in all within a row
- moves: int32 [64, 2, 3], P('fsdp'), may hold values from 0 to 15, as said below
- out_weight: bfloat16 [896, 896], P('fsdp'), may hold values from -0.1875 to 0.1875
Outputs:
- home_grad: bfloat16 [16, 64, 192, 3, 896], P('dp', 'fsdp')
- inbox_grad: bfloat16 [16, 64, 128, 3, 896], P('dp', 'fsdp')
- weight_grad: float32 [896, 896], P('fsdp', 'dp')
Inputs may be any that keep to these rules, and one draw needn't show every extreme that they name: In each fsdp column the sources of the moves differ from one another, and each destination is (source + 1) mod 16; the clip index is below 3. `lengths`: each device's counts sum to 192.
All inputs are finite; a program needn't handle non-finite values.
Results may differ from a plain program's by a relative error of at most 0.023.
Values may be sent and summed in bfloat16 or wider, within the bound.
No kernel may reach another device: no remote copies, remote signals or barrier semaphores. Data moves between devices by JAX's collectives and lax.ppermute only.
A program may use at most 32 MiB of HBM per device.

v0:
```python
import jax
import jax.numpy as jnp
from jax import lax
from jax.sharding import PartitionSpec as P

HEADS = 8
HSIZE = 112
TOK_DEV = 192
CLIP_MAX = 128


def passed_along(shard, axis, by):
    length = lax.axis_size(axis)
    return lax.ppermute(shard, axis, [(i, (i + by) % length) for i in range(length)])


def attend(rows, allowed, live):
    length = rows.shape[0]
    split = rows.reshape(length, 3, HEADS, HSIZE)
    queries = split[:, 0]
    keys = split[:, 1]
    values = split[:, 2]
    scores = jnp.einsum(
        "qhd,khd->hqk", queries, keys, preferred_element_type=jnp.float32
    ) * HSIZE ** (-0.5)
    scores = jnp.where(allowed[None], scores, -1000000000.0)
    probs = jax.nn.softmax(scores, axis=-1).astype(jnp.bfloat16)
    mixed = jnp.einsum("hqk,khd->qhd", probs, values, preferred_element_type=jnp.float32)
    mixed = jnp.where(live[:, None, None], mixed, 0.0)
    return mixed.reshape(length, HEADS * HSIZE).astype(jnp.bfloat16)


def clip_start(counts, which):
    starts = jnp.cumsum(counts) - counts
    clips = jnp.arange(counts.shape[0], dtype=jnp.int32)
    return (
        jnp.sum(jnp.where(clips == which, starts, 0)),
        jnp.sum(jnp.where(clips == which, counts, 0)),
    )


def home_masks(counts, moving, rank):
    ends = jnp.cumsum(counts)
    places = jnp.arange(TOK_DEV, dtype=jnp.int32)
    segment = jnp.sum((places[:, None] >= ends[None, :]).astype(jnp.int32), axis=1)
    clips = jnp.arange(counts.shape[0], dtype=jnp.int32)
    gone = jnp.any((moving[:, 0:1] == rank) & (moving[:, 2:3] == clips[None, :]), axis=0)
    stays = jnp.logical_not(jnp.any((segment[:, None] == clips[None, :]) & gone[None, :], axis=1))
    return (segment[:, None] == segment[None, :], stays)


def local(qkv, grad_out, lengths, moves, out_weight):
    home_rows = qkv[0, 0]
    home_cot = grad_out[0, 0]
    counts_all = lengths[:, 0]
    moving = moves[0]
    rank = lax.axis_index("dp")
    ranks = jnp.arange(counts_all.shape[0], dtype=jnp.int32)
    counts = jnp.sum(jnp.where((ranks == rank)[:, None], counts_all, 0), axis=0)
    allowed_home, stays = home_masks(counts, moving, rank)
    padded = jnp.concatenate(
        [home_rows, jnp.zeros((CLIP_MAX,) + home_rows.shape[1:], home_rows.dtype)], axis=0
    )
    cot_pad = jnp.concatenate(
        [home_cot, jnp.zeros((CLIP_MAX, home_cot.shape[1]), home_cot.dtype)], axis=0
    )
    send_off = jnp.zeros((), jnp.int32)
    sending = jnp.zeros((), jnp.bool_)
    box_len = jnp.zeros((), jnp.int32)
    receiving = jnp.zeros((), jnp.bool_)
    for step in range(moving.shape[0]):
        source = moving[step, 0]
        which = moving[step, 2]
        mine_out = source == rank
        offset, unused = clip_start(counts, which)
        send_off = jnp.where(mine_out, offset, send_off)
        sending = jnp.logical_or(sending, mine_out)
        source_counts = jnp.sum(jnp.where((ranks == source)[:, None], counts_all, 0), axis=0)
        ignored, length = clip_start(source_counts, which)
        mine_in = moving[step, 1] == rank
        box_len = jnp.where(mine_in, length, box_len)
        receiving = jnp.logical_or(receiving, mine_in)
    out_rows = jnp.where(
        sending,
        lax.dynamic_slice_in_dim(padded, send_off, CLIP_MAX, 0),
        jnp.zeros((), jnp.bfloat16),
    )
    out_cot = jnp.where(
        sending,
        lax.dynamic_slice_in_dim(cot_pad, send_off, CLIP_MAX, 0),
        jnp.zeros((), jnp.bfloat16),
    )
    got_rows, got_cot = passed_along((out_rows, out_cot), "dp", 1)
    box_rows = jnp.where(receiving, got_rows, jnp.zeros((), jnp.bfloat16))
    box_cot = jnp.where(receiving, got_cot, jnp.zeros((), jnp.bfloat16))
    places = jnp.arange(CLIP_MAX, dtype=jnp.int32)
    box_live = places < box_len
    box_allowed = jnp.broadcast_to(box_live[None, :], (CLIP_MAX, CLIP_MAX))

    def forward(home_in, box_in):
        return (attend(home_in, allowed_home, stays), attend(box_in, box_allowed, box_live))

    (mixed_home, mixed_box), pullback = jax.vjp(forward, home_rows, box_rows)
    weights = lax.all_gather(out_weight, "fsdp", axis=0, tiled=True)
    mixed_all = jnp.concatenate([mixed_home, mixed_box], axis=0)
    cot_all = jnp.concatenate([home_cot, box_cot], axis=0)
    back = lax.dot_general(
        cot_all, weights, (((1,), (1,)), ((), ())), preferred_element_type=jnp.float32
    ).astype(jnp.bfloat16)
    tokens_dev = home_rows.shape[0]
    grad_home, grad_box = pullback((back[:tokens_dev], back[tokens_dev:]))
    shard_rows = out_weight.shape[0]
    rank_sum = lax.psum_scatter(
        lax.dot_general(
            cot_all, mixed_all, (((0,), (0,)), ((), ())), preferred_element_type=jnp.float32
        ).astype(jnp.bfloat16),
        "dp",
        scatter_dimension=0,
        tiled=True,
    ).astype(jnp.float32)
    whole = lax.psum(rank_sum, "fsdp")
    piece = lax.dynamic_slice_in_dim(whole, lax.axis_index("fsdp") * shard_rows, shard_rows, 1)
    weight_grad = jnp.transpose(piece)
    return (grad_home[None, None], grad_box[None, None], weight_grad)


def solution(mesh):
    placed = (
        P("dp", "fsdp", None, None, None),
        P("dp", "fsdp", None, None),
        P(None, "fsdp", None),
        P("fsdp", None, None),
        P("fsdp", None),
    )
    return jax.shard_map(
        local,
        mesh=mesh,
        in_specs=placed,
        out_specs=(
            P("dp", "fsdp", None, None, None),
            P("dp", "fsdp", None, None, None),
            P("fsdp", "dp"),
        ),
        check_vma=False,
    )
```

profile of v0, /device:TPU:128, one launch (start us, length us, event | category | flops | bytes accessed | tf_op | source)
XLA Modules:
  0.0 412.4 jit_solution(16271199381941486053)
XLA Ops:
  8.1 0.7 all-gather.3.cloned.1.call-update
  8.8 1.5 fusion.66
  11.0 0.7 iota_compare_fusion.3
  12.2 0.6 iota_compare_fusion.2
  12.8 0.8 fusion.46
  13.7 0.2 reduce-window.8
  13.8 2.0 fusion.49
  17.1 1.7 fusion.37
  18.8 2.2 fusion.25
  21.1 3.4 collective-permute-start.1
  24.5 1.4 reshape_squeeze.3
  25.9 0.2 slice_reduce_fusion
  26.7 0.7 fusion.67
  27.4 0.1 copy-done.9
  27.5 0.1 copy-done.1
  27.7 0.5 fusion.16
  29.5 1.3 fusion.50
  31.4 0.3 copy.66
  31.6 0.3 convert_element_type.108
  32.6 0.7 broadcast_select_fusion.1
  33.4 0.4 copy.61
  33.8 0.4 fusion.68
  34.2 0.3 fusion.19
  34.5 0.2 copy-done.3
  34.6 0.2 copy.68
  34.8 3.3 convolution_convert_fusion
  38.2 72.7 %all-gather.3.cloned.1.call-done = bf16[64,14,896]{2,1,0:T(8,128)(2,1)} async-done(((bf16[1,14,896]{2,1,0:T(8,128)(2,1)}), bf16[64,14,896]{2,1,0:T(8,128)(2,1)}) %all-gather.3.cloned.1.call-update) | async-done | bytes 1605648 | tf_op jit(solution)/shard_map/all_gather | solution.py:104
  110.9 2.5 reshape.138
  113.4 1.8 convolution_convert_fusion.2
  115.3 0.2 copy.60
  115.5 0.4 reshape.134
  115.9 0.4 copy-done.4
  116.3 1.4 multiply_reduce_fusion
  117.7 1.3 fusion.20
  119.1 0.3 fusion.22
  119.4 0.4 fusion.21
  119.8 1.1 copy.69
  121.0 0.5 fusion.8
  121.5 0.4 fusion.17
  122.0 0.5 copy-done.10
  122.5 0.7 fusion.15
  123.2 0.3 copy-done.8
  123.5 0.6 fusion.14
  124.0 0.3 pad_add_fusion
  124.4 0.8 copy.59
  125.1 1.8 reshape.128
  126.9 277.2 %all-reduce.10 = f32[56,896]{1,0:T(8,128)S(1)} all-reduce(bf16[56,896]{1,0:T(8,128)(2,1)} %reduce-scatter.4.cloned.1.call-done), channel_id=1, replica_groups=mesh['dp'=16,'fsdp'=64] {'fsdp'}, use_global_device_ids=true, to_apply=%region_18.19 | all-reduce | flops 50176 | bytes 301056 | tf_op jit(solution)/shard_map/psum | solution.py:121
  404.2 0.7 copy.70
  (49 shorter events, 1.0 us)
Async XLA Ops:
  8.0 16.5 %copy-start = (bf16[1,1,192,3,896]{4,2,3,1,0:T(8,128)(2,1)S(1)}, bf16[1,1,192,3,896]{4,2,3,1,0:T(8,128)(2,1)}, u32[]{:S(2)}) copy-start(bf16[1,1,192,3,896]{4,2,3,1,0:T(8,128)(2,1)} %param.5) | copy-start | bytes 3096580
  8.0 102.9 %all-gather.3.cloned.1.call-start = ((), (), s32[]{:S(2)}) async-start(), calls=%async_computation.1 | async-start | bytes 1863680 | tf_op jit(solution)/shard_map/all_gather | solution.py:104
  8.7 118.2 %reduce-scatter.4.cloned.1.call-start = ((), (), s32[]{:S(2)}) async-start(), calls=%async_computation.2 | async-start | bytes 1705984
  18.8 13.8 %collective-permute-start = (bf16[128,896]{1,0:T(8,128)(2,1)}, bf16[128,896]{1,0:T(8,128)(2,1)}, u32[]{:S(2)}, u32[]{:S(2)}) collective-permute-start(bf16[128,896]{1,0:T(8,128)(2,1)} %fusion.37), channel_id=1, source_target_pairs={{0,64},{64,128},{128,192},{192,256},{256,320},{320,384},{384,448},... | collective-permute-start | bytes 688136 | tf_op jit(solution)/shard_map/ppermute | solution.py:14
  18.8 7.0 %copy-start.14 = (s32[1,2,3]{2,1,0:T(2,128)S(1)}, s32[1,2,3]{2,1,0:T(2,128)}, u32[]{:S(2)}) copy-start(s32[1,2,3]{2,1,0:T(2,128)} %param.8) | copy-start | bytes 76
  21.1 12.3 %collective-permute-start.1 = (bf16[128,3,896]{2,0,1:T(8,128)(2,1)}, bf16[128,3,896]{2,0,1:T(8,128)(2,1)}, u32[]{:S(2)}, u32[]{:S(2)}) collective-permute-start(bf16[128,3,896]{2,0,1:T(8,128)(2,1)} %fusion.25), channel_id=1, source_target_pairs={{0,64},{64,128},{128,192},{192,256},{256,320},{320,384},{384,448},... | collective-permute-start | bytes 2064392 | tf_op jit(solution)/shard_map/ppermute | solution.py:14
  26.5 0.8 copy-start.12
  26.6 0.8 copy-start.7
  26.7 0.9 copy-start.9
  26.7 1.0 copy-start.1
  33.8 0.9 copy-start.3
  34.2 4.0 copy-start.5
  38.2 75.2 %copy-start.11 = (bf16[1,1,192,896]{3,2,1,0:T(8,128)(2,1)S(1)}, bf16[1,1,192,896]{3,2,1,0:T(8,128)(2,1)}, u32[]{:S(2)}) copy-start(bf16[1,1,192,896]{3,2,1,0:T(8,128)(2,1)} %param.6) | copy-start | bytes 1032196
  115.2 1.1 copy-start.4
  116.3 2.8 copy-start.6
  119.8 1.2 copy-start.2
  121.5 1.0 copy-start.10
  121.5 1.0 copy-start.13
  122.5 1.0 copy-start.8
Sparse Core Ops, SparseCore 0:
  13.0 97.8 all-gather.2
Sparse Core Ops, SparseCore 1:
  38.3 74.0 reduce-scatter.3
where the time goes:
time: 413 us; the launch traced here: 412 us
  blocking collectives  277 us (67%)
  waiting for transfers between devices  73.4 us (18%)
  between operations  20.9 us (5%)
  local copies, waits for them, and re-layouts  13.6 us (3%)
  matrix products  12.6 us (3%)
  other arithmetic  11.2 us (3%)
    psum x1, blocking collectives, local(): whole = lax.psum(rank_sum, 'fsdp')  277 us
    all_gather x1, waiting for transfers between devices, local(): weights = lax.all_gather(out_weight, 'fsdp', axis=0, tiled=True)  72.7 us
  transfers between devices with their start and end apart: 4, of which 1 were waited for; matrix products, arithmetic and copies ran while one was open for 8% of the time, Pallas kernels for 0%

commit v1 on v0

v1 whole, which is shorter than its diff:
```python
import jax
import jax.numpy as jnp
import numpy as np
from jax import lax
from jax.experimental import pallas as pl
from jax.experimental.pallas import tpu as pltpu
from jax.sharding import PartitionSpec as P

HEADS = 8
HSIZE = 112
TOK = 192
CLIP_MAX = 128
FEAT = 896
NZ, NCORE, NY, NX = 8, 2, 8, 8
ROWS = 14
COLS = 56
SCALE = HSIZE ** (-0.5)
TILE = 128
VMEM_BYTES = 48 * 1024 * 1024

Z_GROUPS = [[z * NCORE + c for z in range(NZ)] for c in range(NCORE)]
Y_GROUPS = [[y * NX + x for y in range(NY)] for x in range(NX)]
X_GROUPS = [[y * NX + x for x in range(NX)] for y in range(NY)]
NT = (((1,), (1,)), ((), ()))
NN = (((1,), (0,)), ((), ()))
TN = (((0,), (0,)), ((), ()))


def spread_rows():
    pick = np.zeros((2 * 8 * NY * NX, FEAT), np.float32)
    for b in range(2):
        for f in range(NY * NX):
            for i in range(ROWS // 2):
                pick[b * 512 + 8 * f + i, ROWS * f + 2 * i + b] = 1.0
    return pick.astype(jnp.bfloat16)


def gathered_rows():
    pick = np.zeros((16 * NY * NX, FEAT), np.float32)
    for x in range(NX):
        for y in range(NY):
            for k in range(ROWS):
                pick[(x * NY + y) * 16 + k, ROWS * (y * NX + x) + k] = 1.0
    return pick.astype(jnp.bfloat16)


def dot(a, b, dims):
    return lax.dot_general(a, b, dims, preferred_element_type=jnp.float32)


def window(head):
    low = HSIZE * head
    start = TILE * (low // TILE)
    stop = TILE * (-(-(low + HSIZE) // TILE))
    return start, stop


def own_lanes(head):
    start, stop = window(head)
    lane = lax.broadcasted_iota(jnp.int32, (1, stop - start), 1) + start
    return (lane >= HSIZE * head) & (lane < HSIZE * (head + 1))


def kept(mask, value):
    return jnp.where(mask, value, jnp.zeros((), value.dtype))


def clip_ends(len_ref, rank):
    first = len_ref[0, rank]
    return first, first + len_ref[1, rank]


def forward_body(len_ref, qkv_ref, cot_ref, pick_ref, own_ref, other_ref, prob_ref, mix_ref):
    rank = lax.axis_index("dp")
    first, second = clip_ends(len_ref, rank)

    def segment(shape, dim):
        place = lax.broadcasted_iota(jnp.int32, shape, dim)
        return (place >= first).astype(jnp.int32) + (place >= second).astype(jnp.int32)

    allowed = segment((TOK, TOK), 0) == segment((TOK, TOK), 1)
    tiles = [None] * (FEAT // TILE)
    for head in range(HEADS):
        start, stop = window(head)
        lanes = own_lanes(head)
        query = kept(lanes, qkv_ref[0, :, start:stop])
        value = kept(lanes, qkv_ref[2, :, start:stop])
        scores = dot(query, qkv_ref[1, :, start:stop], NT) * SCALE
        scores = jnp.where(allowed, scores, -1000000000.0)
        peak = jnp.max(scores, axis=1, keepdims=True)
        grown = jnp.exp(scores - peak)
        probs = (grown * (1.0 / jnp.sum(grown, axis=1, keepdims=True))).astype(jnp.bfloat16)
        prob_ref[head] = probs
        part = dot(probs, value, NN)
        for tile in range(start // TILE, stop // TILE):
            piece = part[:, tile * TILE - start:(tile + 1) * TILE - start]
            tiles[tile] = piece if tiles[tile] is None else tiles[tile] + piece
            if HSIZE * (head + 1) >= TILE * (tile + 1):
                mix_ref[:, tile * TILE:(tile + 1) * TILE] = tiles[tile].astype(jnp.bfloat16)

    spread = dot(pick_ref[...], mix_ref[...], NT).astype(jnp.bfloat16)
    half = spread.shape[0] // 2
    core = lax.rem(rank, NCORE)
    cot = cot_ref[...]
    wide = cot.astype(jnp.float32)
    up = pltpu.roll(wide, COLS, 1).astype(jnp.bfloat16)
    down = pltpu.roll(wide, FEAT - COLS, 1).astype(jnp.bfloat16)
    lane = lax.broadcasted_iota(jnp.int32, (1, FEAT), 1)
    low = lax.rem(lane, 2 * COLS) < COLS
    at_zero = jnp.broadcast_to(core, (1, FEAT)) == 0
    zero = jnp.zeros((), jnp.bfloat16)
    straight_low = jnp.where(low, cot, zero)
    straight_high = jnp.where(low, zero, cot)
    moved_low = jnp.where(low, down, zero)
    moved_high = jnp.where(low, zero, up)
    own_ref[...] = (
        dot(spread[:half], jnp.where(at_zero, straight_low, moved_low), NN)
        + dot(spread[half:], jnp.where(at_zero, moved_high, straight_high), NN)
    ).astype(jnp.bfloat16)
    other_ref[...] = (
        dot(spread[:half], jnp.where(at_zero, moved_low, straight_low), NN)
        + dot(spread[half:], jnp.where(at_zero, straight_high, moved_high), NN)
    ).astype(jnp.bfloat16)


def backward_body(
    len_ref, move_ref, qkv_ref, cot_ref, weight_ref, pick_ref, prob_ref,
    home_ref, send_ref, back_ref, full_ref,
):
    rank = lax.axis_index("dp")
    first, second = clip_ends(len_ref, rank)
    begin = jnp.int32(0)
    count = jnp.int32(0)
    for step in range(move_ref.shape[0]):
        mine = move_ref[step, 0] == rank
        clip = move_ref[step, 2]
        clip_begin = jnp.where(clip == 0, 0, jnp.where(clip == 1, first, second))
        clip_end = jnp.where(clip == 0, first, jnp.where(clip == 1, second, TOK))
        begin = jnp.where(mine, clip_begin, begin)
        count = jnp.where(mine, clip_end - clip_begin, count)

    packed = dot(cot_ref[...], weight_ref[...], NT).astype(jnp.bfloat16)
    back_ref[...] = dot(packed, pick_ref[...], NN).astype(jnp.bfloat16)

    place = lax.broadcasted_iota(jnp.int32, (TOK, TILE), 0)
    stays = (place < begin) | (place >= begin + count)
    tiles = [[None] * (FEAT // TILE) for _ in range(3)]
    for head in range(HEADS):
        start, stop = window(head)
        lanes = own_lanes(head)
        query = kept(lanes, qkv_ref[0, :, start:stop])
        key = kept(lanes, qkv_ref[1, :, start:stop])
        back = kept(lanes, back_ref[:, start:stop])
        grad_p = dot(back, qkv_ref[2, :, start:stop], NT)
        probs = prob_ref[head]
        wide = probs.astype(jnp.float32)
        weighted = wide * grad_p
        grad_s = weighted - wide * jnp.sum(weighted, axis=1, keepdims=True)
        grad_s = (grad_s * SCALE).astype(jnp.bfloat16)
        parts = (
            dot(grad_s, key, NN),
            dot(grad_s, query, TN),
            dot(probs, back, TN),
        )
        for which, part in enumerate(parts):
            for tile in range(start // TILE, stop // TILE):
                piece = part[:, tile * TILE - start:(tile + 1) * TILE - start]
                held = tiles[which][tile]
                held = piece if held is None else held + piece
                tiles[which][tile] = held
                if HSIZE * (head + 1) >= TILE * (tile + 1):
                    at = slice(tile * TILE, (tile + 1) * TILE)
                    full_ref[which, :, at] = held.astype(jnp.bfloat16)
                    home_ref[which, :, at] = jnp.where(stays, held, 0.0).astype(jnp.bfloat16)

    row = lax.broadcasted_iota(jnp.int32, (CLIP_MAX, TOK), 0)
    col = lax.broadcasted_iota(jnp.int32, (CLIP_MAX, TOK), 1)
    pick = ((col == row + begin) & (row < count)).astype(jnp.float32).astype(jnp.bfloat16)
    for which in range(3):
        send_ref[which] = dot(pick, full_ref[which], NN).astype(jnp.bfloat16)


def column_body(got_ref, out_ref):
    total = jnp.sum(got_ref[...].astype(jnp.float32), axis=0)
    for z in range(NZ):
        out_ref[z, :, :2 * COLS] = total[:, 2 * COLS * z:2 * COLS * (z + 1)]
        out_ref[z, :, 2 * COLS:] = jnp.zeros((8, TILE - 2 * COLS), jnp.float32)


def in_vmem():
    return pl.BlockSpec(memory_space=pltpu.VMEM)


def in_smem():
    return pl.BlockSpec(memory_space=pltpu.SMEM)


def shape_of(shape, dtype):
    return jax.ShapeDtypeStruct(shape, dtype)


def forward(counts, qkv, cot, pick):
    return pl.pallas_call(
        forward_body,
        out_shape=(
            shape_of((512, FEAT), jnp.bfloat16),
            shape_of((512, FEAT), jnp.bfloat16),
            shape_of((HEADS, TOK, TOK), jnp.bfloat16),
        ),
        in_specs=[in_smem()] + [in_vmem()] * 3,
        out_specs=(in_vmem(),) * 3,
        scratch_shapes=[pltpu.VMEM((TOK, FEAT), jnp.bfloat16)],
        compiler_params=pltpu.CompilerParams(vmem_limit_bytes=VMEM_BYTES),
        cost_estimate=pl.CostEstimate(flops=2_000_000_000, bytes_accessed=8_000_000, transcendentals=300_000),
        name="forward",
    )(counts, qkv, cot, pick)


def backward(counts, moving, qkv, cot, weights, pick, probs):
    return pl.pallas_call(
        backward_body,
        out_shape=(
            shape_of((3, TOK, FEAT), jnp.bfloat16),
            shape_of((3, CLIP_MAX, FEAT), jnp.bfloat16),
        ),
        in_specs=[in_smem()] * 2 + [in_vmem()] * 5,
        out_specs=(in_vmem(),) * 2,
        scratch_shapes=[
            pltpu.VMEM((TOK, FEAT), jnp.bfloat16),
            pltpu.VMEM((3, TOK, FEAT), jnp.bfloat16),
        ],
        compiler_params=pltpu.CompilerParams(vmem_limit_bytes=VMEM_BYTES),
        cost_estimate=pl.CostEstimate(flops=2_000_000_000, bytes_accessed=8_000_000, transcendentals=0),
        name="backward",
    )(counts, moving, qkv, cot, weights, pick, probs)


def column_sum(got):
    return pl.pallas_call(
        column_body,
        out_shape=shape_of((NZ, 8, TILE), jnp.float32),
        in_specs=[in_vmem()],
        out_specs=in_vmem(),
        name="column_sum",
    )(got)


def local(qkv, grad_out, lengths, moves, out_weight):
    rows = jnp.transpose(qkv[0, 0], (1, 0, 2))
    cot = grad_out[0, 0]
    counts = jnp.transpose(lengths[:, 0])
    moving = moves[0]
    spread = jnp.asarray(spread_rows())
    gathered = jnp.asarray(gathered_rows())

    with jax.named_scope("weights_y"):
        shard = jnp.pad(out_weight, ((0, 16 - ROWS), (0, 0)))
        copies = jnp.broadcast_to(shard[None], (NY,) + shard.shape)
        column = lax.all_to_all(copies, "fsdp", 0, 0, tiled=True, axis_index_groups=Y_GROUPS)
    column, rows, cot = lax.optimization_barrier((column, rows, cot))
    with jax.named_scope("weights_x"):
        weights = lax.all_gather(
            column.reshape(NY * 16, FEAT), "fsdp", axis=0, tiled=True, axis_index_groups=X_GROUPS
        )

    own, other, probs = forward(counts, rows, cot, spread)
    swapped = lax.ppermute(
        other, "dp", [(z * NCORE + c, z * NCORE + 1 - c) for z in range(NZ) for c in range(NCORE)]
    )
    pair = (own.astype(jnp.float32) + swapped.astype(jnp.float32)).astype(jnp.bfloat16)
    with jax.named_scope("reduce_fsdp"):
        got = lax.all_to_all(pair.reshape(NY * NX, 8, FEAT), "fsdp", 0, 0, tiled=True)
    weights, got = lax.optimization_barrier((weights, got))

    home, send = backward(counts, moving, rows, cot, weights, gathered, probs)
    got, send = lax.optimization_barrier((got, send))
    inbox = lax.ppermute(send, "dp", [(i, (i + 1) % (NZ * NCORE)) for i in range(NZ * NCORE)])

    with jax.named_scope("reduce_z"):
        parts = lax.all_to_all(column_sum(got), "dp", 0, 0, tiled=True, axis_index_groups=Z_GROUPS)
    total = jnp.sum(parts, axis=0)[:ROWS // 2, :2 * COLS]
    weight_grad = total.reshape(ROWS, COLS)
    return (
        jnp.transpose(home, (1, 0, 2))[None, None],
        jnp.transpose(inbox, (1, 0, 2))[None, None],
        weight_grad,
    )


def solution(mesh):
    placed = (
        P("dp", "fsdp", None, None, None),
        P("dp", "fsdp", None, None),
        P(None, "fsdp", None),
        P("fsdp", None, None),
        P("fsdp", None),
    )
    return jax.shard_map(
        local,
        mesh=mesh,
        in_specs=placed,
        out_specs=(
            P("dp", "fsdp", None, None, None),
            P("dp", "fsdp", None, None, None),
            P("fsdp", "dp"),
        ),
        check_vma=False,
    )
```

time: 413 us -> 129 us (0.31)
  the two profiles are of different devices: /device:TPU:128 before, /device:TPU:1 now
where the time goes in v1:
time: 129 us; the launch traced here: 128 us
  blocking collectives  70.4 us (55%)
  starting transfers between devices  17 us (13%)
  between operations  14.1 us (11%)
  Pallas kernels  12.7 us (10%)
  local copies, waits for them, and re-layouts  8.18 us (6%)
  waiting for transfers between devices  5.55 us (4%)
    all_to_all x1, blocking collectives, local(): lax.all_to_all(pair.reshape(NY * NX, 8, FEAT), 'fsdp', 0, 0, tiled=True)  40.2 us
    all_to_all x1, blocking collectives, local(): lax.all_to_all(copies, 'fsdp', 0, 0, tiled=True, axis_index_groups=Y_GROUPS)  17 us
    all_to_all x1, blocking collectives, local(): lax.all_to_all(column_sum(got), 'dp', 0, 0, tiled=True, axis_index_groups...  13.3 us
    ppermute x1, starting transfers between devices, local(): lax.ppermute(other, 'dp', [(z * NCORE + c, z * NCORE + 1 - c) for z in ra...  12.3 us
    unnamed x16, local copies, waits for them, and re-layouts  6.74 us
    pallas_call x1, Pallas kernels, backward(): pl.pallas_call(backward_body, out_shape=(shape_of((3, TOK, FEAT), jnp.bfl...  6.32 us
    ppermute x1, starting transfers between devices, local(): lax.ppermute(send, 'dp', [(i, (i + 1) % (NZ * NCORE)) for i in range(NZ *...  4.67 us
    pallas_call x1, Pallas kernels, forward(): pl.pallas_call(forward_body, out_shape=(shape_of((512, FEAT), jnp.bfloat1...  4.37 us
  transfers between devices with their start and end apart: 3, of which 2 were waited for; matrix products, arithmetic and copies ran while one was open for 1% of the time, Pallas kernels for 5%

profile of v1, /device:TPU:1, one launch (start us, length us, event | category | flops | bytes accessed | tf_op | source)
XLA Modules:
  0.0 128.1 jit_solution(6951687172565215217)
XLA Ops:
  7.2 0.0 all-gather.2.cloned.1.call-start
  7.2 0.8 pad.4
  8.0 17.0 %all_to_all.15 = bf16[8,16,896]{2,1,0:T(8,128)(2,1)} all-to-all(bf16[8,16,896]{2,1,0:T(8,128)(2,1)S(1)} %broadcast_in_dim.12), channel_id=1, replica_groups={{0,8,16,24,32,40,48,56},{1,9,17,25,33,41,49,57},{2,10,18,26,34,42,50,58..., dimensions={0} | all-to-all | bytes 458752 | tf_op jit(solution)/shard_map/weights_y/all_to_all | solution.py:259
  25.0 0.0 all-gather.2.cloned.1.call-update
  25.0 0.7 copy.12
  25.7 0.0 copy-start.1
  25.7 1.2 copy-done.1
  26.9 0.0 copy-start.3
  26.9 1.0 copy-done.3
  27.9 0.0 copy-start.6
  27.9 1.5 %copy-done.6 = bf16[1024,896]{1,0:T(8,128)(2,1)S(1)} copy-done((bf16[1024,896]{1,0:T(8,128)(2,1)S(1)}, bf16[1024,896]{1,0:T(8,128)(2,1)}, u32[]{:S(2)}) %copy-start.6) | copy-done | bytes 1835032
  29.4 4.4 %forward.1 = (bf16[512,896]{1,0:T(8,128)(2,1)S(1)}, bf16[512,896]{1,0:T(8,128)(2,1)S(1)}, bf16[8,192,192]{2,1,0:T(8,128)(2,1)S(1)}) custom-call(s32[3,16]{1,0:T(4,128)S(1)} %bitcast.20, bf16[3,192,896]{2,1,0:T(8,128)(2,1)S(1)} %bitcast.22, bf16[192,896]{1,0:T(8,128)(2,1)S(1)} %bitcast.24, bf16[1024,896]{1,0:T(8,128)(2,1)S(1)} %copy-done.6), custom_call_target="tpu_custom_call" | custom-call | flops 2000000000 | bytes 8000000 | tf_op jit(solution)/shard_map/forward/pallas_call | solution.py:203
  33.8 12.3 %collective-permute-start = (bf16[512,896]{1,0:T(8,128)(2,1)S(1)}, bf16[512,896]{1,0:T(8,128)(2,1)S(1)}, u32[]{:S(2)}, u32[]{:S(2)}) collective-permute-start(bf16[512,896]{1,0:T(8,128)(2,1)S(1)} %get-tuple-element.19), channel_id=1, source_target_pairs={{0,64},{64,0},{128,192},{192,128},{256,320},{320,256},{384,448},{4... | collective-permute-start | bytes 2752520 | tf_op jit(solution)/shard_map/ppermute | solution.py:267
  46.0 2.1 %collective-permute-done = bf16[512,896]{1,0:T(8,128)(2,1)S(1)} collective-permute-done((bf16[512,896]{1,0:T(8,128)(2,1)S(1)}, bf16[512,896]{1,0:T(8,128)(2,1)S(1)}, u32[]{:S(2)}, u32[]{:S(2)}) %collective-permute-start) | collective-permute-done | bytes 917536 | tf_op jit(solution)/shard_map/ppermute | solution.py:267
  48.1 0.0 copy-start.2
  48.1 0.0 copy-start.4
  48.1 0.0 copy-start.5
  48.1 0.2 fusion
  48.3 40.2 %all_to_all.16.got_ref = bf16[64,8,896]{2,1,0:T(8,128)(2,1)} all-to-all(bf16[64,8,896]{2,1,0:T(8,128)(2,1)S(1)} %fusion), channel_id=1, replica_groups=mesh['dp'=16,'fsdp'=64] {'fsdp'}, dimensions={0} | all-to-all | bytes 1835008 | tf_op jit(solution)/shard_map/reduce_fsdp/all_to_all | solution.py:272
  88.5 3.5 %all-gather.2.cloned.1.call-done.weight_ref = bf16[1024,896]{1,0:T(8,128)(2,1)} async-done(((bf16[128,896]{1,0:T(8,128)(2,1)}), bf16[1024,896]{1,0:T(8,128)(2,1)}) %all-gather.2.cloned.1.call-update) | async-done | bytes 1835024 | tf_op jit(solution)/shard_map/weights_x/all_gather | solution.py:262
  92.0 0.0 copy-done.2
  92.0 0.0 copy-done.4
  92.0 0.0 copy-done.5
  92.0 0.0 copy-start
  92.0 1.5 %copy-done = bf16[1024,896]{1,0:T(8,128)(2,1)S(1)} copy-done((bf16[1024,896]{1,0:T(8,128)(2,1)S(1)}, bf16[1024,896]{1,0:T(8,128)(2,1)}, u32[]{:S(2)}) %copy-start) | copy-done | bytes 1835032
  93.5 6.3 %backward.1 = (bf16[3,192,896]{2,1,0:T(8,128)(2,1)}, bf16[3,128,896]{2,1,0:T(8,128)(2,1)S(1)}) custom-call(s32[3,16]{1,0:T(4,128)S(1)} %bitcast.21, s32[2,3]{1,0:T(2,128)S(1)} %bitcast.26, bf16[3,192,896]{2,1,0:T(8,128)(2,1)S(1)} %bitcast.23, bf16[192,896]{1,0:T(8,128)(2,1)S(1)} %bitcast.25, bf16[1024,896]{1,0:T(8,128)(2,1)S(1)} %copy-done, ...), custom_call_target="tpu_custom_call" | custom-call | flops 2000000000 | bytes 8000000 | tf_op jit(solution)/shard_map/backward/pallas_call | solution.py:220
  99.8 4.7 %collective-permute-start.1 = (bf16[3,128,896]{2,1,0:T(8,128)(2,1)S(1)}, bf16[3,128,896]{2,1,0:T(8,128)(2,1)S(1)}, u32[]{:S(2)}, u32[]{:S(2)}) collective-permute-start(bf16[3,128,896]{2,1,0:T(8,128)(2,1)S(1)} %get-tuple-element.25), channel_id=1, source_target_pairs={{0,64},{64,128},{128,192},{192,256},{256,320},{320,384},{384,448},... | collective-permute-start | bytes 2064392 | tf_op jit(solution)/shard_map/ppermute | solution.py:277
  104.5 2.0 %column_sum.1 = f32[8,8,128]{2,1,0:T(8,128)} custom-call(bf16[64,8,896]{2,1,0:T(8,128)(2,1)} %all_to_all.16.got_ref), custom_call_target="tpu_custom_call" | custom-call | tf_op jit(solution)/shard_map/reduce_z/column_sum/pallas_call | solution.py:239
  106.5 13.3 %all_to_all.17 = f32[8,8,128]{2,1,0:T(8,128)S(1)} all-to-all(f32[8,8,128]{2,1,0:T(8,128)} %column_sum.1), channel_id=1, replica_groups={{0,128,256,384,512,640,768,896},{64,192,320,448,576,704,832,960},{1,129..., dimensions={0} | all-to-all | bytes 65536 | tf_op jit(solution)/shard_map/reduce_z/all_to_all | solution.py:280
  119.8 0.7 reshape.18
  120.4 0.0 collective-permute-done.1
  120.4 0.8 copy.14
  (2 shorter events, 0.0 us)
Async XLA Ops:
  7.2 84.8 %all-gather.2.cloned.1.call-start = ((), (), s32[]{:S(2)}) async-start(), calls=%async_computation.3 | async-start | bytes 2064384 | tf_op jit(solution)/shard_map/weights_x/all_gather | solution.py:262
  25.7 1.2 copy-start.1
  26.9 1.0 copy-start.3
  27.9 1.5 %copy-start.6 = (bf16[1024,896]{1,0:T(8,128)(2,1)S(1)}, bf16[1024,896]{1,0:T(8,128)(2,1)}, u32[]{:S(2)}) copy-start(bf16[1024,896]{1,0:T(8,128)(2,1)} %constant.9.clone.pick_ref) | copy-start | bytes 5505028
  33.8 14.3 %collective-permute-start = (bf16[512,896]{1,0:T(8,128)(2,1)S(1)}, bf16[512,896]{1,0:T(8,128)(2,1)S(1)}, u32[]{:S(2)}, u32[]{:S(2)}) collective-permute-start(bf16[512,896]{1,0:T(8,128)(2,1)S(1)} %get-tuple-element.19), channel_id=1, source_target_pairs={{0,64},{64,0},{128,192},{192,128},{256,320},{320,256},{384,448},{4... | collective-permute-start | bytes 2752520 | tf_op jit(solution)/shard_map/ppermute | solution.py:267
  48.1 43.9 %copy-start.2 = (bf16[1,1,192,3,896]{4,2,3,1,0:T(8,128)(2,1)S(1)}, bf16[1,1,192,3,896]{4,2,3,1,0:T(8,128)(2,1)}, u32[]{:S(2)}) copy-start(bf16[1,1,192,3,896]{4,2,3,1,0:T(8,128)(2,1)} %param.7) | copy-start | bytes 3096580
  48.1 43.9 %copy-start.4 = (bf16[1,1,192,896]{3,2,1,0:T(8,128)(2,1)S(1)}, bf16[1,1,192,896]{3,2,1,0:T(8,128)(2,1)}, u32[]{:S(2)}) copy-start(bf16[1,1,192,896]{3,2,1,0:T(8,128)(2,1)} %param.8) | copy-start | bytes 1032196
  48.1 43.9 %copy-start.5 = (s32[1,2,3]{2,1,0:T(2,128)S(1)}, s32[1,2,3]{2,1,0:T(2,128)}, u32[]{:S(2)}) copy-start(s32[1,2,3]{2,1,0:T(2,128)} %param.10) | copy-start | bytes 76
  92.0 1.5 %copy-start = (bf16[1024,896]{1,0:T(8,128)(2,1)S(1)}, bf16[1024,896]{1,0:T(8,128)(2,1)}, u32[]{:S(2)}) copy-start(bf16[1024,896]{1,0:T(8,128)(2,1)} %all-gather.2.cloned.1.call-done.weight_ref) | copy-start | bytes 5505028
  99.8 20.6 %collective-permute-start.1 = (bf16[3,128,896]{2,1,0:T(8,128)(2,1)S(1)}, bf16[3,128,896]{2,1,0:T(8,128)(2,1)S(1)}, u32[]{:S(2)}, u32[]{:S(2)}) collective-permute-start(bf16[3,128,896]{2,1,0:T(8,128)(2,1)S(1)} %get-tuple-element.25), channel_id=1, source_target_pairs={{0,64},{64,128},{128,192},{192,256},{256,320},{320,384},{384,448},... | collective-permute-start | bytes 2064392 | tf_op jit(solution)/shard_map/ppermute | solution.py:277
Sparse Core Ops, SparseCore 0:
  25.1 66.7 all-gather.1

commit v2 on v1

v2 whole, which is shorter than its diff:
```python
import jax
import jax.numpy as jnp
import numpy as np
from jax import lax
from jax.experimental import pallas as pl
from jax.experimental.pallas import tpu as pltpu
from jax.sharding import PartitionSpec as P

HEADS = 8
HSIZE = 112
TOK = 192
CLIP_MAX = 128
FEAT = 896
NZ, NCORE, NY, NX = 8, 2, 8, 8
ROWS = 14
COLS = 56
SCALE = HSIZE ** (-0.5)
TILE = 128
VMEM_BYTES = 48 * 1024 * 1024

Y_GROUPS = [[y * NX + x for y in range(NY)] for x in range(NX)]
X_GROUPS = [[y * NX + x for x in range(NX)] for y in range(NY)]
PLANE_GROUPS = [
    [(z * NCORE + c) * NY * NX + y * NX + x for z in range(NZ) for y in range(NY)]
    for c in range(NCORE)
    for x in range(NX)
]
NT = (((1,), (1,)), ((), ()))
NN = (((1,), (0,)), ((), ()))
TN = (((0,), (0,)), ((), ()))


def dot(a, b, dims):
    return lax.dot_general(a, b, dims, preferred_element_type=jnp.float32)


def window(head):
    low = HSIZE * head
    start = TILE * (low // TILE)
    stop = TILE * (-(-(low + HSIZE) // TILE))
    return start, stop


def own_lanes(head):
    start, stop = window(head)
    lane = lax.broadcasted_iota(jnp.int32, (1, stop - start), 1) + start
    return (lane >= HSIZE * head) & (lane < HSIZE * (head + 1))


def gathered_lanes(width):
    row = lax.broadcasted_iota(jnp.int32, (TILE, width), 0)
    lane = lax.broadcasted_iota(jnp.int32, (TILE, width), 1)
    inner = row & 15
    return jnp.where(inner < ROWS, lane - (row >> 4) * ROWS - inner, -1)


def kept(mask, value):
    return jnp.where(mask, value, jnp.zeros((), value.dtype))


def as_bf16(mask):
    return mask.astype(jnp.float32).astype(jnp.bfloat16)


def clip_ends(len_ref, rank):
    first = len_ref[0, rank]
    return first, first + len_ref[1, rank]


def forward_body(len_ref, qkv_ref, cot_ref, own_ref, other_ref, prob_ref, mix_ref, term_ref):
    rank = lax.axis_index("dp")
    first, second = clip_ends(len_ref, rank)

    def segment(shape, dim):
        place = lax.broadcasted_iota(jnp.int32, shape, dim)
        return (place >= first).astype(jnp.int32) + (place >= second).astype(jnp.int32)

    allowed = segment((TOK, TOK), 0) == segment((TOK, TOK), 1)
    for head in range(HEADS):
        start, stop = window(head)
        lanes = own_lanes(head)
        query = kept(lanes, qkv_ref[0, :, start:stop])
        value = kept(lanes, qkv_ref[2, :, start:stop])
        scores = dot(query, qkv_ref[1, :, start:stop], NT) * SCALE
        scores = jnp.where(allowed, scores, -1000000000.0)
        peak = jnp.max(scores, axis=1, keepdims=True)
        grown = jnp.exp(scores - peak)
        probs = (grown * (1.0 / jnp.sum(grown, axis=1, keepdims=True))).astype(jnp.bfloat16)
        prob_ref[head] = probs
        mixed = dot(probs, value, NN)
        offset = HSIZE * head - start
        if offset:
            mixed = pltpu.roll(mixed, stop - start - offset, 1)
        mix_ref[:, head * TILE:(head + 1) * TILE] = mixed[:, :TILE].astype(jnp.bfloat16)

    term_ref[...] = dot(cot_ref[...], mix_ref[...], TN)
    core = lax.rem(rank, NCORE)
    for z in range(NZ):
        for ref, part in ((own_ref, core), (other_ref, 1 - core)):
            rows = pl.ds(pl.multiple_of(2 * COLS * z + COLS * part, 8), COLS)
            for y in range(NY):
                ref[z * NY + y] = term_ref[rows, y * TILE:(y + 1) * TILE].astype(jnp.bfloat16)


def backward_body(
    len_ref, move_ref, qkv_ref, cot_ref, weight_ref, prob_ref,
    home_ref, send_ref, full_ref,
):
    rank = lax.axis_index("dp")
    first, second = clip_ends(len_ref, rank)
    begin = jnp.int32(0)
    count = jnp.int32(0)
    for step in range(move_ref.shape[0]):
        mine = move_ref[step, 0] == rank
        clip = move_ref[step, 2]
        clip_begin = jnp.where(clip == 0, 0, jnp.where(clip == 1, first, second))
        clip_end = jnp.where(clip == 0, first, jnp.where(clip == 1, second, TOK))
        begin = jnp.where(mine, clip_begin, begin)
        count = jnp.where(mine, clip_end - clip_begin, count)

    place = lax.broadcasted_iota(jnp.int32, (TOK, TILE), 0)
    stays = (place < begin) | (place >= begin + count)
    cot = cot_ref[...]
    tiles = [[None] * (FEAT // TILE) for _ in range(3)]
    for head in range(HEADS):
        start, stop = window(head)
        lanes = own_lanes(head)
        query = kept(lanes, qkv_ref[0, :, start:stop])
        key = kept(lanes, qkv_ref[1, :, start:stop])
        weights = weight_ref[:, head].reshape(TILE, FEAT)
        packed = dot(cot, weights, NT).astype(jnp.bfloat16)
        offset = HSIZE * head - start
        pick = as_bf16(gathered_lanes(stop - start) == offset)
        back = dot(packed, pick, NN).astype(jnp.bfloat16)
        grad_p = dot(back, qkv_ref[2, :, start:stop], NT)
        probs = prob_ref[head]
        wide = probs.astype(jnp.float32)
        weighted = wide * grad_p
        grad_s = weighted - wide * jnp.sum(weighted, axis=1, keepdims=True)
        grad_s = (grad_s * SCALE).astype(jnp.bfloat16)
        parts = (
            dot(grad_s, key, NN),
            dot(grad_s, query, TN),
            dot(probs, back, TN),
        )
        for which, part in enumerate(parts):
            for tile in range(start // TILE, stop // TILE):
                piece = part[:, tile * TILE - start:(tile + 1) * TILE - start]
                held = tiles[which][tile]
                held = piece if held is None else held + piece
                tiles[which][tile] = held
                if HSIZE * (head + 1) >= TILE * (tile + 1):
                    at = slice(tile * TILE, (tile + 1) * TILE)
                    full_ref[which, :, at] = held.astype(jnp.bfloat16)
                    home_ref[which, :, at] = jnp.where(stays, held, 0.0).astype(jnp.bfloat16)

    row = lax.broadcasted_iota(jnp.int32, (CLIP_MAX, TOK), 0)
    col = lax.broadcasted_iota(jnp.int32, (CLIP_MAX, TOK), 1)
    pick = as_bf16((col == row + begin) & (row < count))
    for which in range(3):
        send_ref[which] = dot(pick, full_ref[which], NN).astype(jnp.bfloat16)


def plane_body(got_ref, out_ref, turned_ref):
    total = jnp.sum(got_ref[...].astype(jnp.float32), axis=0)
    total = jnp.concatenate([total, jnp.zeros((TILE - COLS, TILE), jnp.float32)], axis=0)
    turned_ref[...] = jnp.transpose(total)
    out_ref[...] = jnp.zeros(out_ref.shape, jnp.float32)
    for x in range(NX):
        for b in range(2):
            rows = turned_ref[pl.ds(ROWS * x + b, ROWS // 2, stride=2), :]
            out_ref[x, :ROWS // 2, b * COLS:(b + 1) * COLS] = rows[:, :COLS]


def row_body(got_ref, out_ref):
    total = jnp.sum(got_ref[...], axis=0)
    for b in range(2):
        out_ref[pl.ds(b, ROWS // 2, stride=2), :] = total[:ROWS // 2, b * COLS:(b + 1) * COLS]


def in_vmem():
    return pl.BlockSpec(memory_space=pltpu.VMEM)


def in_smem():
    return pl.BlockSpec(memory_space=pltpu.SMEM)


def shape_of(shape, dtype):
    return jax.ShapeDtypeStruct(shape, dtype)


def forward(counts, qkv, cot):
    return pl.pallas_call(
        forward_body,
        out_shape=(
            shape_of((NZ * NY, COLS, TILE), jnp.bfloat16),
            shape_of((NZ * NY, COLS, TILE), jnp.bfloat16),
            shape_of((HEADS, TOK, TOK), jnp.bfloat16),
        ),
        in_specs=[in_smem()] + [in_vmem()] * 2,
        out_specs=(in_vmem(),) * 3,
        scratch_shapes=[
            pltpu.VMEM((TOK, HEADS * TILE), jnp.bfloat16),
            pltpu.VMEM((FEAT, HEADS * TILE), jnp.float32),
        ],
        compiler_params=pltpu.CompilerParams(vmem_limit_bytes=VMEM_BYTES),
        cost_estimate=pl.CostEstimate(flops=2_000_000_000, bytes_accessed=8_000_000, transcendentals=300_000),
        name="forward",
    )(counts, qkv, cot)


def backward(counts, moving, qkv, cot, weights, probs):
    return pl.pallas_call(
        backward_body,
        out_shape=(
            shape_of((3, TOK, FEAT), jnp.bfloat16),
            shape_of((3, CLIP_MAX, FEAT), jnp.bfloat16),
        ),
        in_specs=[in_smem()] * 2 + [in_vmem()] * 4,
        out_specs=(in_vmem(),) * 2,
        scratch_shapes=[pltpu.VMEM((3, TOK, FEAT), jnp.bfloat16)],
        compiler_params=pltpu.CompilerParams(vmem_limit_bytes=VMEM_BYTES),
        cost_estimate=pl.CostEstimate(flops=2_000_000_000, bytes_accessed=8_000_000, transcendentals=0),
        name="backward",
    )(counts, moving, qkv, cot, weights, probs)


def plane_sum(got):
    return pl.pallas_call(
        plane_body,
        out_shape=shape_of((NX, 8, TILE), jnp.float32),
        in_specs=[in_vmem()],
        out_specs=in_vmem(),
        scratch_shapes=[pltpu.VMEM((TILE, TILE), jnp.float32)],
        name="plane_sum",
    )(got)


def row_sum(got):
    return pl.pallas_call(
        row_body,
        out_shape=shape_of((ROWS, COLS), jnp.float32),
        in_specs=[in_vmem()],
        out_specs=in_vmem(),
        name="row_sum",
    )(got)


def local(qkv, grad_out, lengths, moves, out_weight):
    rows = jnp.transpose(qkv[0, 0], (1, 0, 2))
    cot = grad_out[0, 0]
    counts = jnp.transpose(lengths[:, 0])
    moving = moves[0]

    with jax.named_scope("weights_y"):
        shard = jnp.pad(out_weight, ((0, 16 - ROWS), (0, 0)))
        copies = jnp.broadcast_to(shard[None], (NY,) + shard.shape)
        column = lax.all_to_all(copies, "fsdp", 0, 0, tiled=True, axis_index_groups=Y_GROUPS)
    column, counts = lax.optimization_barrier((column, counts))
    with jax.named_scope("weights_x"):
        weights = lax.all_gather(
            column.reshape(NY * 16, FEAT), "fsdp", axis=0, tiled=True, axis_index_groups=X_GROUPS
        )

    own, other, probs = forward(counts, rows, cot)
    swapped = lax.ppermute(
        other, "dp", [(z * NCORE + c, z * NCORE + 1 - c) for z in range(NZ) for c in range(NCORE)]
    )
    pair = (own.astype(jnp.float32) + swapped.astype(jnp.float32)).astype(jnp.bfloat16)
    with jax.named_scope("reduce_zy"):
        got = lax.all_to_all(
            pair, ("dp", "fsdp"), 0, 0, tiled=True, axis_index_groups=PLANE_GROUPS
        )
    weights, got = lax.optimization_barrier((weights, got))

    home, send = backward(
        counts, moving, rows, cot, weights.reshape(NX, NY, 16, FEAT), probs
    )
    got, send = lax.optimization_barrier((got, send))
    inbox = lax.ppermute(send, "dp", [(i, (i + 1) % (NZ * NCORE)) for i in range(NZ * NCORE)])

    with jax.named_scope("reduce_x"):
        parts = lax.all_to_all(plane_sum(got), "fsdp", 0, 0, tiled=True, axis_index_groups=X_GROUPS)
    return (
        jnp.transpose(home, (1, 0, 2))[None, None],
        jnp.transpose(inbox, (1, 0, 2))[None, None],
        row_sum(parts),
    )


def solution(mesh):
    placed = (
        P("dp", "fsdp", None, None, None),
        P("dp", "fsdp", None, None),
        P(None, "fsdp", None),
        P("fsdp", None, None),
        P("fsdp", None),
    )
    return jax.shard_map(
        local,
        mesh=mesh,
        in_specs=placed,
        out_specs=(
            P("dp", "fsdp", None, None, None),
            P("dp", "fsdp", None, None, None),
            P("fsdp", "dp"),
        ),
        check_vma=False,
    )
```

time: 129 us -> 120 us (0.930)
  blocking collectives: 70.4 us -> 48.5 us
  starting transfers between devices: 17 us -> 23.8 us
  waiting for transfers between devices: 5.55 us -> 10.4 us
  Pallas kernels: 12.7 us -> 14.6 us
    all_to_all x3 -> x2, blocking collectives: 70.4 us -> 48.5 us  [the longest x1 35.1 us: local(): lax.all_to_all(pair, ('dp', 'fsdp'), 0, 0, tiled=True, axis_index_groups=...]
    all_to_all x0 -> x1, waiting for transfers between devices: none -> 8.25 us  [local(): lax.all_to_all(copies, 'fsdp', 0, 0, tiled=True, axis_index_groups=Y_GROUPS)]
    all_to_all x0 -> x1, starting transfers between devices: none -> 8.11 us  [local(): lax.all_to_all(copies, 'fsdp', 0, 0, tiled=True, axis_index_groups=Y_GROUPS)]
    all_gather x1, waiting for transfers between devices: 3.45 us -> 0.01 us  [local(): lax.all_gather(column.reshape(NY * 16, FEAT), 'fsdp', axis=0, tiled=True,...]
    ppermute x1, starting transfers between devices: 4.67 us -> 3.29 us  [local(): lax.ppermute(send, 'dp', [(i, (i + 1) % (NZ * NCORE)) for i in range(NZ *...]
    pallas_call x2 -> x3, Pallas kernels: 6.4 us -> 7.47 us  [the longest x1 3.92 us: forward(): pl.pallas_call(forward_body, out_shape=(shape_of((NZ * NY, COLS, TILE), j...]
  transfers between devices with their start and end apart: 3 -> 4, of which waited for: 2 -> 2; matrix products, arithmetic and copies ran while one was open for 1% -> 1% of each run, Pallas kernels for 5% -> 6%
where the time goes in v2:
time: 120 us; the launch traced here: 119 us
  blocking collectives  48.5 us (40%)
  starting transfers between devices  23.8 us (20%)
  Pallas kernels  14.6 us (12%)
  between operations  14.1 us (12%)
  waiting for transfers between devices  10.4 us (9%)
  local copies, waits for them, and re-layouts  7.38 us (6%)
    all_to_all x1, blocking collectives, local(): lax.all_to_all(pair, ('dp', 'fsdp'), 0, 0, tiled=True, axis_index_groups=...  35.1 us
    all_to_all x1, blocking collectives, local(): lax.all_to_all(plane_sum(got), 'fsdp', 0, 0, tiled=True, axis_index_group...  13.5 us
    ppermute x1, starting transfers between devices, local(): lax.ppermute(other, 'dp', [(z * NCORE + c, z * NCORE + 1 - c) for z in ra...  12.4 us
    all_to_all x1, waiting for transfers between devices, local(): lax.all_to_all(copies, 'fsdp', 0, 0, tiled=True, axis_index_groups=Y_GROUPS)  8.25 us
    all_to_all x1, starting transfers between devices, local(): lax.all_to_all(copies, 'fsdp', 0, 0, tiled=True, axis_index_groups=Y_GROUPS)  8.11 us
    pallas_call x1, Pallas kernels, backward(): pl.pallas_call(backward_body, out_shape=(shape_of((3, TOK, FEAT), jnp.bfl...  7.12 us
    unnamed x16, local copies, waits for them, and re-layouts  5.92 us
    pallas_call x1, Pallas kernels, forward(): pl.pallas_call(forward_body, out_shape=(shape_of((NZ * NY, COLS, TILE), j...  3.92 us
  transfers between devices with their start and end apart: 4, of which 2 were waited for; matrix products, arithmetic and copies ran while one was open for 1% of the time, Pallas kernels for 6%

profile of v2, /device:TPU:1, one launch (start us, length us, event | category | flops | bytes accessed | tf_op | source)
XLA Modules:
  0.0 119.0 jit_solution(13358133240542624774)
XLA Ops:
  7.2 0.8 pad.4
  7.9 0.7 broadcast_in_dim.12
  8.6 8.1 %all-to-all-start = ((bf16[8,16,896]{2,1,0:T(8,128)(2,1)}), bf16[8,16,896]{2,1,0:T(8,128)(2,1)S(1)}, u32[]{:S(2)}, u32[]{:S(2)}) async-start(bf16[8,16,896]{2,1,0:T(8,128)(2,1)} %broadcast_in_dim.12), calls=%async_computation | async-start | bytes 458752 | tf_op jit(solution)/shard_map/weights_y/all_to_all | solution.py:259
  16.7 0.0 all-gather.2.cloned.1.call-start
  16.8 0.7 copy.10
  17.5 8.3 %all-to-all-done = bf16[8,16,896]{2,1,0:T(8,128)(2,1)S(1)} async-done(((bf16[8,16,896]{2,1,0:T(8,128)(2,1)}), bf16[8,16,896]{2,1,0:T(8,128)(2,1)S(1)}, u32[]{:S(2)}, u32[]{:S(2)}) %all-to-all-start) | async-done | bytes 229408 | tf_op jit(solution)/shard_map/weights_y/all_to_all | solution.py:259
  25.7 0.0 copy-start.6
  25.7 0.7 copy-done.6
  26.4 0.0 all-gather.2.cloned.1.call-update
  26.4 0.0 copy-start.1
  26.4 1.2 %copy-done.1 = bf16[1,1,192,3,896]{4,2,3,1,0:T(8,128)(2,1)S(1)} copy-done((bf16[1,1,192,3,896]{4,2,3,1,0:T(8,128)(2,1)S(1)}, bf16[1,1,192,3,896]{4,2,3,1,0:T(8,128)(2,1)}, u32[]{:S(2)}) %copy-start.1) | copy-done | bytes 1032216
  27.7 0.0 copy-start.3
  27.7 1.0 copy-done.3
  28.6 3.9 %forward.1 = (bf16[64,56,128]{2,1,0:T(8,128)(2,1)S(1)}, bf16[64,56,128]{2,1,0:T(8,128)(2,1)S(1)}, bf16[8,192,192]{2,1,0:T(8,128)(2,1)S(1)}) custom-call(s32[3,16]{1,0:T(4,128)S(1)} %bitcast.18, bf16[3,192,896]{2,1,0:T(8,128)(2,1)S(1)} %bitcast.21, bf16[192,896]{1,0:T(8,128)(2,1)S(1)} %bitcast.23), custom_call_target="tpu_custom_call" | custom-call | flops 2000000000 | bytes 8000000 | tf_op jit(solution)/shard_map/forward/pallas_call | solution.py:194
  32.6 12.4 %collective-permute-start = (bf16[64,56,128]{2,1,0:T(8,128)(2,1)S(1)}, bf16[64,56,128]{2,1,0:T(8,128)(2,1)S(1)}, u32[]{:S(2)}, u32[]{:S(2)}) collective-permute-start(bf16[64,56,128]{2,1,0:T(8,128)(2,1)S(1)} %get-tuple-element.17), channel_id=1, source_target_pairs={{0,64},{64,0},{128,192},{192,128},{256,320},{320,256},{384,448},{4... | collective-permute-start | bytes 2752520 | tf_op jit(solution)/shard_map/ppermute | solution.py:267
  45.0 2.1 %collective-permute-done = bf16[64,56,128]{2,1,0:T(8,128)(2,1)S(1)} collective-permute-done((bf16[64,56,128]{2,1,0:T(8,128)(2,1)S(1)}, bf16[64,56,128]{2,1,0:T(8,128)(2,1)S(1)}, u32[]{:S(2)}, u32[]{:S(2)}) %collective-permute-start) | collective-permute-done | bytes 917536 | tf_op jit(solution)/shard_map/ppermute | solution.py:267
  47.1 0.0 copy-start.2
  47.1 0.0 copy-start.4
  47.1 0.0 copy-start.5
  47.1 0.2 add_convert_fusion
  47.3 35.1 %all_to_all.15.got_ref = bf16[64,56,128]{2,1,0:T(8,128)(2,1)} all-to-all(bf16[64,56,128]{2,1,0:T(8,128)(2,1)S(1)} %add_convert_fusion), channel_id=1, replica_groups={{0,8,16,24,32,40,48,56,128,136,144,152,160,168,176,184,256,264,272,280,..., dimensions={0} | all-to-all | bytes 1835008 | tf_op jit(solution)/shard_map/reduce_zy/all_to_all | solution.py:272
  82.4 0.0 all-gather.2.cloned.1.call-done
  82.4 0.0 copy-done.2
  82.4 0.0 copy-done.4
  82.4 0.0 copy-done.5
  82.4 0.0 copy-start
  82.4 1.5 %copy-done = bf16[1024,896]{1,0:T(8,128)(2,1)S(1)} copy-done((bf16[1024,896]{1,0:T(8,128)(2,1)S(1)}, bf16[1024,896]{1,0:T(8,128)(2,1)}, u32[]{:S(2)}) %copy-start) | copy-done | bytes 1835032
  83.9 7.1 %backward.1 = (bf16[3,192,896]{2,1,0:T(8,128)(2,1)}, bf16[3,128,896]{2,1,0:T(8,128)(2,1)S(1)}) custom-call(s32[3,16]{1,0:T(4,128)S(1)} %bitcast.19, s32[2,3]{1,0:T(2,128)S(1)} %bitcast.25, bf16[3,192,896]{2,1,0:T(8,128)(2,1)S(1)} %bitcast.22, bf16[192,896]{1,0:T(8,128)(2,1)S(1)} %bitcast.24, bf16[8,8,16,896]{3,2,1,0:T(8,128)(2,1)S(1)} %bitcast.20, ...), custom_call_target="tpu_custom_call" | custom-call | flops 2000000000 | bytes 8000000 | tf_op jit(solution)/shard_map/backward/pallas_call | solution.py:214
  91.0 3.3 %collective-permute-start.1 = (bf16[3,128,896]{2,1,0:T(8,128)(2,1)S(1)}, bf16[3,128,896]{2,1,0:T(8,128)(2,1)S(1)}, u32[]{:S(2)}, u32[]{:S(2)}) collective-permute-start(bf16[3,128,896]{2,1,0:T(8,128)(2,1)S(1)} %get-tuple-element.23), channel_id=1, source_target_pairs={{0,64},{64,128},{128,192},{192,256},{256,320},{320,384},{384,448},... | collective-permute-start | bytes 2064392 | tf_op jit(solution)/shard_map/ppermute | solution.py:281
  94.3 2.1 %plane_sum.1 = f32[8,8,128]{2,1,0:T(8,128)} custom-call(bf16[64,56,128]{2,1,0:T(8,128)(2,1)} %all_to_all.15.got_ref), custom_call_target="tpu_custom_call" | custom-call | tf_op jit(solution)/shard_map/reduce_x/plane_sum/pallas_call | solution.py:230
  96.4 13.5 %all_to_all.16.got_ref = f32[8,8,128]{2,1,0:T(8,128)} all-to-all(f32[8,8,128]{2,1,0:T(8,128)} %plane_sum.1), channel_id=1, replica_groups={{0,1,2,3,4,5,6,7},{8,9,10,11,12,13,14,15},{16,17,18,19,20,21,22,23},{24..., dimensions={0} | all-to-all | bytes 65536 | tf_op jit(solution)/shard_map/reduce_x/all_to_all | solution.py:284
  109.9 1.4 %row_sum.1 = f32[14,56]{1,0:T(8,128)} custom-call(f32[8,8,128]{2,1,0:T(8,128)} %all_to_all.16.got_ref), custom_call_target="tpu_custom_call" | custom-call | tf_op jit(solution)/shard_map/row_sum/pallas_call | solution.py:241
  111.3 0.0 collective-permute-done.1
  111.3 0.8 copy.12
Async XLA Ops:
  8.6 17.1 %all-to-all-start = ((bf16[8,16,896]{2,1,0:T(8,128)(2,1)}), bf16[8,16,896]{2,1,0:T(8,128)(2,1)S(1)}, u32[]{:S(2)}, u32[]{:S(2)}) async-start(bf16[8,16,896]{2,1,0:T(8,128)(2,1)} %broadcast_in_dim.12), calls=%async_computation | async-start | bytes 458752 | tf_op jit(solution)/shard_map/weights_y/all_to_all | solution.py:259
  16.7 65.6 %all-gather.2.cloned.1.call-start = ((), (), s32[]{:S(2)}) async-start(), calls=%async_computation.3 | async-start | bytes 2064384 | tf_op jit(solution)/shard_map/weights_x/all_gather | solution.py:262
  25.7 0.7 copy-start.6
  26.4 1.2 %copy-start.1 = (bf16[1,1,192,3,896]{4,2,3,1,0:T(8,128)(2,1)S(1)}, bf16[1,1,192,3,896]{4,2,3,1,0:T(8,128)(2,1)}, u32[]{:S(2)}) copy-start(bf16[1,1,192,3,896]{4,2,3,1,0:T(8,128)(2,1)} %param.5) | copy-start | bytes 3096580
  27.7 1.0 copy-start.3
  32.6 14.5 %collective-permute-start = (bf16[64,56,128]{2,1,0:T(8,128)(2,1)S(1)}, bf16[64,56,128]{2,1,0:T(8,128)(2,1)S(1)}, u32[]{:S(2)}, u32[]{:S(2)}) collective-permute-start(bf16[64,56,128]{2,1,0:T(8,128)(2,1)S(1)} %get-tuple-element.17), channel_id=1, source_target_pairs={{0,64},{64,0},{128,192},{192,128},{256,320},{320,256},{384,448},{4... | collective-permute-start | bytes 2752520 | tf_op jit(solution)/shard_map/ppermute | solution.py:267
  47.1 35.3 %copy-start.2 = (bf16[1,1,192,3,896]{4,2,3,1,0:T(8,128)(2,1)S(1)}, bf16[1,1,192,3,896]{4,2,3,1,0:T(8,128)(2,1)}, u32[]{:S(2)}) copy-start(bf16[1,1,192,3,896]{4,2,3,1,0:T(8,128)(2,1)} %param.5) | copy-start | bytes 3096580
  47.1 35.3 %copy-start.4 = (bf16[1,1,192,896]{3,2,1,0:T(8,128)(2,1)S(1)}, bf16[1,1,192,896]{3,2,1,0:T(8,128)(2,1)}, u32[]{:S(2)}) copy-start(bf16[1,1,192,896]{3,2,1,0:T(8,128)(2,1)} %param.6) | copy-start | bytes 1032196
  47.1 35.3 %copy-start.5 = (s32[1,2,3]{2,1,0:T(2,128)S(1)}, s32[1,2,3]{2,1,0:T(2,128)}, u32[]{:S(2)}) copy-start(s32[1,2,3]{2,1,0:T(2,128)} %param.8) | copy-start | bytes 76
  82.4 1.5 %copy-start = (bf16[1024,896]{1,0:T(8,128)(2,1)S(1)}, bf16[1024,896]{1,0:T(8,128)(2,1)}, u32[]{:S(2)}) copy-start(bf16[1024,896]{1,0:T(8,128)(2,1)} %all-gather.2.cloned.1.call-done) | copy-start | bytes 5505028
  91.0 20.3 %collective-permute-start.1 = (bf16[3,128,896]{2,1,0:T(8,128)(2,1)S(1)}, bf16[3,128,896]{2,1,0:T(8,128)(2,1)S(1)}, u32[]{:S(2)}, u32[]{:S(2)}) collective-permute-start(bf16[3,128,896]{2,1,0:T(8,128)(2,1)S(1)} %get-tuple-element.23), channel_id=1, source_target_pairs={{0,64},{64,128},{128,192},{192,256},{256,320},{320,384},{384,448},... | collective-permute-start | bytes 2064392 | tf_op jit(solution)/shard_map/ppermute | solution.py:281
Sparse Core Ops, SparseCore 0:
  26.6 49.7 all-gather.1

commit v3 on v2

v3 whole, which is shorter than its diff:
```python
import jax
import jax.numpy as jnp
import numpy as np
from jax import lax
from jax.experimental import pallas as pl
from jax.experimental.pallas import tpu as pltpu
from jax.sharding import PartitionSpec as P

HEADS = 8
HSIZE = 112
TOK = 192
CLIP_MAX = 128
FEAT = 896
NZ, NCORE, NY, NX = 8, 2, 8, 8
ROWS = 14
COLS = 56
SCALE = HSIZE ** (-0.5)
TILE = 128
VMEM_BYTES = 14 * 1024 * 1024

Y_GROUPS = [[y * NX + x for y in range(NY)] for x in range(NX)]
X_GROUPS = [[y * NX + x for x in range(NX)] for y in range(NY)]
PLANE_GROUPS = [
    [(z * NCORE + c) * NY * NX + y * NX + x for z in range(NZ) for y in range(NY)]
    for c in range(NCORE)
    for x in range(NX)
]
NT = (((1,), (1,)), ((), ()))
NN = (((1,), (0,)), ((), ()))
TN = (((0,), (0,)), ((), ()))


def dot(a, b, dims):
    return lax.dot_general(a, b, dims, preferred_element_type=jnp.float32)


def window(head):
    low = HSIZE * head
    start = TILE * (low // TILE)
    stop = TILE * (-(-(low + HSIZE) // TILE))
    return start, stop


def own_lanes(head):
    start, stop = window(head)
    lane = lax.broadcasted_iota(jnp.int32, (1, stop - start), 1) + start
    return (lane >= HSIZE * head) & (lane < HSIZE * (head + 1))


def gathered_lanes(width):
    row = lax.broadcasted_iota(jnp.int32, (TILE, width), 0)
    lane = lax.broadcasted_iota(jnp.int32, (TILE, width), 1)
    inner = row & 15
    return jnp.where(inner < ROWS, lane - (row >> 4) * ROWS - inner, -1)


def kept(mask, value):
    return jnp.where(mask, value, jnp.zeros((), value.dtype))


def as_bf16(mask):
    return mask.astype(jnp.float32).astype(jnp.bfloat16)


def clip_ends(len_ref, rank):
    first = len_ref[0, 0, rank]
    return first, first + len_ref[1, 0, rank]


def moved_clip(len_ref, move_ref, source):
    first, second = clip_ends(len_ref, source)
    begin = jnp.int32(0)
    count = jnp.int32(0)
    for step in range(move_ref.shape[0]):
        mine = move_ref[step, 0] == source
        clip = move_ref[step, 2]
        clip_begin = jnp.where(clip == 0, 0, jnp.where(clip == 1, first, second))
        clip_end = jnp.where(clip == 0, first, jnp.where(clip == 1, second, TOK))
        begin = jnp.where(mine, clip_begin, begin)
        count = jnp.where(mine, clip_end - clip_begin, count)
    return begin, count


def attention(query, key, allowed):
    scores = dot(query, key, NT) * SCALE
    scores = jnp.where(allowed, scores, -1000000000.0)
    peak = jnp.max(scores, axis=1, keepdims=True)
    grown = jnp.exp(scores - peak)
    return grown * (1.0 / jnp.sum(grown, axis=1, keepdims=True))


def pack_body(len_ref, move_ref, qkv_ref, cot_ref, box_ref):
    rank = lax.axis_index("dp")
    begin, count = moved_clip(len_ref, move_ref, rank)
    row = lax.broadcasted_iota(jnp.int32, (CLIP_MAX, TOK), 0)
    col = lax.broadcasted_iota(jnp.int32, (CLIP_MAX, TOK), 1)
    pick = as_bf16((col == row + begin) & (row < count))
    for which in range(3):
        box_ref[which] = dot(pick, qkv_ref[which], NN).astype(jnp.bfloat16)
    box_ref[3] = dot(pick, cot_ref[...], NN).astype(jnp.bfloat16)


def box_body(len_ref, move_ref, box_ref, prob_ref):
    rank = lax.axis_index("dp")
    _, count = moved_clip(len_ref, move_ref, lax.rem(rank + NZ * NCORE - 1, NZ * NCORE))
    row = lax.broadcasted_iota(jnp.int32, (CLIP_MAX, CLIP_MAX), 0)
    col = lax.broadcasted_iota(jnp.int32, (CLIP_MAX, CLIP_MAX), 1)
    for head in range(HEADS):
        start, stop = window(head)
        query = kept(own_lanes(head), box_ref[0, :, start:stop])
        probs = attention(query, box_ref[1, :, start:stop], col < count)
        prob_ref[head] = jnp.where(row < count, probs, 0.0).astype(jnp.bfloat16)


def forward_body(len_ref, qkv_ref, cot_ref, own_ref, other_ref, prob_ref, mix_ref, term_ref):
    rank = lax.axis_index("dp")
    first, second = clip_ends(len_ref, rank)

    def segment(shape, dim):
        place = lax.broadcasted_iota(jnp.int32, shape, dim)
        return (place >= first).astype(jnp.int32) + (place >= second).astype(jnp.int32)

    allowed = segment((TOK, TOK), 0) == segment((TOK, TOK), 1)
    for head in range(HEADS):
        start, stop = window(head)
        lanes = own_lanes(head)
        query = kept(lanes, qkv_ref[0, :, start:stop])
        value = kept(lanes, qkv_ref[2, :, start:stop])
        probs = attention(query, qkv_ref[1, :, start:stop], allowed).astype(jnp.bfloat16)
        prob_ref[head] = probs
        mixed = dot(probs, value, NN)
        offset = HSIZE * head - start
        if offset:
            mixed = pltpu.roll(mixed, stop - start - offset, 1)
        mix_ref[:, head * TILE:(head + 1) * TILE] = mixed[:, :TILE].astype(jnp.bfloat16)

    term_ref[...] = dot(cot_ref[...], mix_ref[...], TN)
    core = lax.rem(rank, NCORE)
    for z in range(NZ):
        for ref, part in ((own_ref, core), (other_ref, 1 - core)):
            rows = pl.ds(pl.multiple_of(2 * COLS * z + COLS * part, 8), COLS)
            for y in range(NY):
                ref[z * NY + y] = term_ref[rows, y * TILE:(y + 1) * TILE].astype(jnp.bfloat16)


class Tiles:
    def __init__(self, ref, mask):
        self.ref = ref
        self.mask = mask
        self.held = [[None] * (FEAT // TILE) for _ in range(3)]

    def add(self, which, head, part):
        start, stop = window(head)
        for tile in range(start // TILE, stop // TILE):
            piece = part[:, tile * TILE - start:(tile + 1) * TILE - start]
            held = self.held[which][tile]
            held = piece if held is None else held + piece
            self.held[which][tile] = held
            if HSIZE * (head + 1) >= TILE * (tile + 1):
                if self.mask is not None:
                    held = jnp.where(self.mask, held, 0.0)
                self.ref[which, :, tile * TILE:(tile + 1) * TILE] = held.astype(jnp.bfloat16)


def add_gradient(tiles, head, rows_ref, probs, back):
    start, stop = window(head)
    lanes = own_lanes(head)
    query = kept(lanes, rows_ref[0, :, start:stop])
    key = kept(lanes, rows_ref[1, :, start:stop])
    grad_p = dot(back, rows_ref[2, :, start:stop], NT)
    wide = probs.astype(jnp.float32)
    weighted = wide * grad_p
    grad_s = weighted - wide * jnp.sum(weighted, axis=1, keepdims=True)
    grad_s = (grad_s * SCALE).astype(jnp.bfloat16)
    tiles.add(0, head, dot(grad_s, key, NN))
    tiles.add(1, head, dot(grad_s, query, TN))
    tiles.add(2, head, dot(probs, back, TN))


def backward_body(
    len_ref, move_ref, qkv_ref, cot_ref, box_ref, prob_ref, box_prob_ref, weight_ref,
    home_ref, inbox_ref, held_ref, both_ref, sem,
):
    def weight_copy(head):
        return pltpu.make_async_copy(weight_ref.at[:, head], held_ref.at[head], sem.at[head])

    for head in range(HEADS):
        weight_copy(head).start()
    rank = lax.axis_index("dp")
    begin, count = moved_clip(len_ref, move_ref, rank)
    place = lax.broadcasted_iota(jnp.int32, (TOK, TILE), 0)
    home = Tiles(home_ref, (place < begin) | (place >= begin + count))
    inbox = Tiles(inbox_ref, None)
    both_ref[:TOK] = cot_ref[...]
    both_ref[TOK:] = box_ref[3]
    for head in range(HEADS):
        start, stop = window(head)
        weight_copy(head).wait()
        weights = held_ref[head].reshape(TILE, FEAT)
        packed = dot(both_ref[...], weights, NT).astype(jnp.bfloat16)
        pick = as_bf16(gathered_lanes(stop - start) == HSIZE * head - start)
        back = dot(packed, pick, NN).astype(jnp.bfloat16)
        add_gradient(home, head, qkv_ref, prob_ref[head], back[:TOK])
        add_gradient(inbox, head, box_ref, box_prob_ref[head], back[TOK:])


def plane_body(got_ref, out_ref, turned_ref):
    total = jnp.sum(got_ref[...].astype(jnp.float32), axis=0)
    total = jnp.concatenate([total, jnp.zeros((TILE - COLS, TILE), jnp.float32)], axis=0)
    turned_ref[...] = jnp.transpose(total)
    out_ref[...] = jnp.zeros(out_ref.shape, jnp.float32)
    for x in range(NX):
        for b in range(2):
            rows = turned_ref[pl.ds(ROWS * x + b, ROWS // 2, stride=2), :]
            out_ref[x, :ROWS // 2, b * COLS:(b + 1) * COLS] = rows[:, :COLS]


def row_body(got_ref, out_ref):
    total = jnp.sum(got_ref[...], axis=0)
    for b in range(2):
        out_ref[pl.ds(b, ROWS // 2, stride=2), :] = total[:ROWS // 2, b * COLS:(b + 1) * COLS]


def in_vmem():
    return pl.BlockSpec(memory_space=pltpu.VMEM)


def in_smem():
    return pl.BlockSpec(memory_space=pltpu.SMEM)


def shape_of(shape, dtype):
    return jax.ShapeDtypeStruct(shape, dtype)


def forward(counts, qkv, cot):
    return pl.pallas_call(
        forward_body,
        out_shape=(
            shape_of((NZ * NY, COLS, TILE), jnp.bfloat16),
            shape_of((NZ * NY, COLS, TILE), jnp.bfloat16),
            shape_of((HEADS, TOK, TOK), jnp.bfloat16),
        ),
        in_specs=[in_smem()] + [in_vmem()] * 2,
        out_specs=(in_vmem(),) * 3,
        scratch_shapes=[
            pltpu.VMEM((TOK, HEADS * TILE), jnp.bfloat16),
            pltpu.VMEM((FEAT, HEADS * TILE), jnp.float32),
        ],
        compiler_params=pltpu.CompilerParams(vmem_limit_bytes=VMEM_BYTES),
        cost_estimate=pl.CostEstimate(flops=2_000_000_000, bytes_accessed=8_000_000, transcendentals=300_000),
        name="forward",
    )(counts, qkv, cot)


def pack(counts, moving, qkv, cot):
    return pl.pallas_call(
        pack_body,
        out_shape=shape_of((4, CLIP_MAX, FEAT), jnp.bfloat16),
        in_specs=[in_smem()] * 2 + [in_vmem()] * 2,
        out_specs=in_vmem(),
        compiler_params=pltpu.CompilerParams(vmem_limit_bytes=VMEM_BYTES),
        cost_estimate=pl.CostEstimate(flops=500_000_000, bytes_accessed=2_000_000, transcendentals=0),
        name="pack",
    )(counts, moving, qkv, cot)


def box_forward(counts, moving, box):
    return pl.pallas_call(
        box_body,
        out_shape=shape_of((HEADS, CLIP_MAX, CLIP_MAX), jnp.bfloat16),
        in_specs=[in_smem()] * 2 + [in_vmem()],
        out_specs=in_vmem(),
        compiler_params=pltpu.CompilerParams(vmem_limit_bytes=VMEM_BYTES),
        cost_estimate=pl.CostEstimate(flops=1_000_000_000, bytes_accessed=2_000_000, transcendentals=100_000),
        name="box_forward",
    )(counts, moving, box)


def backward(counts, moving, qkv, cot, box, probs, box_probs, weights):
    return pl.pallas_call(
        backward_body,
        out_shape=(
            shape_of((3, TOK, FEAT), jnp.bfloat16),
            shape_of((3, CLIP_MAX, FEAT), jnp.bfloat16),
        ),
        in_specs=[in_smem()] * 2 + [in_vmem()] * 5 + [pl.BlockSpec(memory_space=pl.ANY)],
        out_specs=(in_vmem(),) * 2,
        scratch_shapes=[
            pltpu.VMEM((HEADS, NX, 16, FEAT), jnp.bfloat16),
            pltpu.VMEM((TOK + CLIP_MAX, FEAT), jnp.bfloat16),
            pltpu.SemaphoreType.DMA((HEADS,)),
        ],
        compiler_params=pltpu.CompilerParams(vmem_limit_bytes=VMEM_BYTES),
        cost_estimate=pl.CostEstimate(flops=8_000_000_000, bytes_accessed=8_000_000, transcendentals=0),
        name="backward",
    )(counts, moving, qkv, cot, box, probs, box_probs, weights)


def plane_sum(got):
    return pl.pallas_call(
        plane_body,
        out_shape=shape_of((NX, 8, TILE), jnp.float32),
        in_specs=[in_vmem()],
        out_specs=in_vmem(),
        scratch_shapes=[pltpu.VMEM((TILE, TILE), jnp.float32)],
        compiler_params=pltpu.CompilerParams(vmem_limit_bytes=VMEM_BYTES),
        name="plane_sum",
    )(got)


def row_sum(got):
    return pl.pallas_call(
        row_body,
        out_shape=shape_of((ROWS, COLS), jnp.float32),
        in_specs=[in_vmem()],
        out_specs=in_vmem(),
        compiler_params=pltpu.CompilerParams(vmem_limit_bytes=VMEM_BYTES),
        name="row_sum",
    )(got)


def local(qkv, grad_out, lengths, moves, out_weight):
    rows = jnp.transpose(qkv[0, 0], (1, 0, 2))
    cot = grad_out[0, 0]
    counts = jnp.transpose(lengths, (2, 1, 0))
    moving = moves[0]
    ranks = NZ * NCORE

    with jax.named_scope("weights_y"):
        copies = jnp.pad(
            jnp.broadcast_to(out_weight[None], (NY,) + out_weight.shape),
            ((0, 0), (0, 16 - ROWS), (0, 0)),
        )
        column = lax.all_to_all(copies, "fsdp", 0, 0, tiled=True, axis_index_groups=Y_GROUPS)

    send = pack(counts, moving, rows, cot)
    send, later = lax.optimization_barrier((send, counts))
    box = lax.ppermute(send, "dp", [(i, (i + 1) % ranks) for i in range(ranks)])
    own, other, probs = forward(later, rows, cot)
    column, other = lax.optimization_barrier((column, other))
    with jax.named_scope("weights_x"):
        weights = lax.all_gather(
            column.reshape(NY * 16, FEAT), "fsdp", axis=0, tiled=True, axis_index_groups=X_GROUPS
        )
    swapped = lax.ppermute(other, "dp", [(i, i + 1 - 2 * (i % NCORE)) for i in range(ranks)])
    pair = (own.astype(jnp.float32) + swapped.astype(jnp.float32)).astype(jnp.bfloat16)
    with jax.named_scope("reduce_zy"):
        got = lax.all_to_all(
            pair, ("dp", "fsdp"), 0, 0, tiled=True, axis_index_groups=PLANE_GROUPS
        )
    box_probs = box_forward(counts, moving, box)
    plane = plane_sum(got)
    weights, _ = lax.optimization_barrier((weights, plane))
    with jax.named_scope("reduce_x"):
        parts = lax.all_to_all(plane, "fsdp", 0, 0, tiled=True, axis_index_groups=X_GROUPS)
    home, inbox = backward(
        counts, moving, rows, cot, box, probs, box_probs, weights.reshape(NX, NY, 16, FEAT)
    )
    return (
        jnp.transpose(home, (1, 0, 2))[None, None],
        jnp.transpose(inbox, (1, 0, 2))[None, None],
        row_sum(parts),
    )


def solution(mesh):
    placed = (
        P("dp", "fsdp", None, None, None),
        P("dp", "fsdp", None, None),
        P(None, "fsdp", None),
        P("fsdp", None, None),
        P("fsdp", None),
    )
    return jax.shard_map(
        local,
        mesh=mesh,
        in_specs=placed,
        out_specs=(
            P("dp", "fsdp", None, None, None),
            P("dp", "fsdp", None, None, None),
            P("fsdp", "dp"),
        ),
        check_vma=False,
    )
```

time: 120 us -> 121 us (level)
  the two profiles are of different devices: /device:TPU:1 before, /device:TPU:16 now
where the time goes in v3:
time: 121 us; the launch traced here: 120 us
  starting transfers between devices  39.4 us (33%)
  waiting for transfers between devices  35.7 us (30%)
  Pallas kernels  20.3 us (17%)
  between operations  14.2 us (12%)
  local copies, waits for them, and re-layouts  9.11 us (8%)
    all_to_all x1, waiting for transfers between devices, local(): lax.all_to_all(pair, ('dp', 'fsdp'), 0, 0, tiled=True, axis_index_groups=...  26.9 us
    all_to_all x1, starting transfers between devices, local(): lax.all_to_all(copies, 'fsdp', 0, 0, tiled=True, axis_index_groups=Y_GROUPS)  16.3 us
    all_to_all x1, starting transfers between devices, local(): lax.all_to_all(pair, ('dp', 'fsdp'), 0, 0, tiled=True, axis_index_groups=...  14.3 us
    pallas_call x1, Pallas kernels, backward(): pl.pallas_call(backward_body, out_shape=(shape_of((3, TOK, FEAT), jnp.bfl...  12 us
    unnamed x26, local copies, waits for them, and re-layouts  7.55 us
    all_to_all x1, starting transfers between devices, local(): lax.all_to_all(plane, 'fsdp', 0, 0, tiled=True, axis_index_groups=X_GROUPS)  6.78 us
    all_to_all x1, waiting for transfers between devices, local(): lax.all_to_all(plane, 'fsdp', 0, 0, tiled=True, axis_index_groups=X_GROUPS)  6.19 us
    pallas_call x1, Pallas kernels, forward(): pl.pallas_call(forward_body, out_shape=(shape_of((NZ * NY, COLS, TILE), j...  3.92 us
  transfers between devices with their start and end apart: 6, of which 3 were waited for; matrix products, arithmetic and copies ran while one was open for 1% of the time, Pallas kernels for 7%

profile of v3, /device:TPU:16, one launch (start us, length us, event | category | flops | bytes accessed | tf_op | source)
XLA Modules:
  0.0 119.9 jit_solution(14835716562571520865)
XLA Ops:
  7.2 0.0 copy-start.1
  7.2 0.9 broadcast_in_dim.12
  8.0 0.7 pad.4
  8.7 16.3 %all-to-all-start = ((bf16[8,16,896]{2,1,0:T(8,128)(2,1)}), bf16[8,16,896]{2,1,0:T(8,128)(2,1)S(1)}, u32[]{:S(2)}, u32[]{:S(2)}) async-start(bf16[8,16,896]{2,1,0:T(8,128)(2,1)} %pad.4), calls=%async_computation | async-start | bytes 458752 | tf_op jit(solution)/shard_map/weights_y/all_to_all | solution.py:335
  25.0 0.0 all-gather.2.cloned.1.call-start
  25.0 0.0 copy-start
  25.0 1.2 %copy-done = bf16[1,1,192,3,896]{4,2,3,1,0:T(8,128)(2,1)S(1)} copy-done((bf16[1,1,192,3,896]{4,2,3,1,0:T(8,128)(2,1)S(1)}, bf16[1,1,192,3,896]{4,2,3,1,0:T(8,128)(2,1)}, u32[]{:S(2)}) %copy-start) | copy-done | bytes 1032216
  26.3 0.0 copy-start.2
  26.3 1.0 copy-done.2
  27.2 0.0 copy-start.4
  27.2 0.7 copy-done.4
  27.9 0.0 copy-start.6
  27.9 0.7 copy-done.6
  28.6 1.0 pack.1
  29.6 0.0 copy-done.1
  29.6 3.9 %forward.1 = (bf16[64,56,128]{2,1,0:T(8,128)(2,1)S(1)}, bf16[64,56,128]{2,1,0:T(8,128)(2,1)S(1)}, bf16[8,192,192]{2,1,0:T(8,128)(2,1)S(1)}) custom-call(s32[3,1,16]{2,1,0:T(1,128)S(1)} %bitcast.21, bf16[3,192,896]{2,1,0:T(8,128)(2,1)S(1)} %bitcast.15, bf16[192,896]{1,0:T(8,128)(2,1)S(1)} %bitcast.18), custom_call_target="tpu_custom_call" | custom-call | flops 2000000000 | bytes 8000000 | tf_op jit(solution)/shard_map/forward/pallas_call | solution.py:237
  33.5 0.0 copy-start.9
  33.5 0.9 copy-done.9
  34.5 0.0 copy-start.10
  34.5 0.9 copy-done.10
  35.3 0.0 all-to-all-done
  35.3 0.0 copy-start.12
  35.3 0.7 copy-done.12
  36.0 0.0 all-gather.2.cloned.1.call-update
  36.0 1.9 %collective-permute-start.1 = (bf16[64,56,128]{2,1,0:T(8,128)(2,1)}, bf16[64,56,128]{2,1,0:T(8,128)(2,1)S(1)}, u32[]{:S(2)}, u32[]{:S(2)}) collective-permute-start(bf16[64,56,128]{2,1,0:T(8,128)(2,1)} %copy-done.9), channel_id=1, source_target_pairs={{0,64},{64,0},{128,192},{192,128},{256,320},{320,256},{384,448},{4... | collective-permute-start | bytes 2752520 | tf_op jit(solution)/shard_map/ppermute | solution.py:346
  38.0 2.6 %collective-permute-done.1 = bf16[64,56,128]{2,1,0:T(8,128)(2,1)S(1)} collective-permute-done((bf16[64,56,128]{2,1,0:T(8,128)(2,1)}, bf16[64,56,128]{2,1,0:T(8,128)(2,1)S(1)}, u32[]{:S(2)}, u32[]{:S(2)}) %collective-permute-start.1) | collective-permute-done | bytes 917536 | tf_op jit(solution)/shard_map/ppermute | solution.py:346
  40.6 1.2 add_convert_fusion
  41.8 0.0 copy-start.5
  41.8 0.0 copy-start.7
  41.8 14.3 %all-to-all-start.1 = ((bf16[64,56,128]{2,1,0:T(8,128)(2,1)}), bf16[64,56,128]{2,1,0:T(8,128)(2,1)S(1)}, u32[]{:S(2)}, u32[]{:S(2)}) async-start(bf16[64,56,128]{2,1,0:T(8,128)(2,1)} %add_convert_fusion), calls=%async_computation.1 | async-start | bytes 1835008 | tf_op jit(solution)/shard_map/reduce_zy/all_to_all | solution.py:349
  56.2 0.0 collective-permute-start
  56.2 26.9 %all-to-all-done.1.got_ref = bf16[64,56,128]{2,1,0:T(8,128)(2,1)S(1)} async-done(((bf16[64,56,128]{2,1,0:T(8,128)(2,1)}), bf16[64,56,128]{2,1,0:T(8,128)(2,1)S(1)}, u32[]{:S(2)}, u32[]{:S(2)}) %all-to-all-start.1) | async-done | bytes 917536 | tf_op jit(solution)/shard_map/reduce_zy/all_to_all | solution.py:349
  83.1 0.9 plane_sum.1
  84.0 6.8 %all-to-all-start.2 = ((f32[8,8,128]{2,1,0:T(8,128)}), f32[8,8,128]{2,1,0:T(8,128)S(1)}, u32[]{:S(2)}, u32[]{:S(2)}) async-start(f32[8,8,128]{2,1,0:T(8,128)} %plane_sum.1), calls=%async_computation.2 | async-start | bytes 65536 | tf_op jit(solution)/shard_map/reduce_x/all_to_all | solution.py:356
  90.8 0.0 copy-start.3
  90.8 0.0 copy-start.11
  90.8 0.0 collective-permute-done.box_ref
  90.8 0.0 copy-done.5
  90.8 0.0 copy-done.7
  90.8 1.8 %box_forward.1.box_prob_ref = bf16[8,128,128]{2,1,0:T(8,128)(2,1)S(1)} custom-call(s32[3,1,16]{2,1,0:T(1,128)S(1)} %bitcast.22, s32[2,3]{1,0:T(2,128)S(1)} %bitcast.25, bf16[4,128,896]{2,1,0:T(8,128)(2,1)} %collective-permute-done.box_ref), custom_call_target="tpu_custom_call" | custom-call | flops 1000000000 | bytes 2000000 | tf_op jit(solution)/shard_map/box_forward/pallas_call | solution.py:269
  92.6 6.2 %all-to-all-done.2.got_ref = f32[8,8,128]{2,1,0:T(8,128)S(1)} async-done(((f32[8,8,128]{2,1,0:T(8,128)}), f32[8,8,128]{2,1,0:T(8,128)S(1)}, u32[]{:S(2)}, u32[]{:S(2)}) %all-to-all-start.2) | async-done | bytes 32800 | tf_op jit(solution)/shard_map/reduce_x/all_to_all | solution.py:356
  98.8 0.7 row_sum.1
  99.5 0.0 all-gather.2.cloned.1.call-done
  99.5 0.0 copy-done.3
  99.5 0.0 copy-done.11
  99.5 0.0 copy-start.8
  99.5 1.5 %copy-done.8 = bf16[1024,896]{1,0:T(8,128)(2,1)S(1)} copy-done((bf16[1024,896]{1,0:T(8,128)(2,1)S(1)}, bf16[1024,896]{1,0:T(8,128)(2,1)}, u32[]{:S(2)}) %copy-start.8) | copy-done | bytes 1835032
  101.0 12.0 %backward.1 = (bf16[3,192,896]{2,1,0:T(8,128)(2,1)}, bf16[3,128,896]{2,1,0:T(8,128)(2,1)}) custom-call(s32[3,1,16]{2,1,0:T(1,128)S(1)} %bitcast.23, s32[2,3]{1,0:T(2,128)S(1)} %bitcast.26, bf16[3,192,896]{2,1,0:T(8,128)(2,1)S(1)} %bitcast.16, bf16[192,896]{1,0:T(8,128)(2,1)S(1)} %bitcast.19, bf16[4,128,896]{2,1,0:T(8,128)(2,1)} %collective-permute-done.box_ref, ...), custom_call_target="tpu_custom_call" | custom-call | flops 8000000000 | bytes 8000000 | tf_op jit(solution)/shard_map/backward/pallas_call | solution.py:281
Async XLA Ops:
  7.2 22.4 %copy-start.1 = (bf16[1,1,192,3,896]{4,2,3,1,0:T(8,128)(2,1)S(1)}, bf16[1,1,192,3,896]{4,2,3,1,0:T(8,128)(2,1)}, u32[]{:S(2)}) copy-start(bf16[1,1,192,3,896]{4,2,3,1,0:T(8,128)(2,1)} %param.5) | copy-start | bytes 3096580
  8.7 26.6 %all-to-all-start = ((bf16[8,16,896]{2,1,0:T(8,128)(2,1)}), bf16[8,16,896]{2,1,0:T(8,128)(2,1)S(1)}, u32[]{:S(2)}, u32[]{:S(2)}) async-start(bf16[8,16,896]{2,1,0:T(8,128)(2,1)} %pad.4), calls=%async_computation | async-start | bytes 458752 | tf_op jit(solution)/shard_map/weights_y/all_to_all | solution.py:335
  25.0 74.4 %all-gather.2.cloned.1.call-start = ((), (), s32[]{:S(2)}) async-start(), calls=%async_computation.3 | async-start | bytes 2064384 | tf_op jit(solution)/shard_map/weights_x/all_gather | solution.py:343
  25.0 1.2 %copy-start = (bf16[1,1,192,3,896]{4,2,3,1,0:T(8,128)(2,1)S(1)}, bf16[1,1,192,3,896]{4,2,3,1,0:T(8,128)(2,1)}, u32[]{:S(2)}) copy-start(bf16[1,1,192,3,896]{4,2,3,1,0:T(8,128)(2,1)} %param.5) | copy-start | bytes 3096580
  26.3 1.0 copy-start.2
  27.2 0.7 copy-start.4
  27.9 0.7 copy-start.6
  33.5 0.9 copy-start.9
  34.5 0.9 copy-start.10
  35.3 0.7 copy-start.12
  36.0 4.6 %collective-permute-start.1 = (bf16[64,56,128]{2,1,0:T(8,128)(2,1)}, bf16[64,56,128]{2,1,0:T(8,128)(2,1)S(1)}, u32[]{:S(2)}, u32[]{:S(2)}) collective-permute-start(bf16[64,56,128]{2,1,0:T(8,128)(2,1)} %copy-done.9), channel_id=1, source_target_pairs={{0,64},{64,0},{128,192},{192,128},{256,320},{320,256},{384,448},{4... | collective-permute-start | bytes 2752520 | tf_op jit(solution)/shard_map/ppermute | solution.py:346
  41.8 49.0 %copy-start.5 = (s32[16,1,3]{0,1,2:T(1,128)S(1)}, s32[16,1,3]{0,1,2:T(1,128)}, u32[]{:S(2)}) copy-start(s32[16,1,3]{0,1,2:T(1,128)} %param.7) | copy-start | bytes 580
  41.8 49.0 %copy-start.7 = (s32[1,2,3]{2,1,0:T(2,128)S(1)}, s32[1,2,3]{2,1,0:T(2,128)}, u32[]{:S(2)}) copy-start(s32[1,2,3]{2,1,0:T(2,128)} %param.8) | copy-start | bytes 76
  41.8 41.2 %all-to-all-start.1 = ((bf16[64,56,128]{2,1,0:T(8,128)(2,1)}), bf16[64,56,128]{2,1,0:T(8,128)(2,1)S(1)}, u32[]{:S(2)}, u32[]{:S(2)}) async-start(bf16[64,56,128]{2,1,0:T(8,128)(2,1)} %add_convert_fusion), calls=%async_computation.1 | async-start | bytes 1835008 | tf_op jit(solution)/shard_map/reduce_zy/all_to_all | solution.py:349
  56.2 34.6 %collective-permute-start = (bf16[4,128,896]{2,1,0:T(8,128)(2,1)S(1)}, bf16[4,128,896]{2,1,0:T(8,128)(2,1)}, u32[]{:S(2)}, u32[]{:S(2)}) collective-permute-start(bf16[4,128,896]{2,1,0:T(8,128)(2,1)S(1)} %pack.1), channel_id=1, source_target_pairs={{0,64},{64,128},{128,192},{192,256},{256,320},{320,384},{384,448},... | collective-permute-start | bytes 2752520 | tf_op jit(solution)/shard_map/ppermute | solution.py:339
  84.0 14.8 %all-to-all-start.2 = ((f32[8,8,128]{2,1,0:T(8,128)}), f32[8,8,128]{2,1,0:T(8,128)S(1)}, u32[]{:S(2)}, u32[]{:S(2)}) async-start(f32[8,8,128]{2,1,0:T(8,128)} %plane_sum.1), calls=%async_computation.2 | async-start | bytes 65536 | tf_op jit(solution)/shard_map/reduce_x/all_to_all | solution.py:356
  90.8 8.7 %copy-start.3 = (bf16[1,1,192,896]{3,2,1,0:T(8,128)(2,1)S(1)}, bf16[1,1,192,896]{3,2,1,0:T(8,128)(2,1)}, u32[]{:S(2)}) copy-start(bf16[1,1,192,896]{3,2,1,0:T(8,128)(2,1)} %param.6) | copy-start | bytes 1032196
  90.8 8.7 %copy-start.11 = (bf16[8,192,192]{2,1,0:T(8,128)(2,1)S(1)}, bf16[8,192,192]{2,1,0:T(8,128)(2,1)}, u32[]{:S(2)}) copy-start(bf16[8,192,192]{2,1,0:T(8,128)(2,1)} %copy-done.10) | copy-start | bytes 1769476
  99.5 1.5 %copy-start.8 = (bf16[1024,896]{1,0:T(8,128)(2,1)S(1)}, bf16[1024,896]{1,0:T(8,128)(2,1)}, u32[]{:S(2)}) copy-start(bf16[1024,896]{1,0:T(8,128)(2,1)} %all-gather.2.cloned.1.call-done) | copy-start | bytes 5505028
Sparse Core Ops, SparseCore 0:
  36.2 47.6 all-gather.1

commit v4 on v3

--- a/solution.py
+++ b/solution.py
@@ -102,7 +102,7 @@
 
 def box_body(len_ref, move_ref, box_ref, prob_ref):
     rank = lax.axis_index("dp")
-    _, count = moved_clip(len_ref, move_ref, lax.rem(rank + NZ * NCORE - 1, NZ * NCORE))
+    _, count = moved_clip(len_ref, move_ref, rank)
     row = lax.broadcasted_iota(jnp.int32, (CLIP_MAX, CLIP_MAX), 0)
     col = lax.broadcasted_iota(jnp.int32, (CLIP_MAX, CLIP_MAX), 1)
     for head in range(HEADS):
@@ -112,7 +112,9 @@
         prob_ref[head] = jnp.where(row < count, probs, 0.0).astype(jnp.bfloat16)
 
 
-def forward_body(len_ref, qkv_ref, cot_ref, own_ref, other_ref, prob_ref, mix_ref, term_ref):
+def forward_body(
+    len_ref, qkv_ref, cot_ref, own_ref, other_ref, prob_ref, token_ref, mix_ref, term_ref,
+):
     rank = lax.axis_index("dp")
     first, second = clip_ends(len_ref, rank)
 
@@ -141,6 +143,7 @@
             rows = pl.ds(pl.multiple_of(2 * COLS * z + COLS * part, 8), COLS)
             for y in range(NY):
                 ref[z * NY + y] = term_ref[rows, y * TILE:(y + 1) * TILE].astype(jnp.bfloat16)
+    token_ref[...] = jnp.zeros(token_ref.shape, jnp.float32)
 
 
 class Tiles:
@@ -177,31 +180,40 @@
     tiles.add(2, head, dot(probs, back, TN))
 
 
-def backward_body(
-    len_ref, move_ref, qkv_ref, cot_ref, box_ref, prob_ref, box_prob_ref, weight_ref,
-    home_ref, inbox_ref, held_ref, both_ref, sem,
+def back_window(head, cot, weight_ref):
+    start, stop = window(head)
+    packed = dot(cot, weight_ref[:, head].reshape(TILE, FEAT), NT).astype(jnp.bfloat16)
+    pick = as_bf16(gathered_lanes(stop - start) == HSIZE * head - start)
+    return dot(packed, pick, NN).astype(jnp.bfloat16)
+
+
+def box_backward_body(box_ref, prob_ref, weight_ref, send_ref, token_ref):
+    tiles = Tiles(send_ref, None)
+    cot = box_ref[3]
+    for head in range(HEADS):
+        add_gradient(tiles, head, box_ref, prob_ref[head], back_window(head, cot, weight_ref))
+    token_ref[...] = jnp.zeros(token_ref.shape, jnp.float32)
+
+
+def home_backward_body(
+    len_ref, move_ref, qkv_ref, cot_ref, prob_ref, weight_ref, order_ref, home_ref, token_ref,
 ):
-    def weight_copy(head):
-        return pltpu.make_async_copy(weight_ref.at[:, head], held_ref.at[head], sem.at[head])
-
-    for head in range(HEADS):
-        weight_copy(head).start()
     rank = lax.axis_index("dp")
     begin, count = moved_clip(len_ref, move_ref, rank)
     place = lax.broadcasted_iota(jnp.int32, (TOK, TILE), 0)
-    home = Tiles(home_ref, (place < begin) | (place >= begin + count))
-    inbox = Tiles(inbox_ref, None)
-    both_ref[:TOK] = cot_ref[...]
-    both_ref[TOK:] = box_ref[3]
+    tiles = Tiles(home_ref, (place < begin) | (place >= begin + count))
+    cot = cot_ref[...]
     for head in range(HEADS):
-        start, stop = window(head)
-        weight_copy(head).wait()
-        weights = held_ref[head].reshape(TILE, FEAT)
-        packed = dot(both_ref[...], weights, NT).astype(jnp.bfloat16)
-        pick = as_bf16(gathered_lanes(stop - start) == HSIZE * head - start)
-        back = dot(packed, pick, NN).astype(jnp.bfloat16)
-        add_gradient(home, head, qkv_ref, prob_ref[head], back[:TOK])
-        add_gradient(inbox, head, box_ref, box_prob_ref[head], back[TOK:])
+        add_gradient(tiles, head, qkv_ref, prob_ref[head], back_window(head, cot, weight_ref))
+    token_ref[...] = order_ref[...]
+
+
+def copies_body(shard_ref, copies_ref):
+    shard = shard_ref[...].astype(jnp.float32)
+    shard = jnp.concatenate([shard, jnp.zeros((16 - ROWS, FEAT), jnp.float32)], axis=0)
+    shard = shard.astype(jnp.bfloat16)
+    for y in range(NY):
+        copies_ref[y] = shard
 
 
 def plane_body(got_ref, out_ref, turned_ref):
@@ -215,7 +227,7 @@
             out_ref[x, :ROWS // 2, b * COLS:(b + 1) * COLS] = rows[:, :COLS]
 
 
-def row_body(got_ref, out_ref):
+def row_body(got_ref, order_ref, out_ref):
     total = jnp.sum(got_ref[...], axis=0)
     for b in range(2):
         out_ref[pl.ds(b, ROWS // 2, stride=2), :] = total[:ROWS // 2, b * COLS:(b + 1) * COLS]
@@ -233,91 +245,24 @@
     return jax.ShapeDtypeStruct(shape, dtype)
 
 
-def forward(counts, qkv, cot):
+TOKEN = shape_of((8, TILE), jnp.float32)
+
+
+def kernel(body, name, outs, scalars, arrays, scratch=(), flops=100_000_000):
     return pl.pallas_call(
-        forward_body,
-        out_shape=(
-            shape_of((NZ * NY, COLS, TILE), jnp.bfloat16),
-            shape_of((NZ * NY, COLS, TILE), jnp.bfloat16),
-            shape_of((HEADS, TOK, TOK), jnp.bfloat16),
-        ),
-        in_specs=[in_smem()] + [in_vmem()] * 2,
-        out_specs=(in_vmem(),) * 3,
-        scratch_shapes=[
-            pltpu.VMEM((TOK, HEADS * TILE), jnp.bfloat16),
-            pltpu.VMEM((FEAT, HEADS * TILE), jnp.float32),
-        ],
+        body,
+        out_shape=outs,
+        in_specs=[in_smem()] * len(scalars) + [in_vmem()] * len(arrays),
+        out_specs=tuple(in_vmem() for _ in outs),
+        scratch_shapes=list(scratch),
         compiler_params=pltpu.CompilerParams(vmem_limit_bytes=VMEM_BYTES),
-        cost_estimate=pl.CostEstimate(flops=2_000_000_000, bytes_accessed=8_000_000, transcendentals=300_000),
-        name="forward",
-    )(counts, qkv, cot)
-
-
-def pack(counts, moving, qkv, cot):
-    return pl.pallas_call(
-        pack_body,
-        out_shape=shape_of((4, CLIP_MAX, FEAT), jnp.bfloat16),
-        in_specs=[in_smem()] * 2 + [in_vmem()] * 2,
-        out_specs=in_vmem(),
-        compiler_params=pltpu.CompilerParams(vmem_limit_bytes=VMEM_BYTES),
-        cost_estimate=pl.CostEstimate(flops=500_000_000, bytes_accessed=2_000_000, transcendentals=0),
-        name="pack",
-    )(counts, moving, qkv, cot)
-
-
-def box_forward(counts, moving, box):
-    return pl.pallas_call(
-        box_body,
-        out_shape=shape_of((HEADS, CLIP_MAX, CLIP_MAX), jnp.bfloat16),
-        in_specs=[in_smem()] * 2 + [in_vmem()],
-        out_specs=in_vmem(),
-        compiler_params=pltpu.CompilerParams(vmem_limit_bytes=VMEM_BYTES),
-        cost_estimate=pl.CostEstimate(flops=1_000_000_000, bytes_accessed=2_000_000, transcendentals=100_000),
-        name="box_forward",
-    )(counts, moving, box)
-
-
-def backward(counts, moving, qkv, cot, box, probs, box_probs, weights):
-    return pl.pallas_call(
-        backward_body,
-        out_shape=(
-            shape_of((3, TOK, FEAT), jnp.bfloat16),
-            shape_of((3, CLIP_MAX, FEAT), jnp.bfloat16),
-        ),
-        in_specs=[in_smem()] * 2 + [in_vmem()] * 5 + [pl.BlockSpec(memory_space=pl.ANY)],
-        out_specs=(in_vmem(),) * 2,
-        scratch_shapes=[
-            pltpu.VMEM((HEADS, NX, 16, FEAT), jnp.bfloat16),
-            pltpu.VMEM((TOK + CLIP_MAX, FEAT), jnp.bfloat16),
-            pltpu.SemaphoreType.DMA((HEADS,)),
-        ],
-        compiler_params=pltpu.CompilerParams(vmem_limit_bytes=VMEM_BYTES),
-        cost_estimate=pl.CostEstimate(flops=8_000_000_000, bytes_accessed=8_000_000, transcendentals=0),
-        name="backward",
-    )(counts, moving, qkv, cot, box, probs, box_probs, weights)
-
-
-def plane_sum(got):
-    return pl.pallas_call(
-        plane_body,
-        out_shape=shape_of((NX, 8, TILE), jnp.float32),
-        in_specs=[in_vmem()],
-        out_specs=in_vmem(),
-        scratch_shapes=[pltpu.VMEM((TILE, TILE), jnp.float32)],
-        compiler_params=pltpu.CompilerParams(vmem_limit_bytes=VMEM_BYTES),
-        name="plane_sum",
-    )(got)
-
-
-def row_sum(got):
-    return pl.pallas_call(
-        row_body,
-        out_shape=shape_of((ROWS, COLS), jnp.float32),
-        in_specs=[in_vmem()],
-        out_specs=in_vmem(),
-        compiler_params=pltpu.CompilerParams(vmem_limit_bytes=VMEM_BYTES),
-        name="row_sum",
-    )(got)
+        cost_estimate=pl.CostEstimate(flops=flops, bytes_accessed=4_000_000, transcendentals=0),
+        name=name,
+    )(*scalars, *arrays)
+
+
+def after(value, *others):
+    return lax.optimization_barrier((value,) + others)[0]
 
 
 def local(qkv, grad_out, lengths, moves, out_weight):
@@ -326,41 +271,75 @@
     counts = jnp.transpose(lengths, (2, 1, 0))
     moving = moves[0]
     ranks = NZ * NCORE
+    bf16 = jnp.bfloat16
 
     with jax.named_scope("weights_y"):
-        copies = jnp.pad(
-            jnp.broadcast_to(out_weight[None], (NY,) + out_weight.shape),
-            ((0, 0), (0, 16 - ROWS), (0, 0)),
+        (copies,) = kernel(
+            copies_body, "copies", (shape_of((NY, 16, FEAT), bf16),), (), (out_weight,)
         )
         column = lax.all_to_all(copies, "fsdp", 0, 0, tiled=True, axis_index_groups=Y_GROUPS)
 
-    send = pack(counts, moving, rows, cot)
-    send, later = lax.optimization_barrier((send, counts))
-    box = lax.ppermute(send, "dp", [(i, (i + 1) % ranks) for i in range(ranks)])
-    own, other, probs = forward(later, rows, cot)
-    column, other = lax.optimization_barrier((column, other))
+    own, other, probs, token = kernel(
+        forward_body,
+        "forward",
+        (
+            shape_of((NZ * NY, COLS, TILE), bf16),
+            shape_of((NZ * NY, COLS, TILE), bf16),
+            shape_of((HEADS, TOK, TOK), bf16),
+            TOKEN,
+        ),
+        (counts,),
+        (rows, cot),
+        scratch=(
+            pltpu.VMEM((TOK, HEADS * TILE), bf16),
+            pltpu.VMEM((FEAT, HEADS * TILE), jnp.float32),
+        ),
+        flops=3_000_000_000,
+    )
+    column = after(column, token)
     with jax.named_scope("weights_x"):
         weights = lax.all_gather(
             column.reshape(NY * 16, FEAT), "fsdp", axis=0, tiled=True, axis_index_groups=X_GROUPS
         )
     swapped = lax.ppermute(other, "dp", [(i, i + 1 - 2 * (i % NCORE)) for i in range(ranks)])
-    pair = (own.astype(jnp.float32) + swapped.astype(jnp.float32)).astype(jnp.bfloat16)
+    pair = (own.astype(jnp.float32) + swapped.astype(jnp.float32)).astype(bf16)
     with jax.named_scope("reduce_zy"):
         got = lax.all_to_all(
             pair, ("dp", "fsdp"), 0, 0, tiled=True, axis_index_groups=PLANE_GROUPS
         )
-    box_probs = box_forward(counts, moving, box)
-    plane = plane_sum(got)
-    weights, _ = lax.optimization_barrier((weights, plane))
+
+    later = after(counts, token)
+    (box,) = kernel(
+        pack_body, "pack", (shape_of((4, CLIP_MAX, FEAT), bf16),), (later, moving), (rows, cot)
+    )
+    (box_probs,) = kernel(
+        box_body, "box_forward", (shape_of((HEADS, CLIP_MAX, CLIP_MAX), bf16),),
+        (later, moving), (box,), flops=1_000_000_000,
+    )
+
+    (plane,) = kernel(
+        plane_body, "plane_sum", (shape_of((NX, 8, TILE), jnp.float32),), (), (got,),
+        scratch=(pltpu.VMEM((TILE, TILE), jnp.float32),),
+    )
     with jax.named_scope("reduce_x"):
         parts = lax.all_to_all(plane, "fsdp", 0, 0, tiled=True, axis_index_groups=X_GROUPS)
-    home, inbox = backward(
-        counts, moving, rows, cot, box, probs, box_probs, weights.reshape(NX, NY, 16, FEAT)
+    weights = after(weights, plane).reshape(NX, NY, 16, FEAT)
+    send, token = kernel(
+        box_backward_body, "box_backward", (shape_of((3, CLIP_MAX, FEAT), bf16), TOKEN), (),
+        (box, box_probs, weights), flops=3_000_000_000,
+    )
+    inbox = lax.ppermute(send, "dp", [(i, (i + 1) % ranks) for i in range(ranks)])
+    home, token = kernel(
+        home_backward_body, "home_backward", (shape_of((3, TOK, FEAT), bf16), TOKEN),
+        (counts, moving), (rows, cot, probs, weights, token), flops=6_000_000_000,
+    )
+    (weight_grad,) = kernel(
+        row_body, "row_sum", (shape_of((ROWS, COLS), jnp.float32),), (), (parts, token)
     )
     return (
         jnp.transpose(home, (1, 0, 2))[None, None],
         jnp.transpose(inbox, (1, 0, 2))[None, None],
-        row_sum(parts),
+        weight_grad,
     )
 
 

time: 121 us -> 116 us (0.959)
  the two profiles are of different devices: /device:TPU:16 before, /device:TPU:1 now
where the time goes in v4:
time: 116 us
  starting transfers between devices  42.7 us (37%)
  waiting for transfers between devices  25.8 us (22%)
  Pallas kernels  20.6 us (18%)
  between operations  14.1 us (12%)
  local copies, waits for them, and re-layouts  11.3 us (10%)
  other arithmetic  1.16 us (1%)
    all_to_all x1, waiting for transfers between devices, local(): lax.all_to_all(pair, ('dp', 'fsdp'), 0, 0, tiled=True, axis_index_groups=...  22.9 us
    pallas_call x8, Pallas kernels, kernel(): pl.pallas_call(body, out_shape=outs, in_specs=[in_smem()] * len(scalars)...  20.6 us
    ppermute x1, starting transfers between devices, local(): lax.ppermute(other, 'dp', [(i, i + 1 - 2 * (i % NCORE)) for i in range(ra...  12.4 us
    all_to_all x1, starting transfers between devices, local(): lax.all_to_all(pair, ('dp', 'fsdp'), 0, 0, tiled=True, axis_index_groups=...  12.4 us
    unnamed x27, local copies, waits for them, and re-layouts  11.3 us
    all_to_all x1, starting transfers between devices, local(): lax.all_to_all(copies, 'fsdp', 0, 0, tiled=True, axis_index_groups=Y_GROUPS)  8.11 us
    all_to_all x1, starting transfers between devices, local(): lax.all_to_all(plane, 'fsdp', 0, 0, tiled=True, axis_index_groups=X_GROUPS)  5.47 us
    ppermute x1, starting transfers between devices, local(): lax.ppermute(send, 'dp', [(i, (i + 1) % ranks) for i in range(ranks)])  4.26 us
  transfers between devices with their start and end apart: 6, of which 3 were waited for; matrix products, arithmetic and copies ran while one was open for 1% of the time, Pallas kernels for 13%

profile of v4, /device:TPU:1, one launch (start us, length us, event | category | flops | bytes accessed | tf_op | source)
XLA Modules:
  0.0 115.7 jit_solution(21365097328952395)
XLA Ops:
  7.2 0.0 copy-start.9
  7.2 0.7 copy-done.9
  7.9 0.7 copies.1
  8.6 8.1 %all-to-all-start = ((bf16[8,16,896]{2,1,0:T(8,128)(2,1)}), bf16[8,16,896]{2,1,0:T(8,128)(2,1)S(1)}, u32[]{:S(2)}, u32[]{:S(2)}) async-start(bf16[8,16,896]{2,1,0:T(8,128)(2,1)} %copies.1), calls=%async_computation | async-start | bytes 458752 | tf_op jit(solution)/shard_map/weights_y/all_to_all | solution.py:280
  16.7 0.0 all-gather.2.cloned.1.call-start
  16.8 0.0 copy-start
  16.8 1.2 %copy-done = bf16[1,1,192,3,896]{4,2,3,1,0:T(8,128)(2,1)S(1)} copy-done((bf16[1,1,192,3,896]{4,2,3,1,0:T(8,128)(2,1)S(1)}, bf16[1,1,192,3,896]{4,2,3,1,0:T(8,128)(2,1)}, u32[]{:S(2)}) %copy-start) | copy-done | bytes 1032216
  18.0 0.0 copy-start.2
  18.0 1.0 copy-done.2
  19.0 0.0 copy-start.4
  19.0 0.7 copy-done.4
  19.7 4.4 %forward.1 = (bf16[64,56,128]{2,1,0:T(8,128)(2,1)S(1)}, bf16[64,56,128]{2,1,0:T(8,128)(2,1)S(1)}, bf16[8,192,192]{2,1,0:T(8,128)(2,1)S(1)}, f32[8,128]{1,0:T(8,128)}) custom-call(s32[3,1,16]{2,1,0:T(1,128)S(1)} %bitcast.20, bf16[3,192,896]{2,1,0:T(8,128)(2,1)S(1)} %bitcast.14, bf16[192,896]{1,0:T(8,128)(2,1)S(1)} %bitcast.17), custom_call_target="tpu_custom_call" | custom-call | flops 3000000000 | bytes 4000000 | tf_op jit(solution)/shard_map/forward/pallas_call | solution.py:252
  24.0 0.0 copy-start.10
  24.0 0.9 copy-done.10
  24.9 0.8 all-to-all-done
  25.7 0.0 copy-start.12
  25.7 0.7 copy-done.12
  26.4 0.0 all-gather.2.cloned.1.call-update
  26.4 12.4 %collective-permute-start = (bf16[64,56,128]{2,1,0:T(8,128)(2,1)S(1)}, bf16[64,56,128]{2,1,0:T(8,128)(2,1)S(1)}, u32[]{:S(2)}, u32[]{:S(2)}) collective-permute-start(bf16[64,56,128]{2,1,0:T(8,128)(2,1)S(1)} %get-tuple-element.18), channel_id=1, source_target_pairs={{0,64},{64,0},{128,192},{192,128},{256,320},{320,256},{384,448},{4... | collective-permute-start | bytes 2752520 | tf_op jit(solution)/shard_map/ppermute | solution.py:304
  38.9 2.1 %collective-permute-done = bf16[64,56,128]{2,1,0:T(8,128)(2,1)S(1)} collective-permute-done((bf16[64,56,128]{2,1,0:T(8,128)(2,1)S(1)}, bf16[64,56,128]{2,1,0:T(8,128)(2,1)S(1)}, u32[]{:S(2)}, u32[]{:S(2)}) %collective-permute-start) | collective-permute-done | bytes 917536 | tf_op jit(solution)/shard_map/ppermute | solution.py:304
  40.9 0.0 copy-start.1
  40.9 0.0 copy-start.3
  40.9 0.0 copy-start.5
  40.9 1.2 %add_convert_fusion = bf16[64,56,128]{2,1,0:T(8,128)(2,1)} fusion(bf16[64,56,128]{2,1,0:T(8,128)(2,1)S(1)} %collective-permute-done, bf16[64,56,128]{2,1,0:T(8,128)(2,1)S(1)} %get-tuple-element.17), kind=kLoop, calls=%fused_computation | loop fusion | flops 1835008 | bytes 2752512 | tf_op jit(solution)/shard_map/convert_element_type | solution.py:305
  42.1 12.4 %all-to-all-start.1 = ((bf16[64,56,128]{2,1,0:T(8,128)(2,1)}), bf16[64,56,128]{2,1,0:T(8,128)(2,1)S(1)}, u32[]{:S(2)}, u32[]{:S(2)}) async-start(bf16[64,56,128]{2,1,0:T(8,128)(2,1)} %add_convert_fusion), calls=%async_computation.1 | async-start | bytes 1835008 | tf_op jit(solution)/shard_map/reduce_zy/all_to_all | solution.py:307
  54.5 0.0 copy-done.1
  54.5 0.0 copy-done.3
  54.5 0.0 copy-done.5
  54.5 0.0 copy-done.6
  54.5 1.0 pack.1.box_ref
  55.5 1.1 box_forward.1.prob_ref
  56.6 22.9 %all-to-all-done.1.got_ref = bf16[64,56,128]{2,1,0:T(8,128)(2,1)S(1)} async-done(((bf16[64,56,128]{2,1,0:T(8,128)(2,1)}), bf16[64,56,128]{2,1,0:T(8,128)(2,1)S(1)}, u32[]{:S(2)}, u32[]{:S(2)}) %all-to-all-start.1) | async-done | bytes 917536 | tf_op jit(solution)/shard_map/reduce_zy/all_to_all | solution.py:307
  79.5 0.9 plane_sum.1
  80.4 0.0 all-gather.2.cloned.1.call-done
  80.4 0.0 copy-start.7
  80.4 1.5 %copy-done.7 = bf16[1024,896]{1,0:T(8,128)(2,1)S(1)} copy-done((bf16[1024,896]{1,0:T(8,128)(2,1)S(1)}, bf16[1024,896]{1,0:T(8,128)(2,1)}, u32[]{:S(2)}) %copy-start.7) | copy-done | bytes 1835032
  81.9 4.7 %box_backward.1 = (bf16[3,128,896]{2,1,0:T(8,128)(2,1)S(1)}, f32[8,128]{1,0:T(8,128)S(1)}) custom-call(bf16[4,128,896]{2,1,0:T(8,128)(2,1)S(1)} %pack.1.box_ref, bf16[8,128,128]{2,1,0:T(8,128)(2,1)S(1)} %box_forward.1.prob_ref, bf16[8,8,16,896]{3,2,1,0:T(8,128)(2,1)S(1)} %bitcast.27), custom_call_target="tpu_custom_call" | custom-call | flops 3000000000 | bytes 4000000 | tf_op jit(solution)/shard_map/box_backward/pallas_call | solution.py:252
  86.7 4.3 %collective-permute-start.1 = (bf16[3,128,896]{2,1,0:T(8,128)(2,1)S(1)}, bf16[3,128,896]{2,1,0:T(8,128)(2,1)}, u32[]{:S(2)}, u32[]{:S(2)}) collective-permute-start(bf16[3,128,896]{2,1,0:T(8,128)(2,1)S(1)} %get-tuple-element.23), channel_id=1, source_target_pairs={{0,64},{64,128},{128,192},{192,256},{256,320},{320,384},{384,448},... | collective-permute-start | bytes 2064392 | tf_op jit(solution)/shard_map/ppermute | solution.py:331
  91.0 5.5 %all-to-all-start.2 = ((f32[8,8,128]{2,1,0:T(8,128)}), f32[8,8,128]{2,1,0:T(8,128)S(1)}, u32[]{:S(2)}, u32[]{:S(2)}) async-start(f32[8,8,128]{2,1,0:T(8,128)} %plane_sum.1), calls=%async_computation.2 | async-start | bytes 65536 | tf_op jit(solution)/shard_map/reduce_x/all_to_all | solution.py:325
  96.4 0.0 copy-start.8
  96.4 1.5 %copy-done.8 = bf16[1024,896]{1,0:T(8,128)(2,1)S(1)} copy-done((bf16[1024,896]{1,0:T(8,128)(2,1)S(1)}, bf16[1024,896]{1,0:T(8,128)(2,1)}, u32[]{:S(2)}) %copy-start.8) | copy-done | bytes 1835032
  97.9 0.0 copy-start.11
  97.9 1.1 copy-done.11
  99.1 7.1 %home_backward.1 = (bf16[3,192,896]{2,1,0:T(8,128)(2,1)}, f32[8,128]{1,0:T(8,128)S(1)}) custom-call(s32[3,1,16]{2,1,0:T(1,128)S(1)} %bitcast.23, s32[2,3]{1,0:T(2,128)S(1)} %bitcast.26, bf16[3,192,896]{2,1,0:T(8,128)(2,1)S(1)} %bitcast.16, bf16[192,896]{1,0:T(8,128)(2,1)S(1)} %bitcast.19, bf16[8,192,192]{2,1,0:T(8,128)(2,1)S(1)} %copy-done.11, ...), custom_call_target="tpu_custom_call" | custom-call | flops 6000000000 | bytes 4000000 | tf_op jit(solution)/shard_map/home_backward/pallas_call | solution.py:252
  106.2 0.0 all-to-all-done.2.got_ref
  106.2 0.7 row_sum.1
  106.9 0.0 collective-permute-done.1
  106.9 2.0 %copy.9 = bf16[1,1,128,3,896]{4,2,3,1,0:T(8,128)(2,1)} copy(bf16[1,1,128,3,896]{4,2,3,1,0:T(8,128)(2,1)} %bitcast.11) | data formatting | bytes 1376256
  (1 shorter events, 0.0 us)
Async XLA Ops:
  7.2 0.7 copy-start.9
  8.6 17.1 %all-to-all-start = ((bf16[8,16,896]{2,1,0:T(8,128)(2,1)}), bf16[8,16,896]{2,1,0:T(8,128)(2,1)S(1)}, u32[]{:S(2)}, u32[]{:S(2)}) async-start(bf16[8,16,896]{2,1,0:T(8,128)(2,1)} %copies.1), calls=%async_computation | async-start | bytes 458752 | tf_op jit(solution)/shard_map/weights_y/all_to_all | solution.py:280
  16.7 63.7 %all-gather.2.cloned.1.call-start = ((), (), s32[]{:S(2)}) async-start(), calls=%async_computation.3 | async-start | bytes 2064384 | tf_op jit(solution)/shard_map/weights_x/all_gather | solution.py:301
  16.8 1.2 %copy-start = (bf16[1,1,192,3,896]{4,2,3,1,0:T(8,128)(2,1)S(1)}, bf16[1,1,192,3,896]{4,2,3,1,0:T(8,128)(2,1)}, u32[]{:S(2)}) copy-start(bf16[1,1,192,3,896]{4,2,3,1,0:T(8,128)(2,1)} %param.5) | copy-start | bytes 3096580
  18.0 1.0 copy-start.2
  19.0 0.7 copy-start.4
  24.0 0.9 copy-start.10
  25.7 0.7 copy-start.12
  26.4 14.5 %collective-permute-start = (bf16[64,56,128]{2,1,0:T(8,128)(2,1)S(1)}, bf16[64,56,128]{2,1,0:T(8,128)(2,1)S(1)}, u32[]{:S(2)}, u32[]{:S(2)}) collective-permute-start(bf16[64,56,128]{2,1,0:T(8,128)(2,1)S(1)} %get-tuple-element.18), channel_id=1, source_target_pairs={{0,64},{64,0},{128,192},{192,128},{256,320},{320,256},{384,448},{4... | collective-permute-start | bytes 2752520 | tf_op jit(solution)/shard_map/ppermute | solution.py:304
  40.9 13.6 %copy-start.1 = (bf16[1,1,192,3,896]{4,2,3,1,0:T(8,128)(2,1)S(1)}, bf16[1,1,192,3,896]{4,2,3,1,0:T(8,128)(2,1)}, u32[]{:S(2)}) copy-start(bf16[1,1,192,3,896]{4,2,3,1,0:T(8,128)(2,1)} %param.5) | copy-start | bytes 3096580
  40.9 13.6 %copy-start.3 = (bf16[1,1,192,896]{3,2,1,0:T(8,128)(2,1)S(1)}, bf16[1,1,192,896]{3,2,1,0:T(8,128)(2,1)}, u32[]{:S(2)}) copy-start(bf16[1,1,192,896]{3,2,1,0:T(8,128)(2,1)} %param.6) | copy-start | bytes 1032196
  40.9 13.6 %copy-start.5 = (s32[16,1,3]{0,1,2:T(1,128)S(1)}, s32[16,1,3]{0,1,2:T(1,128)}, u32[]{:S(2)}) copy-start(s32[16,1,3]{0,1,2:T(1,128)} %param.7) | copy-start | bytes 580
  40.9 13.6 %copy-start.6 = (s32[1,2,3]{2,1,0:T(2,128)S(1)}, s32[1,2,3]{2,1,0:T(2,128)}, u32[]{:S(2)}) copy-start(s32[1,2,3]{2,1,0:T(2,128)} %param.8) | copy-start | bytes 76
  42.1 37.4 %all-to-all-start.1 = ((bf16[64,56,128]{2,1,0:T(8,128)(2,1)}), bf16[64,56,128]{2,1,0:T(8,128)(2,1)S(1)}, u32[]{:S(2)}, u32[]{:S(2)}) async-start(bf16[64,56,128]{2,1,0:T(8,128)(2,1)} %add_convert_fusion), calls=%async_computation.1 | async-start | bytes 1835008 | tf_op jit(solution)/shard_map/reduce_zy/all_to_all | solution.py:307
  80.4 1.5 %copy-start.7 = (bf16[1024,896]{1,0:T(8,128)(2,1)S(1)}, bf16[1024,896]{1,0:T(8,128)(2,1)}, u32[]{:S(2)}) copy-start(bf16[1024,896]{1,0:T(8,128)(2,1)} %all-gather.2.cloned.1.call-done) | copy-start | bytes 5505028
  86.7 20.2 %collective-permute-start.1 = (bf16[3,128,896]{2,1,0:T(8,128)(2,1)S(1)}, bf16[3,128,896]{2,1,0:T(8,128)(2,1)}, u32[]{:S(2)}, u32[]{:S(2)}) collective-permute-start(bf16[3,128,896]{2,1,0:T(8,128)(2,1)S(1)} %get-tuple-element.23), channel_id=1, source_target_pairs={{0,64},{64,128},{128,192},{192,256},{256,320},{320,384},{384,448},... | collective-permute-start | bytes 2064392 | tf_op jit(solution)/shard_map/ppermute | solution.py:331
  91.0 15.2 %all-to-all-start.2 = ((f32[8,8,128]{2,1,0:T(8,128)}), f32[8,8,128]{2,1,0:T(8,128)S(1)}, u32[]{:S(2)}, u32[]{:S(2)}) async-start(f32[8,8,128]{2,1,0:T(8,128)} %plane_sum.1), calls=%async_computation.2 | async-start | bytes 65536 | tf_op jit(solution)/shard_map/reduce_x/all_to_all | solution.py:325
  96.4 1.5 %copy-start.8 = (bf16[1024,896]{1,0:T(8,128)(2,1)S(1)}, bf16[1024,896]{1,0:T(8,128)(2,1)}, u32[]{:S(2)}) copy-start(bf16[1024,896]{1,0:T(8,128)(2,1)} %all-gather.2.cloned.1.call-done) | copy-start | bytes 5505028
  97.9 1.1 copy-start.11
Sparse Core Ops, SparseCore 0:
  26.5 52.4 all-gather.1

commit v5 on v4

--- a/solution.py
+++ b/solution.py
@@ -16,7 +16,8 @@
 COLS = 56
 SCALE = HSIZE ** (-0.5)
 TILE = 128
-VMEM_BYTES = 14 * 1024 * 1024
+SMALL_GRANT = 14 * 1024 * 1024
+LARGE_GRANT = 60 * 1024 * 1024
 
 Y_GROUPS = [[y * NX + x for y in range(NY)] for x in range(NX)]
 X_GROUPS = [[y * NX + x for x in range(NX)] for y in range(NY)]
@@ -180,31 +181,41 @@
     tiles.add(2, head, dot(probs, back, TN))
 
 
-def back_window(head, cot, weight_ref):
+def weight_copy(head, weight_ref, held_ref, sem):
+    return pltpu.make_async_copy(weight_ref.at[:, head], held_ref.at[head], sem.at[head])
+
+
+def back_window(head, cot, weights):
     start, stop = window(head)
-    packed = dot(cot, weight_ref[:, head].reshape(TILE, FEAT), NT).astype(jnp.bfloat16)
+    packed = dot(cot, weights.reshape(TILE, FEAT), NT).astype(jnp.bfloat16)
     pick = as_bf16(gathered_lanes(stop - start) == HSIZE * head - start)
     return dot(packed, pick, NN).astype(jnp.bfloat16)
 
 
-def box_backward_body(box_ref, prob_ref, weight_ref, send_ref, token_ref):
+def all_gradients(tiles, rows_ref, cot, prob_ref, weight_ref, held_ref, sem):
+    for head in range(HEADS):
+        weight_copy(head, weight_ref, held_ref, sem).start()
+    for head in range(HEADS):
+        weight_copy(head, weight_ref, held_ref, sem).wait()
+        back = back_window(head, cot, held_ref[head])
+        add_gradient(tiles, head, rows_ref, prob_ref[head], back)
+
+
+def box_backward_body(box_ref, prob_ref, weight_ref, send_ref, token_ref, held_ref, sem):
     tiles = Tiles(send_ref, None)
-    cot = box_ref[3]
-    for head in range(HEADS):
-        add_gradient(tiles, head, box_ref, prob_ref[head], back_window(head, cot, weight_ref))
+    all_gradients(tiles, box_ref, box_ref[3], prob_ref, weight_ref, held_ref, sem)
     token_ref[...] = jnp.zeros(token_ref.shape, jnp.float32)
 
 
 def home_backward_body(
-    len_ref, move_ref, qkv_ref, cot_ref, prob_ref, weight_ref, order_ref, home_ref, token_ref,
+    len_ref, move_ref, qkv_ref, cot_ref, prob_ref, order_ref, weight_ref,
+    home_ref, token_ref, held_ref, sem,
 ):
     rank = lax.axis_index("dp")
     begin, count = moved_clip(len_ref, move_ref, rank)
     place = lax.broadcasted_iota(jnp.int32, (TOK, TILE), 0)
     tiles = Tiles(home_ref, (place < begin) | (place >= begin + count))
-    cot = cot_ref[...]
-    for head in range(HEADS):
-        add_gradient(tiles, head, qkv_ref, prob_ref[head], back_window(head, cot, weight_ref))
+    all_gradients(tiles, qkv_ref, cot_ref[...], prob_ref, weight_ref, held_ref, sem)
     token_ref[...] = order_ref[...]
 
 
@@ -248,17 +259,21 @@
 TOKEN = shape_of((8, TILE), jnp.float32)
 
 
-def kernel(body, name, outs, scalars, arrays, scratch=(), flops=100_000_000):
+def kernel(
+    body, name, outs, scalars, arrays, far=(), scratch=(), flops=100_000_000, grant=LARGE_GRANT
+):
     return pl.pallas_call(
         body,
         out_shape=outs,
-        in_specs=[in_smem()] * len(scalars) + [in_vmem()] * len(arrays),
+        in_specs=[in_smem()] * len(scalars)
+        + [in_vmem()] * len(arrays)
+        + [pl.BlockSpec(memory_space=pltpu.HBM)] * len(far),
         out_specs=tuple(in_vmem() for _ in outs),
         scratch_shapes=list(scratch),
-        compiler_params=pltpu.CompilerParams(vmem_limit_bytes=VMEM_BYTES),
-        cost_estimate=pl.CostEstimate(flops=flops, bytes_accessed=4_000_000, transcendentals=0),
+        compiler_params=pltpu.CompilerParams(vmem_limit_bytes=grant),
+        cost_estimate=pl.CostEstimate(flops=flops, bytes_accessed=flops // 100, transcendentals=0),
         name=name,
-    )(*scalars, *arrays)
+    )(*scalars, *arrays, *far)
 
 
 def after(value, *others):
@@ -319,22 +334,27 @@
 
     (plane,) = kernel(
         plane_body, "plane_sum", (shape_of((NX, 8, TILE), jnp.float32),), (), (got,),
-        scratch=(pltpu.VMEM((TILE, TILE), jnp.float32),),
+        scratch=(pltpu.VMEM((TILE, TILE), jnp.float32),), grant=SMALL_GRANT,
     )
     with jax.named_scope("reduce_x"):
         parts = lax.all_to_all(plane, "fsdp", 0, 0, tiled=True, axis_index_groups=X_GROUPS)
     weights = after(weights, plane).reshape(NX, NY, 16, FEAT)
+    held = (
+        pltpu.VMEM((HEADS, NX, 16, FEAT), bf16),
+        pltpu.SemaphoreType.DMA((HEADS,)),
+    )
     send, token = kernel(
         box_backward_body, "box_backward", (shape_of((3, CLIP_MAX, FEAT), bf16), TOKEN), (),
-        (box, box_probs, weights), flops=3_000_000_000,
+        (box, box_probs), far=(weights,), scratch=held, flops=1000,
     )
     inbox = lax.ppermute(send, "dp", [(i, (i + 1) % ranks) for i in range(ranks)])
     home, token = kernel(
         home_backward_body, "home_backward", (shape_of((3, TOK, FEAT), bf16), TOKEN),
-        (counts, moving), (rows, cot, probs, weights, token), flops=6_000_000_000,
+        (counts, moving), (rows, cot, probs, token), far=(weights,), scratch=held, flops=1000,
     )
     (weight_grad,) = kernel(
-        row_body, "row_sum", (shape_of((ROWS, COLS), jnp.float32),), (), (parts, token)
+        row_body, "row_sum", (shape_of((ROWS, COLS), jnp.float32),), (), (parts, token),
+        grant=SMALL_GRANT,
     )
     return (
         jnp.transpose(home, (1, 0, 2))[None, None],

time: 116 us -> 119 us (1.026)
  Pallas kernels: 20.6 us -> 33.6 us
  local copies, waits for them, and re-layouts: 11.3 us -> 2.21 us
  starting transfers between devices: 42.7 us -> 40.7 us
  other arithmetic: 1.16 us -> 2.35 us
    pallas_call x8, Pallas kernels: 20.6 us -> 33.6 us  [kernel(): pl.pallas_call(body, out_shape=outs, in_specs=[in_smem()] * len(scalars)...]
    unnamed x27 -> x5, local copies, waits for them, and re-layouts: 11.3 us -> 2.21 us
    all_to_all x1, waiting for transfers between devices: 22.9 us -> 19.9 us  [local(): lax.all_to_all(pair, ('dp', 'fsdp'), 0, 0, tiled=True, axis_index_groups=...]
    all_to_all x1, waiting for transfers between devices: 0.8 us -> 2.78 us  [local(): lax.all_to_all(copies, 'fsdp', 0, 0, tiled=True, axis_index_groups=Y_GROUPS)]
    all_to_all x1, starting transfers between devices: 12.4 us -> 10.4 us  [local(): lax.all_to_all(pair, ('dp', 'fsdp'), 0, 0, tiled=True, axis_index_groups=...]
  transfers between devices with their start and end apart: 6 -> 6, of which waited for: 3 -> 3; matrix products, arithmetic and copies ran while one was open for 1% -> 2% of each run, Pallas kernels for 13% -> 20%
where the time goes in v5:
time: 119 us; the launch traced here: 118 us
  starting transfers between devices  40.7 us (34%)
  Pallas kernels  33.6 us (28%)
  waiting for transfers between devices  25 us (21%)
  between operations  14.1 us (12%)
  other arithmetic  2.35 us (2%)
  local copies, waits for them, and re-layouts  2.21 us (2%)
    pallas_call x8, Pallas kernels, kernel(): pl.pallas_call(body, out_shape=outs, in_specs=[in_smem()] * len(scalars)...  33.6 us
    all_to_all x1, waiting for transfers between devices, local(): lax.all_to_all(pair, ('dp', 'fsdp'), 0, 0, tiled=True, axis_index_groups=...  19.9 us
    ppermute x1, starting transfers between devices, local(): lax.ppermute(other, 'dp', [(i, i + 1 - 2 * (i % NCORE)) for i in range(ra...  12.4 us
    all_to_all x1, starting transfers between devices, local(): lax.all_to_all(pair, ('dp', 'fsdp'), 0, 0, tiled=True, axis_index_groups=...  10.4 us
    all_to_all x1, starting transfers between devices, local(): lax.all_to_all(copies, 'fsdp', 0, 0, tiled=True, axis_index_groups=Y_GROUPS)  8.11 us
    all_to_all x1, starting transfers between devices, local(): lax.all_to_all(plane, 'fsdp', 0, 0, tiled=True, axis_index_groups=X_GROUPS)  6.48 us
    ppermute x1, starting transfers between devices, local(): lax.ppermute(send, 'dp', [(i, (i + 1) % ranks) for i in range(ranks)])  3.3 us
    all_to_all x1, waiting for transfers between devices, local(): lax.all_to_all(copies, 'fsdp', 0, 0, tiled=True, axis_index_groups=Y_GROUPS)  2.78 us
  transfers between devices with their start and end apart: 6, of which 3 were waited for; matrix products, arithmetic and copies ran while one was open for 2% of the time, Pallas kernels for 20%

profile of v5, /device:TPU:1, one launch (start us, length us, event | category | flops | bytes accessed | tf_op | source)
XLA Modules:
  0.0 118.0 jit_solution(329921690550249971)
XLA Ops:
  7.2 1.5 %copies.1 = bf16[8,16,896]{2,1,0:T(8,128)(2,1)} custom-call(bf16[14,896]{1,0:T(8,128)(2,1)} %shard_ref.1), custom_call_target="tpu_custom_call" | custom-call | flops 100000000 | bytes 1000000 | tf_op jit(solution)/shard_map/weights_y/copies/pallas_call | solution.py:265
  8.6 8.1 %all-to-all-start = ((bf16[8,16,896]{2,1,0:T(8,128)(2,1)}), bf16[8,16,896]{2,1,0:T(8,128)(2,1)S(1)}, u32[]{:S(2)}, u32[]{:S(2)}) async-start(bf16[8,16,896]{2,1,0:T(8,128)(2,1)} %copies.1), calls=%async_computation | async-start | bytes 458752 | tf_op jit(solution)/shard_map/weights_y/all_to_all | solution.py:295
  16.7 0.0 all-gather.2.cloned.1.call-start
  16.8 6.2 %forward.1 = (bf16[64,56,128]{2,1,0:T(8,128)(2,1)}, bf16[64,56,128]{2,1,0:T(8,128)(2,1)}, bf16[8,192,192]{2,1,0:T(8,128)(2,1)}, f32[8,128]{1,0:T(8,128)}) custom-call(s32[3,1,16]{2,1,0:T(1,128)} %bitcast.24, bf16[3,192,896]{2,1,0:T(8,128)(2,1)} %bitcast.16, bf16[192,896]{1,0:T(8,128)(2,1)} %bitcast.19), custom_call_target="tpu_custom_call" | custom-call | flops 3000000000 | bytes 30000000 | tf_op jit(solution)/shard_map/forward/pallas_call | solution.py:265
  22.9 2.8 %all-to-all-done = bf16[8,16,896]{2,1,0:T(8,128)(2,1)S(1)} async-done(((bf16[8,16,896]{2,1,0:T(8,128)(2,1)}), bf16[8,16,896]{2,1,0:T(8,128)(2,1)S(1)}, u32[]{:S(2)}, u32[]{:S(2)}) %all-to-all-start) | async-done | bytes 229408 | tf_op jit(solution)/shard_map/weights_y/all_to_all | solution.py:295
  25.7 0.0 copy-start.1
  25.7 0.7 copy-done.1
  26.4 0.0 all-gather.2.cloned.1.call-update
  26.4 12.4 %collective-permute-start = (bf16[64,56,128]{2,1,0:T(8,128)(2,1)}, bf16[64,56,128]{2,1,0:T(8,128)(2,1)S(1)}, u32[]{:S(2)}, u32[]{:S(2)}) collective-permute-start(bf16[64,56,128]{2,1,0:T(8,128)(2,1)} %get-tuple-element.19), channel_id=1, source_target_pairs={{0,64},{64,0},{128,192},{192,128},{256,320},{320,256},{384,448},{4... | collective-permute-start | bytes 2752520 | tf_op jit(solution)/shard_map/ppermute | solution.py:319
  38.8 2.3 %collective-permute-done = bf16[64,56,128]{2,1,0:T(8,128)(2,1)S(1)} collective-permute-done((bf16[64,56,128]{2,1,0:T(8,128)(2,1)}, bf16[64,56,128]{2,1,0:T(8,128)(2,1)S(1)}, u32[]{:S(2)}, u32[]{:S(2)}) %collective-permute-start) | collective-permute-done | bytes 917536 | tf_op jit(solution)/shard_map/ppermute | solution.py:319
  41.1 2.3 %add_convert_fusion = bf16[64,56,128]{2,1,0:T(8,128)(2,1)} fusion(bf16[64,56,128]{2,1,0:T(8,128)(2,1)S(1)} %collective-permute-done, bf16[64,56,128]{2,1,0:T(8,128)(2,1)} %get-tuple-element.18), kind=kLoop, calls=%fused_computation | loop fusion | flops 1835008 | bytes 2752512 | tf_op jit(solution)/shard_map/convert_element_type | solution.py:320
  43.5 10.4 %all-to-all-start.1 = ((bf16[64,56,128]{2,1,0:T(8,128)(2,1)}), bf16[64,56,128]{2,1,0:T(8,128)(2,1)S(1)}, u32[]{:S(2)}, u32[]{:S(2)}) async-start(bf16[64,56,128]{2,1,0:T(8,128)(2,1)} %add_convert_fusion), calls=%async_computation.1 | async-start | bytes 1835008 | tf_op jit(solution)/shard_map/reduce_zy/all_to_all | solution.py:322
  53.9 2.7 %pack.1.box_ref = bf16[4,128,896]{2,1,0:T(8,128)(2,1)} custom-call(s32[3,1,16]{2,1,0:T(1,128)} %bitcast.25, s32[2,3]{1,0:T(2,128)} %bitcast.28, bf16[3,192,896]{2,1,0:T(8,128)(2,1)} %bitcast.17, bf16[192,896]{1,0:T(8,128)(2,1)} %bitcast.20), custom_call_target="tpu_custom_call" | custom-call | flops 100000000 | bytes 1000000 | tf_op jit(solution)/shard_map/pack/pallas_call | solution.py:265
  56.6 2.4 %box_forward.1.prob_ref = bf16[8,128,128]{2,1,0:T(8,128)(2,1)} custom-call(s32[3,1,16]{2,1,0:T(1,128)} %bitcast.26, s32[2,3]{1,0:T(2,128)} %bitcast.29, bf16[4,128,896]{2,1,0:T(8,128)(2,1)} %pack.1.box_ref), custom_call_target="tpu_custom_call" | custom-call | flops 1000000000 | bytes 10000000 | tf_op jit(solution)/shard_map/box_forward/pallas_call | solution.py:265
  59.0 19.9 %all-to-all-done.1.got_ref = bf16[64,56,128]{2,1,0:T(8,128)(2,1)S(1)} async-done(((bf16[64,56,128]{2,1,0:T(8,128)(2,1)}), bf16[64,56,128]{2,1,0:T(8,128)(2,1)S(1)}, u32[]{:S(2)}, u32[]{:S(2)}) %all-to-all-start.1) | async-done | bytes 917536 | tf_op jit(solution)/shard_map/reduce_zy/all_to_all | solution.py:322
  78.9 0.9 plane_sum.1
  79.8 0.0 all-gather.2.cloned.1.call-done
  79.8 9.0 %box_backward.1 = (bf16[3,128,896]{2,1,0:T(8,128)(2,1)}, f32[8,128]{1,0:T(8,128)}) custom-call(bf16[4,128,896]{2,1,0:T(8,128)(2,1)} %pack.1.box_ref, bf16[8,128,128]{2,1,0:T(8,128)(2,1)} %box_forward.1.prob_ref, bf16[8,8,16,896]{3,2,1,0:T(8,128)(2,1)} %bitcast.14), custom_call_target="tpu_custom_call" | custom-call | flops 1000 | bytes 10 | tf_op jit(solution)/shard_map/box_backward/pallas_call | solution.py:265
  88.8 3.3 %collective-permute-start.1 = (bf16[3,128,896]{2,1,0:T(8,128)(2,1)}, bf16[3,128,896]{2,1,0:T(8,128)(2,1)S(1)}, u32[]{:S(2)}, u32[]{:S(2)}) collective-permute-start(bf16[3,128,896]{2,1,0:T(8,128)(2,1)} %get-tuple-element.23), channel_id=1, source_target_pairs={{0,64},{64,128},{128,192},{192,256},{256,320},{320,384},{384,448},... | collective-permute-start | bytes 2064392 | tf_op jit(solution)/shard_map/ppermute | solution.py:350
  92.1 6.5 %all-to-all-start.2 = ((f32[8,8,128]{2,1,0:T(8,128)}), f32[8,8,128]{2,1,0:T(8,128)S(1)}, u32[]{:S(2)}, u32[]{:S(2)}) async-start(f32[8,8,128]{2,1,0:T(8,128)} %plane_sum.1), calls=%async_computation.2 | async-start | bytes 65536 | tf_op jit(solution)/shard_map/reduce_x/all_to_all | solution.py:340
  98.6 10.3 %home_backward.1 = (bf16[3,192,896]{2,1,0:T(8,128)(2,1)}, f32[8,128]{1,0:T(8,128)}) custom-call(s32[3,1,16]{2,1,0:T(1,128)} %bitcast.27, s32[2,3]{1,0:T(2,128)} %bitcast.30, bf16[3,192,896]{2,1,0:T(8,128)(2,1)} %bitcast.18, bf16[192,896]{1,0:T(8,128)(2,1)} %bitcast.21, bf16[8,192,192]{2,1,0:T(8,128)(2,1)} %get-tuple-element.14.prob_ref, ...), custom_call_target="tpu_custom_call" | custom-call | flops 1000 | bytes 10 | tf_op jit(solution)/shard_map/home_backward/pallas_call | solution.py:265
  108.9 0.0 all-to-all-done.2.got_ref
  108.9 0.0 copy-start
  108.9 0.7 copy-done
  109.6 0.7 row_sum.1
  110.3 0.0 collective-permute-done.1
  110.3 0.8 copy.9
Async XLA Ops:
  8.6 17.1 %all-to-all-start = ((bf16[8,16,896]{2,1,0:T(8,128)(2,1)}), bf16[8,16,896]{2,1,0:T(8,128)(2,1)S(1)}, u32[]{:S(2)}, u32[]{:S(2)}) async-start(bf16[8,16,896]{2,1,0:T(8,128)(2,1)} %copies.1), calls=%async_computation | async-start | bytes 458752 | tf_op jit(solution)/shard_map/weights_y/all_to_all | solution.py:295
  16.7 63.1 %all-gather.2.cloned.1.call-start = ((), (), s32[]{:S(2)}) async-start(), calls=%async_computation.3 | async-start | bytes 2064384 | tf_op jit(solution)/shard_map/weights_x/all_gather | solution.py:316
  25.7 0.7 copy-start.1
  26.4 14.7 %collective-permute-start = (bf16[64,56,128]{2,1,0:T(8,128)(2,1)}, bf16[64,56,128]{2,1,0:T(8,128)(2,1)S(1)}, u32[]{:S(2)}, u32[]{:S(2)}) collective-permute-start(bf16[64,56,128]{2,1,0:T(8,128)(2,1)} %get-tuple-element.19), channel_id=1, source_target_pairs={{0,64},{64,0},{128,192},{192,128},{256,320},{320,256},{384,448},{4... | collective-permute-start | bytes 2752520 | tf_op jit(solution)/shard_map/ppermute | solution.py:319
  43.5 35.4 %all-to-all-start.1 = ((bf16[64,56,128]{2,1,0:T(8,128)(2,1)}), bf16[64,56,128]{2,1,0:T(8,128)(2,1)S(1)}, u32[]{:S(2)}, u32[]{:S(2)}) async-start(bf16[64,56,128]{2,1,0:T(8,128)(2,1)} %add_convert_fusion), calls=%async_computation.1 | async-start | bytes 1835008 | tf_op jit(solution)/shard_map/reduce_zy/all_to_all | solution.py:322
  88.8 21.5 %collective-permute-start.1 = (bf16[3,128,896]{2,1,0:T(8,128)(2,1)}, bf16[3,128,896]{2,1,0:T(8,128)(2,1)S(1)}, u32[]{:S(2)}, u32[]{:S(2)}) collective-permute-start(bf16[3,128,896]{2,1,0:T(8,128)(2,1)} %get-tuple-element.23), channel_id=1, source_target_pairs={{0,64},{64,128},{128,192},{192,256},{256,320},{320,384},{384,448},... | collective-permute-start | bytes 2064392 | tf_op jit(solution)/shard_map/ppermute | solution.py:350
  92.1 16.8 %all-to-all-start.2 = ((f32[8,8,128]{2,1,0:T(8,128)}), f32[8,8,128]{2,1,0:T(8,128)S(1)}, u32[]{:S(2)}, u32[]{:S(2)}) async-start(f32[8,8,128]{2,1,0:T(8,128)} %plane_sum.1), calls=%async_computation.2 | async-start | bytes 65536 | tf_op jit(solution)/shard_map/reduce_x/all_to_all | solution.py:340
  108.9 0.7 copy-start
Sparse Core Ops, SparseCore 0:
  26.5 49.8 all-gather.1

commit v6 on v4

--- a/solution.py
+++ b/solution.py
@@ -82,11 +82,11 @@
 
 
 def attention(query, key, allowed):
-    scores = dot(query, key, NT) * SCALE
+    scores = dot(key, query, NT) * SCALE
     scores = jnp.where(allowed, scores, -1000000000.0)
-    peak = jnp.max(scores, axis=1, keepdims=True)
+    peak = jnp.max(scores, axis=0, keepdims=True)
     grown = jnp.exp(scores - peak)
-    return grown * (1.0 / jnp.sum(grown, axis=1, keepdims=True))
+    return grown * (1.0 / jnp.sum(grown, axis=0, keepdims=True))
 
 
 def pack_body(len_ref, move_ref, qkv_ref, cot_ref, box_ref):
@@ -108,8 +108,8 @@
     for head in range(HEADS):
         start, stop = window(head)
         query = kept(own_lanes(head), box_ref[0, :, start:stop])
-        probs = attention(query, box_ref[1, :, start:stop], col < count)
-        prob_ref[head] = jnp.where(row < count, probs, 0.0).astype(jnp.bfloat16)
+        probs = attention(query, box_ref[1, :, start:stop], row < count)
+        prob_ref[head] = jnp.where(col < count, probs, 0.0).astype(jnp.bfloat16)
 
 
 def forward_body(
@@ -130,7 +130,7 @@
         value = kept(lanes, qkv_ref[2, :, start:stop])
         probs = attention(query, qkv_ref[1, :, start:stop], allowed).astype(jnp.bfloat16)
         prob_ref[head] = probs
-        mixed = dot(probs, value, NN)
+        mixed = dot(probs, value, TN)
         offset = HSIZE * head - start
         if offset:
             mixed = pltpu.roll(mixed, stop - start - offset, 1)
@@ -170,14 +170,14 @@
     lanes = own_lanes(head)
     query = kept(lanes, rows_ref[0, :, start:stop])
     key = kept(lanes, rows_ref[1, :, start:stop])
-    grad_p = dot(back, rows_ref[2, :, start:stop], NT)
+    grad_p = dot(rows_ref[2, :, start:stop], back, NT)
     wide = probs.astype(jnp.float32)
     weighted = wide * grad_p
-    grad_s = weighted - wide * jnp.sum(weighted, axis=1, keepdims=True)
+    grad_s = weighted - wide * jnp.sum(weighted, axis=0, keepdims=True)
     grad_s = (grad_s * SCALE).astype(jnp.bfloat16)
-    tiles.add(0, head, dot(grad_s, key, NN))
-    tiles.add(1, head, dot(grad_s, query, TN))
-    tiles.add(2, head, dot(probs, back, TN))
+    tiles.add(0, head, dot(grad_s, key, TN))
+    tiles.add(1, head, dot(grad_s, query, NN))
+    tiles.add(2, head, dot(probs, back, NN))
 
 
 def back_window(head, cot, weight_ref):
@@ -326,12 +326,12 @@
     weights = after(weights, plane).reshape(NX, NY, 16, FEAT)
     send, token = kernel(
         box_backward_body, "box_backward", (shape_of((3, CLIP_MAX, FEAT), bf16), TOKEN), (),
-        (box, box_probs, weights), flops=3_000_000_000,
+        (box, box_probs, weights), flops=3000000000,
     )
     inbox = lax.ppermute(send, "dp", [(i, (i + 1) % ranks) for i in range(ranks)])
     home, token = kernel(
         home_backward_body, "home_backward", (shape_of((3, TOK, FEAT), bf16), TOKEN),
-        (counts, moving), (rows, cot, probs, weights, token), flops=6_000_000_000,
+        (counts, moving), (rows, cot, probs, weights, token), flops=12000000000,
     )
     (weight_grad,) = kernel(
         row_body, "row_sum", (shape_of((ROWS, COLS), jnp.float32),), (), (parts, token)

time: 116 us -> 114 us (0.983)
  the two profiles are of different devices: /device:TPU:1 before, /device:TPU:2 now
where the time goes in v6:
time: 114 us; the launch traced here: 113 us
  starting transfers between devices  36 us (32%)
  waiting for transfers between devices  35.3 us (31%)
  Pallas kernels  19.2 us (17%)
  between operations  14.2 us (12%)
  local copies, waits for them, and re-layouts  7.55 us (7%)
  other arithmetic  1.16 us (1%)
    all_to_all x1, waiting for transfers between devices, local(): lax.all_to_all(pair, ('dp', 'fsdp'), 0, 0, tiled=True, axis_index_groups=...  25.1 us
    pallas_call x8, Pallas kernels, kernel(): pl.pallas_call(body, out_shape=outs, in_specs=[in_smem()] * len(scalars)...  19.2 us
    all_to_all x1, starting transfers between devices, local(): lax.all_to_all(pair, ('dp', 'fsdp'), 0, 0, tiled=True, axis_index_groups=...  19.2 us
    all_to_all x1, starting transfers between devices, local(): lax.all_to_all(copies, 'fsdp', 0, 0, tiled=True, axis_index_groups=Y_GROUPS)  7.56 us
    unnamed x27, local copies, waits for them, and re-layouts  7.55 us
    all_to_all x1, starting transfers between devices, local(): lax.all_to_all(plane, 'fsdp', 0, 0, tiled=True, axis_index_groups=X_GROUPS)  7.29 us
    ppermute x1, waiting for transfers between devices, local(): lax.ppermute(send, 'dp', [(i, (i + 1) % ranks) for i in range(ranks)])  3.97 us
    all_to_all x1, waiting for transfers between devices, local(): lax.all_to_all(copies, 'fsdp', 0, 0, tiled=True, axis_index_groups=Y_GROUPS)  3.8 us
  transfers between devices with their start and end apart: 6, of which 4 were waited for; matrix products, arithmetic and copies ran while one was open for 1% of the time, Pallas kernels for 16%

profile of v6, /device:TPU:2, one launch (start us, length us, event | category | flops | bytes accessed | tf_op | source)
XLA Modules:
  0.0 113.5 jit_solution(11752895671399045510)
XLA Ops:
  7.2 0.0 copy-start.9
  7.2 0.7 copy-done.9
  7.9 0.7 copies.1
  8.6 7.6 %all-to-all-start = ((bf16[8,16,896]{2,1,0:T(8,128)(2,1)}), bf16[8,16,896]{2,1,0:T(8,128)(2,1)S(1)}, u32[]{:S(2)}, u32[]{:S(2)}) async-start(bf16[8,16,896]{2,1,0:T(8,128)(2,1)} %copies.1), calls=%async_computation | async-start | bytes 458752 | tf_op jit(solution)/shard_map/weights_y/all_to_all | solution.py:280
  16.2 0.0 all-gather.2.cloned.1.call-start
  16.2 0.0 copy-start
  16.2 1.2 %copy-done = bf16[1,1,192,3,896]{4,2,3,1,0:T(8,128)(2,1)S(1)} copy-done((bf16[1,1,192,3,896]{4,2,3,1,0:T(8,128)(2,1)S(1)}, bf16[1,1,192,3,896]{4,2,3,1,0:T(8,128)(2,1)}, u32[]{:S(2)}) %copy-start) | copy-done | bytes 1032216
  17.4 0.0 copy-start.2
  17.4 1.0 copy-done.2
  18.4 0.0 copy-start.4
  18.4 0.7 copy-done.4
  19.1 3.6 %forward.1 = (bf16[64,56,128]{2,1,0:T(8,128)(2,1)S(1)}, bf16[64,56,128]{2,1,0:T(8,128)(2,1)S(1)}, bf16[8,192,192]{2,1,0:T(8,128)(2,1)S(1)}, f32[8,128]{1,0:T(8,128)}) custom-call(s32[3,1,16]{2,1,0:T(1,128)S(1)} %bitcast.20, bf16[3,192,896]{2,1,0:T(8,128)(2,1)S(1)} %bitcast.14, bf16[192,896]{1,0:T(8,128)(2,1)S(1)} %bitcast.17), custom_call_target="tpu_custom_call" | custom-call | flops 3000000000 | bytes 4000000 | tf_op jit(solution)/shard_map/forward/pallas_call | solution.py:252
  22.7 0.0 copy-start.10
  22.7 0.9 copy-done.10
  23.5 3.8 %all-to-all-done = bf16[8,16,896]{2,1,0:T(8,128)(2,1)S(1)} async-done(((bf16[8,16,896]{2,1,0:T(8,128)(2,1)}), bf16[8,16,896]{2,1,0:T(8,128)(2,1)S(1)}, u32[]{:S(2)}, u32[]{:S(2)}) %all-to-all-start) | async-done | bytes 229408 | tf_op jit(solution)/shard_map/weights_y/all_to_all | solution.py:280
  27.4 0.0 copy-start.12
  27.4 0.7 copy-done.12
  28.0 0.0 all-gather.2.cloned.1.call-update
  28.1 1.9 %collective-permute-start = (bf16[64,56,128]{2,1,0:T(8,128)(2,1)S(1)}, bf16[64,56,128]{2,1,0:T(8,128)(2,1)S(1)}, u32[]{:S(2)}, u32[]{:S(2)}) collective-permute-start(bf16[64,56,128]{2,1,0:T(8,128)(2,1)S(1)} %get-tuple-element.18), channel_id=1, source_target_pairs={{0,64},{64,0},{128,192},{192,128},{256,320},{320,256},{384,448},{4... | collective-permute-start | bytes 2752520 | tf_op jit(solution)/shard_map/ppermute | solution.py:304
  30.0 2.4 %collective-permute-done = bf16[64,56,128]{2,1,0:T(8,128)(2,1)S(1)} collective-permute-done((bf16[64,56,128]{2,1,0:T(8,128)(2,1)S(1)}, bf16[64,56,128]{2,1,0:T(8,128)(2,1)S(1)}, u32[]{:S(2)}, u32[]{:S(2)}) %collective-permute-start) | collective-permute-done | bytes 917536 | tf_op jit(solution)/shard_map/ppermute | solution.py:304
  32.4 0.0 copy-start.1
  32.4 0.0 copy-start.3
  32.4 0.0 copy-start.5
  32.4 0.0 copy-start.6
  32.4 1.2 %add_convert_fusion = bf16[64,56,128]{2,1,0:T(8,128)(2,1)} fusion(bf16[64,56,128]{2,1,0:T(8,128)(2,1)S(1)} %collective-permute-done, bf16[64,56,128]{2,1,0:T(8,128)(2,1)S(1)} %get-tuple-element.17), kind=kLoop, calls=%fused_computation | loop fusion | flops 1835008 | bytes 2752512 | tf_op jit(solution)/shard_map/convert_element_type | solution.py:305
  33.6 19.2 %all-to-all-start.1 = ((bf16[64,56,128]{2,1,0:T(8,128)(2,1)}), bf16[64,56,128]{2,1,0:T(8,128)(2,1)S(1)}, u32[]{:S(2)}, u32[]{:S(2)}) async-start(bf16[64,56,128]{2,1,0:T(8,128)(2,1)} %add_convert_fusion), calls=%async_computation.1 | async-start | bytes 1835008 | tf_op jit(solution)/shard_map/reduce_zy/all_to_all | solution.py:307
  52.8 0.0 copy-done.1
  52.8 0.0 copy-done.3
  52.8 0.0 copy-done.5
  52.9 0.0 copy-done.6
  52.9 1.0 pack.1.box_ref
  53.9 1.0 box_forward.1.prob_ref
  54.9 25.1 %all-to-all-done.1.got_ref = bf16[64,56,128]{2,1,0:T(8,128)(2,1)S(1)} async-done(((bf16[64,56,128]{2,1,0:T(8,128)(2,1)}), bf16[64,56,128]{2,1,0:T(8,128)(2,1)S(1)}, u32[]{:S(2)}, u32[]{:S(2)}) %all-to-all-start.1) | async-done | bytes 917536 | tf_op jit(solution)/shard_map/reduce_zy/all_to_all | solution.py:307
  79.9 0.9 plane_sum.1
  80.9 7.3 %all-to-all-start.2 = ((f32[8,8,128]{2,1,0:T(8,128)}), f32[8,8,128]{2,1,0:T(8,128)S(1)}, u32[]{:S(2)}, u32[]{:S(2)}) async-start(f32[8,8,128]{2,1,0:T(8,128)} %plane_sum.1), calls=%async_computation.2 | async-start | bytes 65536 | tf_op jit(solution)/shard_map/reduce_x/all_to_all | solution.py:325
  88.2 0.0 all-gather.2.cloned.1.call-done
  88.2 0.0 copy-start.7
  88.2 1.5 %copy-done.7 = bf16[1024,896]{1,0:T(8,128)(2,1)S(1)} copy-done((bf16[1024,896]{1,0:T(8,128)(2,1)S(1)}, bf16[1024,896]{1,0:T(8,128)(2,1)}, u32[]{:S(2)}) %copy-start.7) | copy-done | bytes 1835032
  89.7 0.0 copy-start.8
  89.7 4.5 %box_backward.1 = (bf16[3,128,896]{2,1,0:T(8,128)(2,1)S(1)}, f32[8,128]{1,0:T(8,128)S(1)}) custom-call(bf16[4,128,896]{2,1,0:T(8,128)(2,1)S(1)} %pack.1.box_ref, bf16[8,128,128]{2,1,0:T(8,128)(2,1)S(1)} %box_forward.1.prob_ref, bf16[8,8,16,896]{3,2,1,0:T(8,128)(2,1)S(1)} %bitcast.27), custom_call_target="tpu_custom_call" | custom-call | flops 3000000000 | bytes 4000000 | tf_op jit(solution)/shard_map/box_backward/pallas_call | solution.py:252
  94.2 0.0 collective-permute-start.1
  94.2 0.0 copy-done.8
  94.2 0.0 copy-done.11
  94.2 6.9 %home_backward.1 = (bf16[3,192,896]{2,1,0:T(8,128)(2,1)}, f32[8,128]{1,0:T(8,128)S(1)}) custom-call(s32[3,1,16]{2,1,0:T(1,128)S(1)} %bitcast.23, s32[2,3]{1,0:T(2,128)S(1)} %bitcast.26, bf16[3,192,896]{2,1,0:T(8,128)(2,1)S(1)} %bitcast.16, bf16[192,896]{1,0:T(8,128)(2,1)S(1)} %bitcast.19, bf16[8,192,192]{2,1,0:T(8,128)(2,1)S(1)} %copy-done.11, ...), custom_call_target="tpu_custom_call" | custom-call | flops 12000000000 | bytes 4000000 | tf_op jit(solution)/shard_map/home_backward/pallas_call | solution.py:252
  101.1 0.0 all-to-all-done.2.got_ref
  101.1 0.7 row_sum.1
  101.8 4.0 %collective-permute-done.1 = bf16[3,128,896]{2,1,0:T(8,128)(2,1)S(1)} collective-permute-done((bf16[3,128,896]{2,1,0:T(8,128)(2,1)S(1)}, bf16[3,128,896]{2,1,0:T(8,128)(2,1)S(1)}, u32[]{:S(2)}, u32[]{:S(2)}) %collective-permute-start.1) | collective-permute-done | bytes 688160 | tf_op jit(solution)/shard_map/ppermute | solution.py:331
  105.8 0.8 copy.9
  (1 shorter events, 0.0 us)
Async XLA Ops:
  7.2 0.7 copy-start.9
  8.6 18.7 %all-to-all-start = ((bf16[8,16,896]{2,1,0:T(8,128)(2,1)}), bf16[8,16,896]{2,1,0:T(8,128)(2,1)S(1)}, u32[]{:S(2)}, u32[]{:S(2)}) async-start(bf16[8,16,896]{2,1,0:T(8,128)(2,1)} %copies.1), calls=%async_computation | async-start | bytes 458752 | tf_op jit(solution)/shard_map/weights_y/all_to_all | solution.py:280
  16.2 72.0 %all-gather.2.cloned.1.call-start = ((), (), s32[]{:S(2)}) async-start(), calls=%async_computation.3 | async-start | bytes 2064384 | tf_op jit(solution)/shard_map/weights_x/all_gather | solution.py:301
  16.2 1.2 %copy-start = (bf16[1,1,192,3,896]{4,2,3,1,0:T(8,128)(2,1)S(1)}, bf16[1,1,192,3,896]{4,2,3,1,0:T(8,128)(2,1)}, u32[]{:S(2)}) copy-start(bf16[1,1,192,3,896]{4,2,3,1,0:T(8,128)(2,1)} %param.5) | copy-start | bytes 3096580
  17.4 1.0 copy-start.2
  18.4 0.7 copy-start.4
  22.7 0.9 copy-start.10
  27.4 0.7 copy-start.12
  28.1 4.4 %collective-permute-start = (bf16[64,56,128]{2,1,0:T(8,128)(2,1)S(1)}, bf16[64,56,128]{2,1,0:T(8,128)(2,1)S(1)}, u32[]{:S(2)}, u32[]{:S(2)}) collective-permute-start(bf16[64,56,128]{2,1,0:T(8,128)(2,1)S(1)} %get-tuple-element.18), channel_id=1, source_target_pairs={{0,64},{64,0},{128,192},{192,128},{256,320},{320,256},{384,448},{4... | collective-permute-start | bytes 2752520 | tf_op jit(solution)/shard_map/ppermute | solution.py:304
  32.4 20.4 %copy-start.1 = (bf16[1,1,192,3,896]{4,2,3,1,0:T(8,128)(2,1)S(1)}, bf16[1,1,192,3,896]{4,2,3,1,0:T(8,128)(2,1)}, u32[]{:S(2)}) copy-start(bf16[1,1,192,3,896]{4,2,3,1,0:T(8,128)(2,1)} %param.5) | copy-start | bytes 3096580
  32.4 20.4 %copy-start.3 = (bf16[1,1,192,896]{3,2,1,0:T(8,128)(2,1)S(1)}, bf16[1,1,192,896]{3,2,1,0:T(8,128)(2,1)}, u32[]{:S(2)}) copy-start(bf16[1,1,192,896]{3,2,1,0:T(8,128)(2,1)} %param.6) | copy-start | bytes 1032196
  32.4 20.4 %copy-start.5 = (s32[16,1,3]{0,1,2:T(1,128)S(1)}, s32[16,1,3]{0,1,2:T(1,128)}, u32[]{:S(2)}) copy-start(s32[16,1,3]{0,1,2:T(1,128)} %param.7) | copy-start | bytes 580
  32.4 20.4 %copy-start.6 = (s32[1,2,3]{2,1,0:T(2,128)S(1)}, s32[1,2,3]{2,1,0:T(2,128)}, u32[]{:S(2)}) copy-start(s32[1,2,3]{2,1,0:T(2,128)} %param.8) | copy-start | bytes 76
  33.6 46.3 %all-to-all-start.1 = ((bf16[64,56,128]{2,1,0:T(8,128)(2,1)}), bf16[64,56,128]{2,1,0:T(8,128)(2,1)S(1)}, u32[]{:S(2)}, u32[]{:S(2)}) async-start(bf16[64,56,128]{2,1,0:T(8,128)(2,1)} %add_convert_fusion), calls=%async_computation.1 | async-start | bytes 1835008 | tf_op jit(solution)/shard_map/reduce_zy/all_to_all | solution.py:307
  80.9 20.3 %all-to-all-start.2 = ((f32[8,8,128]{2,1,0:T(8,128)}), f32[8,8,128]{2,1,0:T(8,128)S(1)}, u32[]{:S(2)}, u32[]{:S(2)}) async-start(f32[8,8,128]{2,1,0:T(8,128)} %plane_sum.1), calls=%async_computation.2 | async-start | bytes 65536 | tf_op jit(solution)/shard_map/reduce_x/all_to_all | solution.py:325
  88.2 1.5 %copy-start.7 = (bf16[1024,896]{1,0:T(8,128)(2,1)S(1)}, bf16[1024,896]{1,0:T(8,128)(2,1)}, u32[]{:S(2)}) copy-start(bf16[1024,896]{1,0:T(8,128)(2,1)} %all-gather.2.cloned.1.call-done) | copy-start | bytes 5505028
  89.7 4.6 %copy-start.8 = (bf16[1024,896]{1,0:T(8,128)(2,1)S(1)}, bf16[1024,896]{1,0:T(8,128)(2,1)}, u32[]{:S(2)}) copy-start(bf16[1024,896]{1,0:T(8,128)(2,1)} %all-gather.2.cloned.1.call-done) | copy-start | bytes 5505028
  89.7 4.6 %copy-start.11 = (bf16[8,192,192]{2,1,0:T(8,128)(2,1)S(1)}, bf16[8,192,192]{2,1,0:T(8,128)(2,1)}, u32[]{:S(2)}) copy-start(bf16[8,192,192]{2,1,0:T(8,128)(2,1)} %copy-done.10) | copy-start | bytes 1769476
  94.2 11.6 %collective-permute-start.1 = (bf16[3,128,896]{2,1,0:T(8,128)(2,1)S(1)}, bf16[3,128,896]{2,1,0:T(8,128)(2,1)S(1)}, u32[]{:S(2)}, u32[]{:S(2)}) collective-permute-start(bf16[3,128,896]{2,1,0:T(8,128)(2,1)S(1)} %get-tuple-element.23), channel_id=1, source_target_pairs={{0,64},{64,128},{128,192},{192,256},{256,320},{320,384},{384,448},... | collective-permute-start | bytes 2064392 | tf_op jit(solution)/shard_map/ppermute | solution.py:331
Sparse Core Ops, SparseCore 0:
  28.2 52.6 all-gather.1

commit v7 on v6

--- a/solution.py
+++ b/solution.py
@@ -45,13 +45,6 @@
     start, stop = window(head)
     lane = lax.broadcasted_iota(jnp.int32, (1, stop - start), 1) + start
     return (lane >= HSIZE * head) & (lane < HSIZE * (head + 1))
-
-
-def gathered_lanes(width):
-    row = lax.broadcasted_iota(jnp.int32, (TILE, width), 0)
-    lane = lax.broadcasted_iota(jnp.int32, (TILE, width), 1)
-    inner = row & 15
-    return jnp.where(inner < ROWS, lane - (row >> 4) * ROWS - inner, -1)
 
 
 def kept(mask, value):
@@ -180,32 +173,48 @@
     tiles.add(2, head, dot(probs, back, NN))
 
 
-def back_window(head, cot, weight_ref):
-    start, stop = window(head)
-    packed = dot(cot, weight_ref[:, head].reshape(TILE, FEAT), NT).astype(jnp.bfloat16)
-    pick = as_bf16(gathered_lanes(stop - start) == HSIZE * head - start)
-    return dot(packed, pick, NN).astype(jnp.bfloat16)
-
-
-def box_backward_body(box_ref, prob_ref, weight_ref, send_ref, token_ref):
+def fill_swap(swap_ref):
+    lane = lax.broadcasted_iota(jnp.int32, (1, FEAT), 1)
+    outer = lax.div(lane, HSIZE)
+    inner = lax.div(lane - HSIZE * outer, ROWS)
+    wanted = lane + (HSIZE - ROWS) * (inner - outer)
+    for part in range(FEAT // HSIZE):
+        rows = lax.broadcasted_iota(jnp.int32, (HSIZE, FEAT), 0) + HSIZE * part
+        swap_ref[HSIZE * part:HSIZE * (part + 1), :] = as_bf16(rows == wanted)
+
+
+def all_gradients(tiles, rows_ref, cot, prob_ref, weight_ref, swap_ref, back_ref):
+    fill_swap(swap_ref)
+    packed = dot(cot, weight_ref[...], NT).astype(jnp.bfloat16)
+    back_ref[...] = dot(packed, swap_ref[...], NN).astype(jnp.bfloat16)
+    for head in range(HEADS):
+        start, stop = window(head)
+        back = kept(own_lanes(head), back_ref[:, start:stop])
+        add_gradient(tiles, head, rows_ref, prob_ref[head], back)
+
+
+def box_backward_body(box_ref, prob_ref, weight_ref, send_ref, token_ref, swap_ref, back_ref):
     tiles = Tiles(send_ref, None)
-    cot = box_ref[3]
-    for head in range(HEADS):
-        add_gradient(tiles, head, box_ref, prob_ref[head], back_window(head, cot, weight_ref))
+    all_gradients(tiles, box_ref, box_ref[3], prob_ref, weight_ref, swap_ref, back_ref)
     token_ref[...] = jnp.zeros(token_ref.shape, jnp.float32)
 
 
 def home_backward_body(
-    len_ref, move_ref, qkv_ref, cot_ref, prob_ref, weight_ref, order_ref, home_ref, token_ref,
+    len_ref, move_ref, qkv_ref, cot_ref, prob_ref, weight_ref, order_ref,
+    home_ref, token_ref, swap_ref, back_ref,
 ):
     rank = lax.axis_index("dp")
     begin, count = moved_clip(len_ref, move_ref, rank)
     place = lax.broadcasted_iota(jnp.int32, (TOK, TILE), 0)
     tiles = Tiles(home_ref, (place < begin) | (place >= begin + count))
-    cot = cot_ref[...]
-    for head in range(HEADS):
-        add_gradient(tiles, head, qkv_ref, prob_ref[head], back_window(head, cot, weight_ref))
+    all_gradients(tiles, qkv_ref, cot_ref[...], prob_ref, weight_ref, swap_ref, back_ref)
     token_ref[...] = order_ref[...]
+
+
+def compact_body(column_ref, shard_ref, wide_ref):
+    for y in range(NY):
+        wide_ref[ROWS * y:ROWS * (y + 1), :] = column_ref[y].astype(jnp.float32)[:ROWS]
+    shard_ref[...] = wide_ref[...].astype(jnp.bfloat16)
 
 
 def copies_body(shard_ref, copies_ref):
@@ -296,10 +305,13 @@
         ),
         flops=3_000_000_000,
     )
-    column = after(column, token)
+    (column,) = kernel(
+        compact_body, "compact", (shape_of((NY * ROWS, FEAT), bf16),), (),
+        (after(column, token),), scratch=(pltpu.VMEM((NY * ROWS, FEAT), jnp.float32),),
+    )
     with jax.named_scope("weights_x"):
         weights = lax.all_gather(
-            column.reshape(NY * 16, FEAT), "fsdp", axis=0, tiled=True, axis_index_groups=X_GROUPS
+            column, "fsdp", axis=0, tiled=True, axis_index_groups=X_GROUPS
         )
     swapped = lax.ppermute(other, "dp", [(i, i + 1 - 2 * (i % NCORE)) for i in range(ranks)])
     pair = (own.astype(jnp.float32) + swapped.astype(jnp.float32)).astype(bf16)
@@ -323,15 +335,17 @@
     )
     with jax.named_scope("reduce_x"):
         parts = lax.all_to_all(plane, "fsdp", 0, 0, tiled=True, axis_index_groups=X_GROUPS)
-    weights = after(weights, plane).reshape(NX, NY, 16, FEAT)
+    weights = after(weights, plane)
     send, token = kernel(
         box_backward_body, "box_backward", (shape_of((3, CLIP_MAX, FEAT), bf16), TOKEN), (),
-        (box, box_probs, weights), flops=3000000000,
+        (box, box_probs, weights),
+        scratch=(pltpu.VMEM((FEAT, FEAT), bf16), pltpu.VMEM((CLIP_MAX, FEAT), bf16)), flops=3000000000,
     )
     inbox = lax.ppermute(send, "dp", [(i, (i + 1) % ranks) for i in range(ranks)])
     home, token = kernel(
         home_backward_body, "home_backward", (shape_of((3, TOK, FEAT), bf16), TOKEN),
-        (counts, moving), (rows, cot, probs, weights, token), flops=12000000000,
+        (counts, moving), (rows, cot, probs, weights, token),
+        scratch=(pltpu.VMEM((FEAT, FEAT), bf16), pltpu.VMEM((TOK, FEAT), bf16)), flops=12000000000,
     )
     (weight_grad,) = kernel(
         row_body, "row_sum", (shape_of((ROWS, COLS), jnp.float32),), (), (parts, token)

time: 114 us -> 112 us (0.982)
  starting transfers between devices: 36 us -> 39.8 us
  Pallas kernels: 19.2 us -> 15.8 us
  waiting for transfers between devices: 35.3 us -> 33.2 us
    all_to_all x1, starting transfers between devices: 19.2 us -> 23 us  [local(): lax.all_to_all(pair, ('dp', 'fsdp'), 0, 0, tiled=True, axis_index_groups=...]
    pallas_call x8 -> x9, Pallas kernels: 19.2 us -> 15.8 us  [kernel(): pl.pallas_call(body, out_shape=outs, in_specs=[in_smem()] * len(scalars)...]
    ppermute x1, waiting for transfers between devices: 2.44 us -> 0.01 us  [local(): lax.ppermute(other, 'dp', [(i, i + 1 - 2 * (i % NCORE)) for i in range(ra...]
    ppermute x1, waiting for transfers between devices: 3.97 us -> 6.24 us  [local(): lax.ppermute(send, 'dp', [(i, (i + 1) % ranks) for i in range(ranks)])]
    all_to_all x1, waiting for transfers between devices: 3.8 us -> 1.88 us  [local(): lax.all_to_all(copies, 'fsdp', 0, 0, tiled=True, axis_index_groups=Y_GROUPS)]
    unnamed x27 -> x25, local copies, waits for them, and re-layouts: 7.55 us -> 6.79 us
  transfers between devices with their start and end apart: 6 -> 6, of which waited for: 4 -> 3; matrix products, arithmetic and copies ran while one was open for 1% -> 1% of each run, Pallas kernels for 16% -> 14%
where the time goes in v7:
time: 112 us; the launch traced here: 111 us
  starting transfers between devices  39.8 us (36%)
  waiting for transfers between devices  33.2 us (30%)
  Pallas kernels  15.8 us (14%)
  between operations  14.2 us (13%)
  local copies, waits for them, and re-layouts  6.79 us (6%)
  other arithmetic  1.16 us (1%)
    all_to_all x1, waiting for transfers between devices, local(): lax.all_to_all(pair, ('dp', 'fsdp'), 0, 0, tiled=True, axis_index_groups=...  25.1 us
    all_to_all x1, starting transfers between devices, local(): lax.all_to_all(pair, ('dp', 'fsdp'), 0, 0, tiled=True, axis_index_groups=...  23 us
    pallas_call x9, Pallas kernels, kernel(): pl.pallas_call(body, out_shape=outs, in_specs=[in_smem()] * len(scalars)...  15.8 us
    all_to_all x1, starting transfers between devices, local(): lax.all_to_all(copies, 'fsdp', 0, 0, tiled=True, axis_index_groups=Y_GROUPS)  7.56 us
    all_to_all x1, starting transfers between devices, local(): lax.all_to_all(plane, 'fsdp', 0, 0, tiled=True, axis_index_groups=X_GROUPS)  7.29 us
    unnamed x25, local copies, waits for them, and re-layouts  6.79 us
    ppermute x1, waiting for transfers between devices, local(): lax.ppermute(send, 'dp', [(i, (i + 1) % ranks) for i in range(ranks)])  6.24 us
  transfers between devices with their start and end apart: 6, of which 3 were waited for; matrix products, arithmetic and copies ran while one was open for 1% of the time, Pallas kernels for 14%

profile of v7, /device:TPU:2, one launch (start us, length us, event | category | flops | bytes accessed | tf_op | source)
XLA Modules:
  0.0 110.9 jit_solution(2790461274977976708)
XLA Ops:
  7.2 0.0 copy-start.9
  7.2 0.7 copy-done.9
  7.9 0.7 copies.1
  8.6 7.6 %all-to-all-start = ((bf16[8,16,896]{2,1,0:T(8,128)(2,1)}), bf16[8,16,896]{2,1,0:T(8,128)(2,1)S(1)}, u32[]{:S(2)}, u32[]{:S(2)}) async-start(bf16[8,16,896]{2,1,0:T(8,128)(2,1)} %copies.1), calls=%async_computation | async-start | bytes 458752 | tf_op jit(solution)/shard_map/weights_y/all_to_all | solution.py:289
  16.2 0.0 all-gather.2.cloned.1.call-start
  16.2 0.0 copy-start
  16.2 1.2 %copy-done = bf16[1,1,192,3,896]{4,2,3,1,0:T(8,128)(2,1)S(1)} copy-done((bf16[1,1,192,3,896]{4,2,3,1,0:T(8,128)(2,1)S(1)}, bf16[1,1,192,3,896]{4,2,3,1,0:T(8,128)(2,1)}, u32[]{:S(2)}) %copy-start) | copy-done | bytes 1032216
  17.4 0.0 copy-start.2
  17.4 1.0 copy-done.2
  18.4 0.0 copy-start.4
  18.4 0.7 copy-done.4
  19.1 3.6 %forward.1 = (bf16[64,56,128]{2,1,0:T(8,128)(2,1)S(1)}, bf16[64,56,128]{2,1,0:T(8,128)(2,1)S(1)}, bf16[8,192,192]{2,1,0:T(8,128)(2,1)S(1)}, f32[8,128]{1,0:T(8,128)}) custom-call(s32[3,1,16]{2,1,0:T(1,128)S(1)} %bitcast.18, bf16[3,192,896]{2,1,0:T(8,128)(2,1)S(1)} %bitcast.12, bf16[192,896]{1,0:T(8,128)(2,1)S(1)} %bitcast.15), custom_call_target="tpu_custom_call" | custom-call | flops 3000000000 | bytes 4000000 | tf_op jit(solution)/shard_map/forward/pallas_call | solution.py:261
  22.7 0.0 copy-start.10
  22.7 0.9 copy-done.10
  23.6 1.9 %collective-permute-start = (bf16[64,56,128]{2,1,0:T(8,128)(2,1)S(1)}, bf16[64,56,128]{2,1,0:T(8,128)(2,1)S(1)}, u32[]{:S(2)}, u32[]{:S(2)}) collective-permute-start(bf16[64,56,128]{2,1,0:T(8,128)(2,1)S(1)} %get-tuple-element.18), channel_id=1, source_target_pairs={{0,64},{64,0},{128,192},{192,128},{256,320},{320,256},{384,448},{4... | collective-permute-start | bytes 2752520 | tf_op jit(solution)/shard_map/ppermute | solution.py:316
  25.5 1.9 %all-to-all-done.column_ref = bf16[8,16,896]{2,1,0:T(8,128)(2,1)S(1)} async-done(((bf16[8,16,896]{2,1,0:T(8,128)(2,1)}), bf16[8,16,896]{2,1,0:T(8,128)(2,1)S(1)}, u32[]{:S(2)}, u32[]{:S(2)}) %all-to-all-start) | async-done | bytes 229408 | tf_op jit(solution)/shard_map/weights_y/all_to_all | solution.py:289
  27.4 0.7 compact.1
  28.1 0.0 all-gather.2.cloned.1.call-update
  28.1 0.0 collective-permute-done
  28.1 1.2 %add_convert_fusion = bf16[64,56,128]{2,1,0:T(8,128)(2,1)} fusion(bf16[64,56,128]{2,1,0:T(8,128)(2,1)S(1)} %collective-permute-done, bf16[64,56,128]{2,1,0:T(8,128)(2,1)S(1)} %get-tuple-element.17), kind=kLoop, calls=%fused_computation | loop fusion | flops 1835008 | bytes 2752512 | tf_op jit(solution)/shard_map/convert_element_type | solution.py:317
  29.3 0.0 copy-start.1
  29.3 0.0 copy-start.3
  29.3 0.0 copy-start.5
  29.3 0.0 copy-start.6
  29.3 23.0 %all-to-all-start.1 = ((bf16[64,56,128]{2,1,0:T(8,128)(2,1)}), bf16[64,56,128]{2,1,0:T(8,128)(2,1)S(1)}, u32[]{:S(2)}, u32[]{:S(2)}) async-start(bf16[64,56,128]{2,1,0:T(8,128)(2,1)} %add_convert_fusion), calls=%async_computation.1 | async-start | bytes 1835008 | tf_op jit(solution)/shard_map/reduce_zy/all_to_all | solution.py:319
  52.3 0.0 copy-done.1
  52.3 0.0 copy-done.3
  52.3 0.0 copy-done.5
  52.3 0.0 copy-done.6
  52.3 1.0 pack.1.box_ref
  53.3 1.0 box_forward.1.prob_ref
  54.3 25.1 %all-to-all-done.1.got_ref = bf16[64,56,128]{2,1,0:T(8,128)(2,1)S(1)} async-done(((bf16[64,56,128]{2,1,0:T(8,128)(2,1)}), bf16[64,56,128]{2,1,0:T(8,128)(2,1)S(1)}, u32[]{:S(2)}, u32[]{:S(2)}) %all-to-all-start.1) | async-done | bytes 917536 | tf_op jit(solution)/shard_map/reduce_zy/all_to_all | solution.py:319
  79.4 0.9 plane_sum.1
  80.3 7.3 %all-to-all-start.2 = ((f32[8,8,128]{2,1,0:T(8,128)}), f32[8,8,128]{2,1,0:T(8,128)S(1)}, u32[]{:S(2)}, u32[]{:S(2)}) async-start(f32[8,8,128]{2,1,0:T(8,128)} %plane_sum.1), calls=%async_computation.2 | async-start | bytes 65536 | tf_op jit(solution)/shard_map/reduce_x/all_to_all | solution.py:337
  87.6 0.0 all-gather.2.cloned.1.call-done.weight_ref
  87.6 0.0 copy-start.7
  87.6 1.4 %copy-done.7 = bf16[896,896]{1,0:T(8,128)(2,1)S(1)} copy-done((bf16[896,896]{1,0:T(8,128)(2,1)S(1)}, bf16[896,896]{1,0:T(8,128)(2,1)}, u32[]{:S(2)}) %copy-start.7) | copy-done | bytes 1605656
  89.0 0.0 copy-start.8
  89.0 0.0 copy-start.11
  89.0 2.6 %box_backward.1 = (bf16[3,128,896]{2,1,0:T(8,128)(2,1)S(1)}, f32[8,128]{1,0:T(8,128)S(1)}) custom-call(bf16[4,128,896]{2,1,0:T(8,128)(2,1)S(1)} %pack.1.box_ref, bf16[8,128,128]{2,1,0:T(8,128)(2,1)S(1)} %box_forward.1.prob_ref, bf16[896,896]{1,0:T(8,128)(2,1)S(1)} %copy-done.7), custom_call_target="tpu_custom_call" | custom-call | flops 3000000000 | bytes 4000000 | tf_op jit(solution)/shard_map/box_backward/pallas_call | solution.py:261
  91.6 0.0 collective-permute-start.1
  91.7 0.0 copy-done.8
  91.7 0.0 copy-done.11
  91.7 4.6 %home_backward.1 = (bf16[3,192,896]{2,1,0:T(8,128)(2,1)}, f32[8,128]{1,0:T(8,128)S(1)}) custom-call(s32[3,1,16]{2,1,0:T(1,128)S(1)} %bitcast.21, s32[2,3]{1,0:T(2,128)S(1)} %bitcast.24, bf16[3,192,896]{2,1,0:T(8,128)(2,1)S(1)} %bitcast.14, bf16[192,896]{1,0:T(8,128)(2,1)S(1)} %bitcast.17, bf16[8,192,192]{2,1,0:T(8,128)(2,1)S(1)} %copy-done.11, ...), custom_call_target="tpu_custom_call" | custom-call | flops 12000000000 | bytes 4000000 | tf_op jit(solution)/shard_map/home_backward/pallas_call | solution.py:261
  96.3 0.0 all-to-all-done.2.got_ref
  96.3 0.7 row_sum.1
  97.0 6.2 %collective-permute-done.1 = bf16[3,128,896]{2,1,0:T(8,128)(2,1)S(1)} collective-permute-done((bf16[3,128,896]{2,1,0:T(8,128)(2,1)S(1)}, bf16[3,128,896]{2,1,0:T(8,128)(2,1)S(1)}, u32[]{:S(2)}, u32[]{:S(2)}) %collective-permute-start.1) | collective-permute-done | bytes 688160 | tf_op jit(solution)/shard_map/ppermute | solution.py:344
  103.2 0.8 copy.9
Async XLA Ops:
  7.2 0.7 copy-start.9
  8.6 18.7 %all-to-all-start = ((bf16[8,16,896]{2,1,0:T(8,128)(2,1)}), bf16[8,16,896]{2,1,0:T(8,128)(2,1)S(1)}, u32[]{:S(2)}, u32[]{:S(2)}) async-start(bf16[8,16,896]{2,1,0:T(8,128)(2,1)} %copies.1), calls=%async_computation | async-start | bytes 458752 | tf_op jit(solution)/shard_map/weights_y/all_to_all | solution.py:289
  16.2 71.4 %all-gather.2.cloned.1.call-start = ((), (), s32[]{:S(2)}) async-start(), calls=%async_computation.3 | async-start | bytes 1806336 | tf_op jit(solution)/shard_map/weights_x/all_gather | solution.py:313
  16.2 1.2 %copy-start = (bf16[1,1,192,3,896]{4,2,3,1,0:T(8,128)(2,1)S(1)}, bf16[1,1,192,3,896]{4,2,3,1,0:T(8,128)(2,1)}, u32[]{:S(2)}) copy-start(bf16[1,1,192,3,896]{4,2,3,1,0:T(8,128)(2,1)} %param.5) | copy-start | bytes 3096580
  17.4 1.0 copy-start.2
  18.4 0.7 copy-start.4
  22.7 0.9 copy-start.10
  23.6 4.5 %collective-permute-start = (bf16[64,56,128]{2,1,0:T(8,128)(2,1)S(1)}, bf16[64,56,128]{2,1,0:T(8,128)(2,1)S(1)}, u32[]{:S(2)}, u32[]{:S(2)}) collective-permute-start(bf16[64,56,128]{2,1,0:T(8,128)(2,1)S(1)} %get-tuple-element.18), channel_id=1, source_target_pairs={{0,64},{64,0},{128,192},{192,128},{256,320},{320,256},{384,448},{4... | collective-permute-start | bytes 2752520 | tf_op jit(solution)/shard_map/ppermute | solution.py:316
  29.3 23.0 %copy-start.1 = (bf16[1,1,192,3,896]{4,2,3,1,0:T(8,128)(2,1)S(1)}, bf16[1,1,192,3,896]{4,2,3,1,0:T(8,128)(2,1)}, u32[]{:S(2)}) copy-start(bf16[1,1,192,3,896]{4,2,3,1,0:T(8,128)(2,1)} %param.5) | copy-start | bytes 3096580
  29.3 23.0 %copy-start.3 = (bf16[1,1,192,896]{3,2,1,0:T(8,128)(2,1)S(1)}, bf16[1,1,192,896]{3,2,1,0:T(8,128)(2,1)}, u32[]{:S(2)}) copy-start(bf16[1,1,192,896]{3,2,1,0:T(8,128)(2,1)} %param.6) | copy-start | bytes 1032196
  29.3 23.0 %copy-start.5 = (s32[16,1,3]{0,1,2:T(1,128)S(1)}, s32[16,1,3]{0,1,2:T(1,128)}, u32[]{:S(2)}) copy-start(s32[16,1,3]{0,1,2:T(1,128)} %param.7) | copy-start | bytes 580
  29.3 23.0 %copy-start.6 = (s32[1,2,3]{2,1,0:T(2,128)S(1)}, s32[1,2,3]{2,1,0:T(2,128)}, u32[]{:S(2)}) copy-start(s32[1,2,3]{2,1,0:T(2,128)} %param.8) | copy-start | bytes 76
  29.3 50.1 %all-to-all-start.1 = ((bf16[64,56,128]{2,1,0:T(8,128)(2,1)}), bf16[64,56,128]{2,1,0:T(8,128)(2,1)S(1)}, u32[]{:S(2)}, u32[]{:S(2)}) async-start(bf16[64,56,128]{2,1,0:T(8,128)(2,1)} %add_convert_fusion), calls=%async_computation.1 | async-start | bytes 1835008 | tf_op jit(solution)/shard_map/reduce_zy/all_to_all | solution.py:319
  80.3 16.0 %all-to-all-start.2 = ((f32[8,8,128]{2,1,0:T(8,128)}), f32[8,8,128]{2,1,0:T(8,128)S(1)}, u32[]{:S(2)}, u32[]{:S(2)}) async-start(f32[8,8,128]{2,1,0:T(8,128)} %plane_sum.1), calls=%async_computation.2 | async-start | bytes 65536 | tf_op jit(solution)/shard_map/reduce_x/all_to_all | solution.py:337
  87.6 1.4 %copy-start.7 = (bf16[896,896]{1,0:T(8,128)(2,1)S(1)}, bf16[896,896]{1,0:T(8,128)(2,1)}, u32[]{:S(2)}) copy-start(bf16[896,896]{1,0:T(8,128)(2,1)} %all-gather.2.cloned.1.call-done.weight_ref) | copy-start | bytes 4816900
  89.0 2.7 %copy-start.8 = (bf16[896,896]{1,0:T(8,128)(2,1)S(1)}, bf16[896,896]{1,0:T(8,128)(2,1)}, u32[]{:S(2)}) copy-start(bf16[896,896]{1,0:T(8,128)(2,1)} %all-gather.2.cloned.1.call-done.weight_ref) | copy-start | bytes 4816900
  89.0 2.7 %copy-start.11 = (bf16[8,192,192]{2,1,0:T(8,128)(2,1)S(1)}, bf16[8,192,192]{2,1,0:T(8,128)(2,1)}, u32[]{:S(2)}) copy-start(bf16[8,192,192]{2,1,0:T(8,128)(2,1)} %copy-done.10) | copy-start | bytes 1769476
  91.6 11.6 %collective-permute-start.1 = (bf16[3,128,896]{2,1,0:T(8,128)(2,1)S(1)}, bf16[3,128,896]{2,1,0:T(8,128)(2,1)S(1)}, u32[]{:S(2)}, u32[]{:S(2)}) collective-permute-start(bf16[3,128,896]{2,1,0:T(8,128)(2,1)S(1)} %get-tuple-element.23), channel_id=1, source_target_pairs={{0,64},{64,128},{128,192},{192,256},{256,320},{320,384},{384,448},... | collective-permute-start | bytes 2064392 | tf_op jit(solution)/shard_map/ppermute | solution.py:344
Sparse Core Ops, SparseCore 0:
  28.2 54.2 all-gather.1

commit v8 on v7

--- a/solution.py
+++ b/solution.py
@@ -213,16 +213,8 @@
 
 def compact_body(column_ref, shard_ref, wide_ref):
     for y in range(NY):
-        wide_ref[ROWS * y:ROWS * (y + 1), :] = column_ref[y].astype(jnp.float32)[:ROWS]
+        wide_ref[ROWS * y:ROWS * (y + 1), :] = column_ref[y].astype(jnp.float32)
     shard_ref[...] = wide_ref[...].astype(jnp.bfloat16)
-
-
-def copies_body(shard_ref, copies_ref):
-    shard = shard_ref[...].astype(jnp.float32)
-    shard = jnp.concatenate([shard, jnp.zeros((16 - ROWS, FEAT), jnp.float32)], axis=0)
-    shard = shard.astype(jnp.bfloat16)
-    for y in range(NY):
-        copies_ref[y] = shard
 
 
 def plane_body(got_ref, out_ref, turned_ref):
@@ -283,9 +275,7 @@
     bf16 = jnp.bfloat16
 
     with jax.named_scope("weights_y"):
-        (copies,) = kernel(
-            copies_body, "copies", (shape_of((NY, 16, FEAT), bf16),), (), (out_weight,)
-        )
+        copies = jnp.broadcast_to(out_weight[None], (NY,) + out_weight.shape)
         column = lax.all_to_all(copies, "fsdp", 0, 0, tiled=True, axis_index_groups=Y_GROUPS)
 
     own, other, probs, token = kernel(

time: 112 us -> 111 us (level)
    broadcast_in_dim x0 -> x1, local copies, waits for them, and re-layouts: none -> 1.45 us  [local(): copies = jnp.broadcast_to(out_weight[None], (NY,) + out_weight.shape)]
    unnamed x25 -> x23, local copies, waits for them, and re-layouts: 6.79 us -> 6.04 us
    pallas_call x9 -> x8, Pallas kernels: 15.8 us -> 15.1 us  [kernel(): pl.pallas_call(body, out_shape=outs, in_specs=[in_smem()] * len(scalars)...]
where the time goes in v8:
time: 111 us
  starting transfers between devices  39.8 us (36%)
  waiting for transfers between devices  33.2 us (30%)
  Pallas kernels  15.1 us (14%)
  between operations  14.2 us (13%)
  local copies, waits for them, and re-layouts  7.5 us (7%)
  other arithmetic  1.16 us (1%)
    all_to_all x1, waiting for transfers between devices, local(): lax.all_to_all(pair, ('dp', 'fsdp'), 0, 0, tiled=True, axis_index_groups=...  25.1 us
    all_to_all x1, starting transfers between devices, local(): lax.all_to_all(pair, ('dp', 'fsdp'), 0, 0, tiled=True, axis_index_groups=...  22.9 us
    pallas_call x8, Pallas kernels, kernel(): pl.pallas_call(body, out_shape=outs, in_specs=[in_smem()] * len(scalars)...  15.1 us
    all_to_all x1, starting transfers between devices, local(): lax.all_to_all(copies, 'fsdp', 0, 0, tiled=True, axis_index_groups=Y_GROUPS)  7.56 us
    all_to_all x1, starting transfers between devices, local(): lax.all_to_all(plane, 'fsdp', 0, 0, tiled=True, axis_index_groups=X_GROUPS)  7.28 us
    ppermute x1, waiting for transfers between devices, local(): lax.ppermute(send, 'dp', [(i, (i + 1) % ranks) for i in range(ranks)])  6.24 us
    unnamed x23, local copies, waits for them, and re-layouts  6.04 us
  transfers between devices with their start and end apart: 6, of which 3 were waited for; matrix products, arithmetic and copies ran while one was open for 1% of the time, Pallas kernels for 14%

profile of v8, /device:TPU:2, one launch (start us, length us, event | category | flops | bytes accessed | tf_op | source)
XLA Modules:
  0.0 110.9 jit_solution(13559406084250758678)
XLA Ops:
  7.2 1.5 %broadcast_in_dim.12 = bf16[8,14,896]{2,1,0:T(8,128)(2,1)} broadcast(bf16[14,896]{1,0:T(8,128)(2,1)} %param.9), dimensions={1,2} | broadcast | bytes 225792 | tf_op jit(solution)/shard_map/weights_y/broadcast_in_dim | solution.py:278
  8.6 7.6 %all-to-all-start = ((bf16[8,14,896]{2,1,0:T(8,128)(2,1)}), bf16[8,14,896]{2,1,0:T(8,128)(2,1)S(1)}, u32[]{:S(2)}, u32[]{:S(2)}) async-start(bf16[8,14,896]{2,1,0:T(8,128)(2,1)} %broadcast_in_dim.12), calls=%async_computation | async-start | bytes 458752 | tf_op jit(solution)/shard_map/weights_y/all_to_all | solution.py:279
  16.2 0.0 all-gather.2.cloned.1.call-start
  16.2 0.0 copy-start
  16.2 1.2 %copy-done = bf16[1,1,192,3,896]{4,2,3,1,0:T(8,128)(2,1)S(1)} copy-done((bf16[1,1,192,3,896]{4,2,3,1,0:T(8,128)(2,1)S(1)}, bf16[1,1,192,3,896]{4,2,3,1,0:T(8,128)(2,1)}, u32[]{:S(2)}) %copy-start) | copy-done | bytes 1032216
  17.4 0.0 copy-start.2
  17.4 1.0 copy-done.2
  18.4 0.0 copy-start.4
  18.4 0.7 copy-done.4
  19.1 3.6 %forward.1 = (bf16[64,56,128]{2,1,0:T(8,128)(2,1)S(1)}, bf16[64,56,128]{2,1,0:T(8,128)(2,1)S(1)}, bf16[8,192,192]{2,1,0:T(8,128)(2,1)S(1)}, f32[8,128]{1,0:T(8,128)}) custom-call(s32[3,1,16]{2,1,0:T(1,128)S(1)} %bitcast.18, bf16[3,192,896]{2,1,0:T(8,128)(2,1)S(1)} %bitcast.12, bf16[192,896]{1,0:T(8,128)(2,1)S(1)} %bitcast.15), custom_call_target="tpu_custom_call" | custom-call | flops 3000000000 | bytes 4000000 | tf_op jit(solution)/shard_map/forward/pallas_call | solution.py:253
  22.7 0.0 copy-start.9
  22.7 0.9 copy-done.9
  23.5 1.9 %collective-permute-start = (bf16[64,56,128]{2,1,0:T(8,128)(2,1)S(1)}, bf16[64,56,128]{2,1,0:T(8,128)(2,1)S(1)}, u32[]{:S(2)}, u32[]{:S(2)}) collective-permute-start(bf16[64,56,128]{2,1,0:T(8,128)(2,1)S(1)} %get-tuple-element.18), channel_id=1, source_target_pairs={{0,64},{64,0},{128,192},{192,128},{256,320},{320,256},{384,448},{4... | collective-permute-start | bytes 2752520 | tf_op jit(solution)/shard_map/ppermute | solution.py:306
  25.5 1.9 %all-to-all-done.column_ref = bf16[8,14,896]{2,1,0:T(8,128)(2,1)S(1)} async-done(((bf16[8,14,896]{2,1,0:T(8,128)(2,1)}), bf16[8,14,896]{2,1,0:T(8,128)(2,1)S(1)}, u32[]{:S(2)}, u32[]{:S(2)}) %all-to-all-start) | async-done | bytes 200736 | tf_op jit(solution)/shard_map/weights_y/all_to_all | solution.py:279
  27.3 0.7 compact.1
  28.1 0.0 all-gather.2.cloned.1.call-update
  28.1 0.0 collective-permute-done
  28.1 1.2 %add_convert_fusion = bf16[64,56,128]{2,1,0:T(8,128)(2,1)} fusion(bf16[64,56,128]{2,1,0:T(8,128)(2,1)S(1)} %collective-permute-done, bf16[64,56,128]{2,1,0:T(8,128)(2,1)S(1)} %get-tuple-element.17), kind=kLoop, calls=%fused_computation | loop fusion | flops 1835008 | bytes 2752512 | tf_op jit(solution)/shard_map/convert_element_type | solution.py:307
  29.3 0.0 copy-start.1
  29.3 0.0 copy-start.3
  29.3 0.0 copy-start.5
  29.3 0.0 copy-start.6
  29.3 22.9 %all-to-all-start.1 = ((bf16[64,56,128]{2,1,0:T(8,128)(2,1)}), bf16[64,56,128]{2,1,0:T(8,128)(2,1)S(1)}, u32[]{:S(2)}, u32[]{:S(2)}) async-start(bf16[64,56,128]{2,1,0:T(8,128)(2,1)} %add_convert_fusion), calls=%async_computation.1 | async-start | bytes 1835008 | tf_op jit(solution)/shard_map/reduce_zy/all_to_all | solution.py:309
  52.2 0.0 copy-done.1
  52.3 0.0 copy-done.3
  52.3 0.0 copy-done.5
  52.3 0.0 copy-done.6
  52.3 1.0 pack.1.box_ref
  53.3 1.0 box_forward.1.prob_ref
  54.3 25.1 %all-to-all-done.1.got_ref = bf16[64,56,128]{2,1,0:T(8,128)(2,1)S(1)} async-done(((bf16[64,56,128]{2,1,0:T(8,128)(2,1)}), bf16[64,56,128]{2,1,0:T(8,128)(2,1)S(1)}, u32[]{:S(2)}, u32[]{:S(2)}) %all-to-all-start.1) | async-done | bytes 917536 | tf_op jit(solution)/shard_map/reduce_zy/all_to_all | solution.py:309
  79.3 0.9 plane_sum.1
  80.3 7.3 %all-to-all-start.2 = ((f32[8,8,128]{2,1,0:T(8,128)}), f32[8,8,128]{2,1,0:T(8,128)S(1)}, u32[]{:S(2)}, u32[]{:S(2)}) async-start(f32[8,8,128]{2,1,0:T(8,128)} %plane_sum.1), calls=%async_computation.2 | async-start | bytes 65536 | tf_op jit(solution)/shard_map/reduce_x/all_to_all | solution.py:327
  87.6 0.0 all-gather.2.cloned.1.call-done.weight_ref
  87.6 0.0 copy-start.7
  87.6 1.4 %copy-done.7 = bf16[896,896]{1,0:T(8,128)(2,1)S(1)} copy-done((bf16[896,896]{1,0:T(8,128)(2,1)S(1)}, bf16[896,896]{1,0:T(8,128)(2,1)}, u32[]{:S(2)}) %copy-start.7) | copy-done | bytes 1605656
  89.0 0.0 copy-start.8
  89.0 0.0 copy-start.10
  89.0 2.6 %box_backward.1 = (bf16[3,128,896]{2,1,0:T(8,128)(2,1)S(1)}, f32[8,128]{1,0:T(8,128)S(1)}) custom-call(bf16[4,128,896]{2,1,0:T(8,128)(2,1)S(1)} %pack.1.box_ref, bf16[8,128,128]{2,1,0:T(8,128)(2,1)S(1)} %box_forward.1.prob_ref, bf16[896,896]{1,0:T(8,128)(2,1)S(1)} %copy-done.7), custom_call_target="tpu_custom_call" | custom-call | flops 3000000000 | bytes 4000000 | tf_op jit(solution)/shard_map/box_backward/pallas_call | solution.py:253
  91.6 0.0 collective-permute-start.1
  91.6 0.0 copy-done.8
  91.6 0.0 copy-done.10
  91.7 4.6 %home_backward.1 = (bf16[3,192,896]{2,1,0:T(8,128)(2,1)}, f32[8,128]{1,0:T(8,128)S(1)}) custom-call(s32[3,1,16]{2,1,0:T(1,128)S(1)} %bitcast.21, s32[2,3]{1,0:T(2,128)S(1)} %bitcast.24, bf16[3,192,896]{2,1,0:T(8,128)(2,1)S(1)} %bitcast.14, bf16[192,896]{1,0:T(8,128)(2,1)S(1)} %bitcast.17, bf16[8,192,192]{2,1,0:T(8,128)(2,1)S(1)} %copy-done.10, ...), custom_call_target="tpu_custom_call" | custom-call | flops 12000000000 | bytes 4000000 | tf_op jit(solution)/shard_map/home_backward/pallas_call | solution.py:253
  96.3 0.0 all-to-all-done.2.got_ref
  96.3 0.7 row_sum.1
  97.0 6.2 %collective-permute-done.1 = bf16[3,128,896]{2,1,0:T(8,128)(2,1)S(1)} collective-permute-done((bf16[3,128,896]{2,1,0:T(8,128)(2,1)S(1)}, bf16[3,128,896]{2,1,0:T(8,128)(2,1)S(1)}, u32[]{:S(2)}, u32[]{:S(2)}) %collective-permute-start.1) | collective-permute-done | bytes 688160 | tf_op jit(solution)/shard_map/ppermute | solution.py:334
  103.2 0.8 copy.9
Async XLA Ops:
  8.6 18.7 %all-to-all-start = ((bf16[8,14,896]{2,1,0:T(8,128)(2,1)}), bf16[8,14,896]{2,1,0:T(8,128)(2,1)S(1)}, u32[]{:S(2)}, u32[]{:S(2)}) async-start(bf16[8,14,896]{2,1,0:T(8,128)(2,1)} %broadcast_in_dim.12), calls=%async_computation | async-start | bytes 458752 | tf_op jit(solution)/shard_map/weights_y/all_to_all | solution.py:279
  16.2 71.4 %all-gather.2.cloned.1.call-start = ((), (), s32[]{:S(2)}) async-start(), calls=%async_computation.3 | async-start | bytes 1806336 | tf_op jit(solution)/shard_map/weights_x/all_gather | solution.py:303
  16.2 1.2 %copy-start = (bf16[1,1,192,3,896]{4,2,3,1,0:T(8,128)(2,1)S(1)}, bf16[1,1,192,3,896]{4,2,3,1,0:T(8,128)(2,1)}, u32[]{:S(2)}) copy-start(bf16[1,1,192,3,896]{4,2,3,1,0:T(8,128)(2,1)} %param.5) | copy-start | bytes 3096580
  17.4 1.0 copy-start.2
  18.4 0.7 copy-start.4
  22.7 0.9 copy-start.9
  23.5 4.6 %collective-permute-start = (bf16[64,56,128]{2,1,0:T(8,128)(2,1)S(1)}, bf16[64,56,128]{2,1,0:T(8,128)(2,1)S(1)}, u32[]{:S(2)}, u32[]{:S(2)}) collective-permute-start(bf16[64,56,128]{2,1,0:T(8,128)(2,1)S(1)} %get-tuple-element.18), channel_id=1, source_target_pairs={{0,64},{64,0},{128,192},{192,128},{256,320},{320,256},{384,448},{4... | collective-permute-start | bytes 2752520 | tf_op jit(solution)/shard_map/ppermute | solution.py:306
  29.3 23.0 %copy-start.1 = (bf16[1,1,192,3,896]{4,2,3,1,0:T(8,128)(2,1)S(1)}, bf16[1,1,192,3,896]{4,2,3,1,0:T(8,128)(2,1)}, u32[]{:S(2)}) copy-start(bf16[1,1,192,3,896]{4,2,3,1,0:T(8,128)(2,1)} %param.5) | copy-start | bytes 3096580
  29.3 23.0 %copy-start.3 = (bf16[1,1,192,896]{3,2,1,0:T(8,128)(2,1)S(1)}, bf16[1,1,192,896]{3,2,1,0:T(8,128)(2,1)}, u32[]{:S(2)}) copy-start(bf16[1,1,192,896]{3,2,1,0:T(8,128)(2,1)} %param.6) | copy-start | bytes 1032196
  29.3 23.0 %copy-start.5 = (s32[16,1,3]{0,1,2:T(1,128)S(1)}, s32[16,1,3]{0,1,2:T(1,128)}, u32[]{:S(2)}) copy-start(s32[16,1,3]{0,1,2:T(1,128)} %param.7) | copy-start | bytes 580
  29.3 23.0 %copy-start.6 = (s32[1,2,3]{2,1,0:T(2,128)S(1)}, s32[1,2,3]{2,1,0:T(2,128)}, u32[]{:S(2)}) copy-start(s32[1,2,3]{2,1,0:T(2,128)} %param.8) | copy-start | bytes 76
  29.3 50.1 %all-to-all-start.1 = ((bf16[64,56,128]{2,1,0:T(8,128)(2,1)}), bf16[64,56,128]{2,1,0:T(8,128)(2,1)S(1)}, u32[]{:S(2)}, u32[]{:S(2)}) async-start(bf16[64,56,128]{2,1,0:T(8,128)(2,1)} %add_convert_fusion), calls=%async_computation.1 | async-start | bytes 1835008 | tf_op jit(solution)/shard_map/reduce_zy/all_to_all | solution.py:309
  80.3 16.0 %all-to-all-start.2 = ((f32[8,8,128]{2,1,0:T(8,128)}), f32[8,8,128]{2,1,0:T(8,128)S(1)}, u32[]{:S(2)}, u32[]{:S(2)}) async-start(f32[8,8,128]{2,1,0:T(8,128)} %plane_sum.1), calls=%async_computation.2 | async-start | bytes 65536 | tf_op jit(solution)/shard_map/reduce_x/all_to_all | solution.py:327
  87.6 1.4 %copy-start.7 = (bf16[896,896]{1,0:T(8,128)(2,1)S(1)}, bf16[896,896]{1,0:T(8,128)(2,1)}, u32[]{:S(2)}) copy-start(bf16[896,896]{1,0:T(8,128)(2,1)} %all-gather.2.cloned.1.call-done.weight_ref) | copy-start | bytes 4816900
  89.0 2.7 %copy-start.8 = (bf16[896,896]{1,0:T(8,128)(2,1)S(1)}, bf16[896,896]{1,0:T(8,128)(2,1)}, u32[]{:S(2)}) copy-start(bf16[896,896]{1,0:T(8,128)(2,1)} %all-gather.2.cloned.1.call-done.weight_ref) | copy-start | bytes 4816900
  89.0 2.7 %copy-start.10 = (bf16[8,192,192]{2,1,0:T(8,128)(2,1)S(1)}, bf16[8,192,192]{2,1,0:T(8,128)(2,1)}, u32[]{:S(2)}) copy-start(bf16[8,192,192]{2,1,0:T(8,128)(2,1)} %copy-done.9) | copy-start | bytes 1769476
  91.6 11.6 %collective-permute-start.1 = (bf16[3,128,896]{2,1,0:T(8,128)(2,1)S(1)}, bf16[3,128,896]{2,1,0:T(8,128)(2,1)S(1)}, u32[]{:S(2)}, u32[]{:S(2)}) collective-permute-start(bf16[3,128,896]{2,1,0:T(8,128)(2,1)S(1)} %get-tuple-element.23), channel_id=1, source_target_pairs={{0,64},{64,128},{128,192},{192,256},{256,320},{320,384},{384,448},... | collective-permute-start | bytes 2064392 | tf_op jit(solution)/shard_map/ppermute | solution.py:334
Sparse Core Ops, SparseCore 0:
  28.2 54.2 all-gather.1
